TPU v7x, 32 devices: a whole 2x2x4 slice. The times are simulated.
32 devices in a mesh: seq: 8 (over z, y), tp: 4 (over x, core).
Axes of the slice: x: 2, y: 2, z: 4, core: 2. Of those that a mesh axis runs over, the one named last changes fastest.
Arguments:
- tokens: bfloat16 [3072, 1024], P(('seq', 'tp')), may hold values from -6 to 6
- w_in: bfloat16 [3, 1024, 1024], P(None, None, 'tp'), may hold values from -0.1875 to 0.1875
- short_taps: float32 [3, 3, 1024], P(None, None, 'tp'), may hold values from -3.5 to 3.5
- skip_bias: float32 [2, 1024], P(None, 'tp'), may hold values from -4 to 4
- filter_spectra: float32 [2, 2, 16, 384, 1024], P(None, None, 'seq', None, 'tp'), may hold values from -6 to 6
- w_out: bfloat16 [1024, 1024], P('tp'), may hold values from -0.1875 to 0.1875
Outputs:
- mixed_out: bfloat16 [3072, 1024], P(('seq', 'tp'))
All inputs are finite; a program needn't handle non-finite values.
Results may differ from a plain program's by a relative error of at most 0.007.
Values may be sent and summed in bfloat16 or wider, within the bound.
No kernel may reach another device: no remote copies, remote signals or barrier semaphores. Data moves between devices by JAX's collectives and lax.ppermute only.
A program may use at most 64 MiB of HBM per device.

v0:
```python
import math

import jax
import jax.numpy as jnp
from jax import lax
from jax.sharding import PartitionSpec as P

PRECISE = lax.Precision.HIGHEST


def passed_along(array, axis, by):
    length = lax.axis_size(axis)
    pairs = [(i, i + by) for i in range(length) if 0 <= i + by < length]
    return lax.ppermute(array, axis, pairs)


def phase_table(row_count, col_count, period, direction):
    row_index = jnp.arange(row_count, dtype=jnp.int32)[:, None]
    col_index = jnp.arange(col_count, dtype=jnp.int32)[None, :]
    phases = row_index * col_index % period
    angles = direction * 2.0 * math.pi / period * phases.astype(jnp.float32)
    return (jnp.cos(angles), jnp.sin(angles))


def conjugate(pair):
    return (pair[0], -pair[1])


def product(first_pair, second_pair):
    real_part = first_pair[0] * second_pair[0] - first_pair[1] * second_pair[1]
    imag_part = first_pair[0] * second_pair[1] + first_pair[1] * second_pair[0]
    return (real_part, imag_part)


def contract(pattern, table_pair, value_pair):
    real_part = jnp.einsum(pattern, table_pair[0], value_pair[0], precision=PRECISE) - jnp.einsum(
        pattern, table_pair[1], value_pair[1], precision=PRECISE
    )
    imag_part = jnp.einsum(pattern, table_pair[0], value_pair[1], precision=PRECISE) + jnp.einsum(
        pattern, table_pair[1], value_pair[0], precision=PRECISE
    )
    return (real_part, imag_part)


def local(tokens, w_in, short_taps, skip_bias, filter_spectra, w_out):
    seq_count = lax.axis_size("seq")
    device = lax.axis_index("seq")
    blocks = 2 * seq_count
    projected = jnp.einsum(
        "rd,sdc->src",
        lax.all_gather(tokens, "tp", axis=0, tiled=True),
        w_in,
        preferred_element_type=jnp.float32,
    ).astype(jnp.bfloat16)
    positions = projected.shape[1]
    channels = projected.shape[2]
    before = passed_along(projected[:, -2:, :], "seq", 1)
    extended = jnp.concatenate([before, projected], axis=1).astype(jnp.float32)
    filtered = (
        short_taps[:, 0, None, :] * extended[:, 2:]
        + short_taps[:, 1, None, :] * extended[:, 1:-1]
        + short_taps[:, 2, None, :] * extended[:, :-2]
    )
    factor_one = max(
        (factor for factor in range(1, math.isqrt(positions) + 1) if positions % factor == 0)
    )
    factor_two = positions // factor_one
    forward_pair = phase_table(blocks, seq_count, blocks, -1.0)
    inverse_pair = phase_table(seq_count, blocks, blocks, 1.0)
    outer_table = phase_table(factor_one, factor_one, factor_one, -1.0)
    inner_table = phase_table(factor_two, factor_two, factor_two, -1.0)
    twist_pair = phase_table(factor_one, factor_two, positions, -1.0)
    twist_pair = (twist_pair[0][None, :, :, None], twist_pair[1][None, :, :, None])
    freq_index = 2 * device + jnp.arange(2, dtype=jnp.int32)[:, None]
    pos_index = jnp.arange(positions, dtype=jnp.int32)[None, :]
    angles = -2.0 * math.pi / (blocks * positions) * (freq_index * pos_index).astype(jnp.float32)
    twiddle = (jnp.cos(angles)[:, :, None], jnp.sin(angles)[:, :, None])
    carried = filtered[0]
    for order_index in range(2):
        columns = lax.all_to_all(carried[None], "seq", split_axis=1, concat_axis=0, tiled=True)
        partial_re = jnp.einsum("kp,pqc->kqc", forward_pair[0], columns, precision=PRECISE)
        partial_im = jnp.einsum("kp,pqc->kqc", forward_pair[1], columns, precision=PRECISE)
        line_pair = (
            lax.all_to_all(partial_re, "seq", split_axis=0, concat_axis=1, tiled=True),
            lax.all_to_all(partial_im, "seq", split_axis=0, concat_axis=1, tiled=True),
        )
        line_pair = product(line_pair, twiddle)
        spectrum = tuple(
            (member.reshape(2, factor_one, factor_two, channels) for member in line_pair)
        )
        spectrum = contract("ca,jabk->jcbk", outer_table, spectrum)
        spectrum = product(spectrum, twist_pair)
        spectrum = contract("db,jcbk->jdck", inner_table, spectrum)
        response = (
            filter_spectra[order_index, 0].reshape(2, factor_two, factor_one, channels),
            filter_spectra[order_index, 1].reshape(2, factor_two, factor_one, channels),
        )
        spectrum = product(spectrum, response)
        spectrum = contract("db,jdck->jcbk", conjugate(inner_table), spectrum)
        spectrum = product(spectrum, conjugate(twist_pair))
        spectrum = contract("ca,jcbk->jabk", conjugate(outer_table), spectrum)
        line_pair = tuple(
            (member.reshape(2, positions, channels) / positions for member in spectrum)
        )
        line_pair = product(line_pair, conjugate(twiddle))
        real_rows = jnp.einsum(
            "pk,kqc->pqc",
            inverse_pair[0],
            lax.all_to_all(line_pair[0], "seq", split_axis=1, concat_axis=0, tiled=True),
            precision=PRECISE,
        ) - jnp.einsum(
            "pk,kqc->pqc",
            inverse_pair[1],
            lax.all_to_all(line_pair[1], "seq", split_axis=1, concat_axis=0, tiled=True),
            precision=PRECISE,
        )
        result = lax.all_to_all(real_rows / blocks, "seq", split_axis=0, concat_axis=1, tiled=True)[
            0
        ]
        carried = filtered[order_index + 1] * (result + skip_bias[order_index] * carried)
    gated_out = carried.astype(jnp.bfloat16)
    summed = lax.psum_scatter(
        jnp.dot(gated_out, w_out, preferred_element_type=jnp.float32),
        "tp",
        scatter_dimension=0,
        tiled=True,
    )
    return summed.astype(jnp.bfloat16)


def solution(mesh):
    in_specs = (
        P(("seq", "tp"), None),
        P(None, None, "tp"),
        P(None, None, "tp"),
        P(None, "tp"),
        P(None, None, "seq", None, "tp"),
        P("tp", None),
    )
    out_specs = P(("seq", "tp"), None)
    return jax.shard_map(local, mesh=mesh, in_specs=in_specs, out_specs=out_specs, check_vma=False)
```

profile of v0, /device:TPU:0, one launch (start us, length us, event | category | flops | bytes accessed | tf_op | source)
XLA Modules:
  0.0 380.3 jit_solution(6962177178743716191)
XLA Ops:
  6.5 10.4 %all_gather.3 = bf16[384,1024]{1,0:T(8,128)(2,1)S(1)} all-gather(bf16[96,1024]{1,0:T(8,128)(2,1)} %param.6), channel_id=1, replica_groups=mesh['seq'=8,'tp'=4] {'tp'}, dimensions={0}, use_global_device_ids=true | all-gather | bytes 983040 | tf_op jit(solution)/shard_map/all_gather | solution.py:51
  16.9 1.0 fusion.12
  18.1 3.4 collective-permute-start
  21.6 4.6 %collective-permute-done = bf16[3,2,256]{1,2,0:T(8,128)(2,1)S(1)} collective-permute-done((bf16[3,2,256]{1,2,0:T(8,128)(2,1)S(1)}, bf16[3,2,256]{1,2,0:T(8,128)(2,1)S(1)}, u32[]{:S(2)}, u32[]{:S(2)}) %collective-permute-start) | collective-permute-done | bytes 3104 | tf_op jit(solution)/shard_map/ppermute | solution.py:14
  26.5 1.1 fusion.15
  28.1 18.4 %all_to_all.186 = f32[1,384,256]{2,0,1:T(1,128)S(1)} all-to-all(f32[1,384,256]{2,0,1:T(1,128)S(1)} %copy.207), channel_id=1, replica_groups=mesh['seq'=8,'tp'=4] {'seq'}, dimensions={1} | all-to-all | bytes 786432 | tf_op jit(solution)/shard_map/all_to_all | solution.py:80
  47.5 1.4 copy.212
  48.9 3.5 all-to-all-start.2
  53.4 1.4 copy.209
  54.8 17.2 %all-to-all-done.2 = f32[16,48,256]{2,1,0:T(8,128)S(1)} async-done(((f32[16,48,256]{2,1,0:T(8,128)}), f32[16,48,256]{2,1,0:T(8,128)S(1)}, u32[]{:S(2)}, u32[]{:S(2)}) %all-to-all-start.2) | async-done | bytes 786464 | tf_op jit(solution)/shard_map/all_to_all | solution.py:85
  71.9 3.8 all-to-all-start.1
  79.3 3.6 fusion.401
  83.0 12.9 %all-to-all-done.1 = f32[16,48,256]{2,1,0:T(8,128)S(1)} async-done(((f32[16,48,256]{2,1,0:T(8,128)}), f32[16,48,256]{2,1,0:T(8,128)S(1)}, u32[]{:S(2)}, u32[]{:S(2)}) %all-to-all-start.1) | async-done | bytes 786464 | tf_op jit(solution)/shard_map/all_to_all | solution.py:84
  96.9 1.0 fusion.56
  97.9 1.0 fusion.52
  99.0 1.0 fusion.11
  100.1 1.3 multiply_subtract_fusion.4
  101.3 1.3 fusion.50
  102.6 1.3 fusion.46
  103.9 1.3 fusion.9
  105.3 2.2 multiply_subtract_fusion.3
  107.5 1.3 fusion.96
  110.5 1.0 subtract_bitcast_fusion.1
  117.0 1.5 copy.242
  118.6 3.5 all-to-all-start.3
  122.1 1.5 copy.245
  123.6 18.9 %all-to-all-done.3 = f32[2,384,256]{2,0,1:T(2,128)S(1)} async-done(((f32[2,384,256]{2,0,1:T(2,128)}), f32[2,384,256]{2,0,1:T(2,128)S(1)}, u32[]{:S(2)}, u32[]{:S(2)}) %all-to-all-start.3) | async-done | bytes 786464 | tf_op jit(solution)/shard_map/all_to_all | solution.py:109
  142.5 3.7 all-to-all-start.4
  147.5 1.3 fusion.218
  148.7 17.8 %all-to-all-done.4 = f32[2,384,256]{2,0,1:T(2,128)S(1)} async-done(((f32[2,384,256]{2,0,1:T(2,128)}), f32[2,384,256]{2,0,1:T(2,128)S(1)}, u32[]{:S(2)}, u32[]{:S(2)}) %all-to-all-start.4) | async-done | bytes 786464 | tf_op jit(solution)/shard_map/all_to_all | solution.py:114
  169.6 3.6 all-to-all-start.5
  173.8 11.3 %all-to-all-done.5 = f32[8,48,256]{2,1,0:T(8,128)S(1)} async-done(((f32[8,48,256]{2,1,0:T(8,128)}), f32[8,48,256]{2,1,0:T(8,128)S(1)}, u32[]{:S(2)}, u32[]{:S(2)}) %all-to-all-start.5) | async-done | bytes 393248 | tf_op jit(solution)/shard_map/all_to_all | solution.py:117
  185.9 15.6 %all_to_all.187 = f32[1,384,256]{2,0,1:T(1,128)S(1)} all-to-all(f32[1,384,256]{2,0,1:T(1,128)S(1)} %copy.250), channel_id=1, replica_groups=mesh['seq'=8,'tp'=4] {'seq'}, dimensions={1} | all-to-all | bytes 786432 | tf_op jit(solution)/shard_map/all_to_all | solution.py:80
  202.4 1.4 copy.252
  203.8 3.5 all-to-all-start.7
  208.3 1.4 copy.255
  209.7 17.5 %all-to-all-done.7 = f32[16,48,256]{2,1,0:T(8,128)S(1)} async-done(((f32[16,48,256]{2,1,0:T(8,128)}), f32[16,48,256]{2,1,0:T(8,128)S(1)}, u32[]{:S(2)}, u32[]{:S(2)}) %all-to-all-start.7) | async-done | bytes 786464 | tf_op jit(solution)/shard_map/all_to_all | solution.py:84
  227.1 3.8 all-to-all-start.8
  231.9 19.1 %all-to-all-done.8 = f32[16,48,256]{2,1,0:T(8,128)S(1)} async-done(((f32[16,48,256]{2,1,0:T(8,128)}), f32[16,48,256]{2,1,0:T(8,128)S(1)}, u32[]{:S(2)}, u32[]{:S(2)}) %all-to-all-start.8) | async-done | bytes 786464 | tf_op jit(solution)/shard_map/all_to_all | solution.py:85
  251.1 1.1 copy-done.2
  252.4 1.0 fusion.38
  253.5 1.0 fusion.34
  254.5 1.1 fusion.5
  255.6 1.3 multiply_subtract_fusion.1
  256.9 1.3 fusion.32
  258.2 1.3 fusion.28
  259.6 1.3 fusion.3
  260.9 2.2 multiply_subtract_fusion
  263.9 1.1 fusion.94
  265.9 1.0 subtract_bitcast_fusion
  272.5 1.5 copy.283
  274.0 3.5 all-to-all-start.9
  277.5 1.5 copy.286
  279.1 18.8 %all-to-all-done.9 = f32[2,384,256]{2,0,1:T(2,128)S(1)} async-done(((f32[2,384,256]{2,0,1:T(2,128)}), f32[2,384,256]{2,0,1:T(2,128)S(1)}, u32[]{:S(2)}, u32[]{:S(2)}) %all-to-all-start.9) | async-done | bytes 786464 | tf_op jit(solution)/shard_map/all_to_all | solution.py:109
  297.9 3.9 %all-to-all-start.10 = ((f32[2,384,256]{2,0,1:T(2,128)}), f32[2,384,256]{2,0,1:T(2,128)S(1)}, u32[]{:S(2)}, u32[]{:S(2)}) async-start(f32[2,384,256]{2,0,1:T(2,128)} %copy.286), calls=%async_computation.10 | async-start | bytes 1572864 | tf_op jit(solution)/shard_map/all_to_all | solution.py:114
  302.4 1.4 all_to_all.168
  303.9 2.4 fusion.216
  306.3 15.8 %all-to-all-done.10 = f32[2,384,256]{2,0,1:T(2,128)S(1)} async-done(((f32[2,384,256]{2,0,1:T(2,128)}), f32[2,384,256]{2,0,1:T(2,128)S(1)}, u32[]{:S(2)}, u32[]{:S(2)}) %all-to-all-start.10) | async-done | bytes 786464 | tf_op jit(solution)/shard_map/all_to_all | solution.py:114
  323.3 1.5 fusion.13
  325.7 3.7 all-to-all-start.11
  329.6 11.6 %all-to-all-done.11 = f32[8,48,256]{2,1,0:T(8,128)S(1)} async-done(((f32[8,48,256]{2,1,0:T(8,128)}), f32[8,48,256]{2,1,0:T(8,128)S(1)}, u32[]{:S(2)}, u32[]{:S(2)}) %all-to-all-start.11) | async-done | bytes 393248 | tf_op jit(solution)/shard_map/all_to_all | solution.py:117
  341.4 2.9 fusion.72
  344.3 27.0 %reduce-scatter.2.cloned.1.call-done = f32[96,1024]{1,0:T(8,128)} async-done(((f32[384,1024]{1,0:T(8,128)}), f32[96,1024]{1,0:T(8,128)}) %reduce-scatter.2.cloned.1.call-update) | async-done | bytes 393232 | tf_op jit(solution)/shard_map/reduce_scatter | solution.py:122
  371.3 1.7 convert_element_type.169
  (116 shorter events, 34.0 us)
Async XLA Ops:
  6.5 10.4 %copy-start = (bf16[3,1024,256]{2,1,0:T(8,128)(2,1)S(1)}, bf16[3,1024,256]{2,1,0:T(8,128)(2,1)}, u32[]{:S(2)}) copy-start(bf16[3,1024,256]{2,1,0:T(8,128)(2,1)} %param.7) | copy-start | bytes 4718596
  16.9 4.6 %copy-start.22 = (f32[3,3,256]{2,1,0:T(4,128)S(1)}, f32[3,3,256]{2,1,0:T(4,128)}, u32[]{:S(2)}) copy-start(f32[3,3,256]{2,1,0:T(4,128)} %param.8) | copy-start | bytes 27652
  18.1 8.1 %collective-permute-start = (bf16[3,2,256]{1,2,0:T(8,128)(2,1)S(1)}, bf16[3,2,256]{1,2,0:T(8,128)(2,1)S(1)}, u32[]{:S(2)}, u32[]{:S(2)}) collective-permute-start(bf16[3,2,256]{1,2,0:T(8,128)(2,1)S(1)} %slice.64), channel_id=1, source_target_pairs={{0,4},{4,8},{8,12},{12,16},{16,20},{20,24},{24,28},{1,5},{5,9},{9,... | collective-permute-start | bytes 9224 | tf_op jit(solution)/shard_map/ppermute | solution.py:14
  48.9 23.0 %all-to-all-start.2 = ((f32[16,48,256]{2,1,0:T(8,128)}), f32[16,48,256]{2,1,0:T(8,128)S(1)}, u32[]{:S(2)}, u32[]{:S(2)}) async-start(f32[16,48,256]{2,1,0:T(8,128)} %copy.212), calls=%async_computation.2 | async-start | bytes 1572864 | tf_op jit(solution)/shard_map/all_to_all | solution.py:85
  71.9 23.9 %all-to-all-start.1 = ((f32[16,48,256]{2,1,0:T(8,128)}), f32[16,48,256]{2,1,0:T(8,128)S(1)}, u32[]{:S(2)}, u32[]{:S(2)}) async-start(f32[16,48,256]{2,1,0:T(8,128)} %copy.209), calls=%async_computation.1 | async-start | bytes 1572864 | tf_op jit(solution)/shard_map/all_to_all | solution.py:84
  95.9 0.7 copy-start.8
  95.9 0.7 copy-start.10
  99.0 1.1 copy-start.12
  103.9 1.3 copy-start.5
  103.9 1.4 copy-start.6
  109.6 0.9 copy-start.14
  109.6 0.9 copy-start.16
  116.1 0.7 copy-start.18
  118.6 23.9 %all-to-all-start.3 = ((f32[2,384,256]{2,0,1:T(2,128)}), f32[2,384,256]{2,0,1:T(2,128)S(1)}, u32[]{:S(2)}, u32[]{:S(2)}) async-start(f32[2,384,256]{2,0,1:T(2,128)} %copy.242), calls=%async_computation.3 | async-start | bytes 1572864 | tf_op jit(solution)/shard_map/all_to_all | solution.py:109
  142.5 24.1 %all-to-all-start.4 = ((f32[2,384,256]{2,0,1:T(2,128)}), f32[2,384,256]{2,0,1:T(2,128)S(1)}, u32[]{:S(2)}, u32[]{:S(2)}) async-start(f32[2,384,256]{2,0,1:T(2,128)} %copy.245), calls=%async_computation.4 | async-start | bytes 1572864 | tf_op jit(solution)/shard_map/all_to_all | solution.py:114
  167.2 1.0 copy-start.7
  168.8 4.4 %copy-start.24 = (f32[2,256]{1,0:T(2,128)S(1)}, f32[2,256]{1,0:T(2,128)}, u32[]{:S(2)}) copy-start(f32[2,256]{1,0:T(2,128)} %param.9) | copy-start | bytes 6148
  169.6 15.4 %all-to-all-start.5 = ((f32[8,48,256]{2,1,0:T(8,128)}), f32[8,48,256]{2,1,0:T(8,128)S(1)}, u32[]{:S(2)}, u32[]{:S(2)}) async-start(f32[8,48,256]{2,1,0:T(8,128)} %copy.248), calls=%async_computation.5 | async-start | bytes 786432 | tf_op jit(solution)/shard_map/all_to_all | solution.py:117
  173.8 11.6 %copy-start.20 = (f32[1,256]{1,0:T(1,128)}, f32[1,256]{1,0:T(1,128)S(1)}, u32[]{:S(2)}) copy-start(f32[1,256]{1,0:T(1,128)S(1)} %get-tuple-element.35) | copy-start | bytes 3076
  203.8 23.3 %all-to-all-start.7 = ((f32[16,48,256]{2,1,0:T(8,128)}), f32[16,48,256]{2,1,0:T(8,128)S(1)}, u32[]{:S(2)}, u32[]{:S(2)}) async-start(f32[16,48,256]{2,1,0:T(8,128)} %copy.252), calls=%async_computation.7 | async-start | bytes 1572864 | tf_op jit(solution)/shard_map/all_to_all | solution.py:84
  227.1 23.9 %all-to-all-start.8 = ((f32[16,48,256]{2,1,0:T(8,128)}), f32[16,48,256]{2,1,0:T(8,128)S(1)}, u32[]{:S(2)}, u32[]{:S(2)}) async-start(f32[16,48,256]{2,1,0:T(8,128)} %copy.255), calls=%async_computation.8 | async-start | bytes 1572864 | tf_op jit(solution)/shard_map/all_to_all | solution.py:85
  231.9 19.2 %copy-start.9 = (f32[2,16,24]{2,1,0:T(8,128)S(1)}, f32[2,16,24]{2,1,0:T(8,128)}, u32[]{:S(2)}) copy-start(f32[2,16,24]{2,1,0:T(8,128)} %get-tuple-element.32) | copy-start | bytes 9220
  231.9 19.2 %copy-start.11 = (f32[2,16,24]{2,1,0:T(8,128)S(1)}, f32[2,16,24]{2,1,0:T(8,128)}, u32[]{:S(2)}) copy-start(f32[2,16,24]{2,1,0:T(8,128)} %get-tuple-element.33) | copy-start | bytes 9220
  251.0 1.1 copy-start.2
  254.5 1.1 copy-start.13
  259.5 1.3 copy-start.3
  259.5 1.4 copy-start.4
  265.0 0.9 copy-start.15
  265.0 0.9 copy-start.17
  271.5 0.7 copy-start.19
  274.0 23.9 %all-to-all-start.9 = ((f32[2,384,256]{2,0,1:T(2,128)}), f32[2,384,256]{2,0,1:T(2,128)S(1)}, u32[]{:S(2)}, u32[]{:S(2)}) async-start(f32[2,384,256]{2,0,1:T(2,128)} %copy.283), calls=%async_computation.9 | async-start | bytes 1572864 | tf_op jit(solution)/shard_map/all_to_all | solution.py:109
  297.9 24.2 %all-to-all-start.10 = ((f32[2,384,256]{2,0,1:T(2,128)}), f32[2,384,256]{2,0,1:T(2,128)S(1)}, u32[]{:S(2)}, u32[]{:S(2)}) async-start(f32[2,384,256]{2,0,1:T(2,128)} %copy.286), calls=%async_computation.10 | async-start | bytes 1572864 | tf_op jit(solution)/shard_map/all_to_all | solution.py:114
  325.7 15.7 %copy-start.21 = (f32[1,256]{1,0:T(1,128)S(1)}, f32[1,256]{1,0:T(1,128)}, u32[]{:S(2)}) copy-start(f32[1,256]{1,0:T(1,128)} %copy-done.20) | copy-start | bytes 3076
  325.7 15.7 %copy-start.23 = (f32[1,256]{1,0:T(1,128)S(1)}, f32[1,256]{1,0:T(1,128)}, u32[]{:S(2)}) copy-start(f32[1,256]{1,0:T(1,128)} %get-tuple-element.34) | copy-start | bytes 3076
  325.7 15.5 %all-to-all-start.11 = ((f32[8,48,256]{2,1,0:T(8,128)}), f32[8,48,256]{2,1,0:T(8,128)S(1)}, u32[]{:S(2)}, u32[]{:S(2)}) async-start(f32[8,48,256]{2,1,0:T(8,128)} %copy.289), calls=%async_computation.11 | async-start | bytes 786432 | tf_op jit(solution)/shard_map/all_to_all | solution.py:117
  329.4 41.9 %reduce-scatter.2.cloned.1.call-start = ((), (), s32[]{:S(2)}) async-start(), calls=%async_computation.13 | async-start | bytes 1966080 | tf_op jit(solution)/shard_map/reduce_scatter | solution.py:122
  341.4 31.6 %copy-start.1 = (bf16[3,1024,256]{2,1,0:T(8,128)(2,1)S(1)}, bf16[3,1024,256]{2,1,0:T(8,128)(2,1)}, u32[]{:S(2)}) copy-start(bf16[3,1024,256]{2,1,0:T(8,128)(2,1)} %param.7) | copy-start | bytes 4718596
Sparse Core Ops, SparseCore 0:
  344.5 26.7 reduce-scatter.1
where the time goes:
time: 387 us; the launch traced here: 380 us
  waiting for transfers between devices  192 us (50%)
  matrix products  50.2 us (13%)
  blocking collectives  44.4 us (11%)
  starting transfers between devices  40 us (10%)
  local copies, waits for them, and re-layouts  31.9 us (8%)
  between operations  14.8 us (4%)
  other arithmetic  6.57 us (2%)
    all_to_all x2, waiting for transfers between devices, local(): lax.all_to_all(line_pair[0], 'seq', split_axis=1, concat_axis=0, tiled=True)  37.7 us
    all_to_all x2, waiting for transfers between devices, local(): lax.all_to_all(partial_im, 'seq', split_axis=0, concat_axis=1, tiled=True)  36.3 us
    all_to_all x2, blocking collectives, local(): lax.all_to_all(carried[None], 'seq', split_axis=1, concat_axis=0, tiled=T...  34 us
    all_to_all x2, waiting for transfers between devices, local(): lax.all_to_all(line_pair[1], 'seq', split_axis=1, concat_axis=0, tiled=True)  33.7 us
    all_to_all x2, waiting for transfers between devices, local(): lax.all_to_all(partial_re, 'seq', split_axis=0, concat_axis=1, tiled=True)  30.3 us
    reduce_scatter x1, waiting for transfers between devices, local(): lax.psum_scatter(jnp.dot(gated_out, w_out, preferred_element_type=jnp.flo...  27 us
    all_to_all x2, waiting for transfers between devices, local(): lax.all_to_all(real_rows / blocks, 'seq', split_axis=0, concat_axis=1, ti...  22.9 us
    dot_general x8, matrix products, contract(): jnp.einsum(pattern, table_pair[1], value_pair[0], precision=PRECISE)  10.6 us
  transfers between devices with their start and end apart: 12, of which 12 were waited for; matrix products, arithmetic and copies ran while one was open for 6% of the time, Pallas kernels for 0%

commit v1 on v0

v1 whole, which is shorter than its diff:
```python
import functools
import math

import jax
import jax.numpy as jnp
import numpy as np
from jax import lax
from jax.experimental import pallas as pl
from jax.experimental.pallas import tpu as pltpu
from jax.sharding import PartitionSpec as P

VMEM = pl.BlockSpec(memory_space=pltpu.VMEM)
LIMIT = 48 * 1024 * 1024


def line_table(length):
    phases = np.outer(np.arange(length), np.arange(length)) % length
    angles = 2.0 * np.pi / length * phases
    cos, sin = np.cos(angles), np.sin(angles)
    return jnp.asarray(np.block([[cos, -sin], [sin, cos]]), jnp.bfloat16)


def twist_tables(blocks, length):
    angles = 2.0 * np.pi / (blocks * length) * np.outer(np.arange(blocks), np.arange(length))
    cos, sin = np.cos(angles), np.sin(angles)
    return jnp.asarray(np.stack([cos, -sin]), jnp.float32)


def plus(a, b):
    return b if a is None else a if b is None else a + b


def minus(a, b):
    return a if b is None else -b if a is None else a - b


def times(pair, k, size, direction):
    re, im = pair
    cos, sin = math.cos(2 * math.pi * k / size), direction * math.sin(2 * math.pi * k / size)
    return re * cos - im * sin, re * sin + im * cos


def forward_half(values):
    if len(values) == 1:
        return [(values[0], None), (values[0], None)]
    even, odd = forward_half(values[0::2]), forward_half(values[1::2])
    half = len(values)
    quarter = half // 2
    out = [None] * (half + 1)
    out[0] = (even[0][0] + odd[0][0], None)
    out[half] = (even[0][0] - odd[0][0], None)
    out[quarter] = (even[quarter][0], -odd[quarter][0])
    for k in range(1, quarter):
        re, im = times(odd[k], k, 2 * half, -1.0)
        out[k] = (even[k][0] + re, even[k][1] + im)
        out[half - k] = (even[k][0] - re, im - even[k][1])
    return out


def inverse_half(bins):
    half = len(bins) - 1
    if half == 1:
        return [bins[0][0] + bins[1][0]]
    quarter = half // 2
    even = [(bins[0][0] + bins[half][0], None)]
    odd = [(bins[0][0] - bins[half][0], None)]
    for k in range(1, quarter):
        (a, b), (c, d) = bins[k], bins[half - k]
        even.append((a + c, b - d))
        odd.append(times((a - c, b + d), k, 2 * half, 1.0))
    even.append((2.0 * bins[quarter][0], None))
    odd.append((-2.0 * bins[quarter][1], None))
    out = [None] * half
    out[0::2] = inverse_half(even)
    out[1::2] = inverse_half(odd)
    return out


def spectra_kernel(spectra_ref, out_ref):
    turned = spectra_ref[0, 0, 0].T
    shape = out_ref.shape
    out_ref[:, 0] = turned.reshape(shape[0], shape[2], shape[3]).astype(jnp.bfloat16)


def send_spectra(spectra, count):
    orders, parts, residues, length, channels = spectra.shape
    each = channels // count
    slabs = orders * parts * residues
    return pl.pallas_call(
        spectra_kernel,
        grid=(slabs,),
        in_specs=[
            pl.BlockSpec(
                (1, 1, 1, length, channels),
                lambda i: (i // (parts * residues), i // residues % parts, i % residues, 0, 0),
            )
        ],
        out_specs=pl.BlockSpec((count, 1, each, length), lambda i: (0, i, 0, 0)),
        out_shape=jax.ShapeDtypeStruct((count, slabs, each, length), jnp.bfloat16),
        compiler_params=pltpu.CompilerParams(vmem_limit_bytes=LIMIT),
    )(spectra)


def project_kernel(tokens_ref, weight_ref, *refs):
    outs, held = refs[:-1], refs[-1]
    count, pieces, each, length = held.shape
    me = lax.axis_index("seq")
    rows = jnp.dot(tokens_ref[...], weight_ref[0], preferred_element_type=jnp.float32)
    for piece in range(pieces):
        turned = rows[piece * length : (piece + 1) * length].T
        held[:, piece] = turned.reshape(count, each, length).astype(jnp.bfloat16)
    for shift, out in enumerate(outs):
        out[0] = held[lax.rem(me + shift, count)]


def project(tokens, weights, count, length):
    rows, depth = tokens.shape
    branches, _, channels = weights.shape
    each, pieces = channels // count, rows // length
    return pl.pallas_call(
        project_kernel,
        grid=(branches,),
        in_specs=[
            pl.BlockSpec((rows, depth), lambda b: (0, 0)),
            pl.BlockSpec((1, depth, channels), lambda b: (b, 0, 0)),
        ],
        out_specs=[pl.BlockSpec((1, pieces, each, length), lambda b: (b, 0, 0, 0))] * count,
        out_shape=[jax.ShapeDtypeStruct((branches, pieces, each, length), jnp.bfloat16)] * count,
        scratch_shapes=[pltpu.VMEM((count, pieces, each, length), jnp.bfloat16)],
        compiler_params=pltpu.CompilerParams(vmem_limit_bytes=LIMIT),
    )(tokens, weights)


def convolve_kernel(count, *refs):
    arrived, refs = refs[:count], refs[count:]
    spectra_ref, taps_ref, skip_ref, table_ref, twist_ref, out_ref = refs[:6]
    held, filtered, lines, wave, gathered, columns = refs[6:]
    branches, positions, each, length = filtered.shape
    residues = spectra_ref.shape[1] // 4
    blocks = count * residues
    pieces = positions // count
    me = lax.axis_index("seq")
    chunk = min(16, each)
    width = 128

    for shift in range(count):
        held[lax.rem(me - shift + count, count)] = arrived[shift][...]

    for branch in range(branches):
        gathered[branch * 3 : branch * 3 + 3] = taps_ref[branch]
    gathered[9:11] = skip_ref[...]
    columns[...] = gathered[...].T
    mine = columns[pl.ds(pl.multiple_of(me * each, each), each), :]
    lane = lax.broadcasted_iota(jnp.int32, (each, length), 1)
    for branch in range(branches):
        last = [jnp.zeros((each, length), jnp.float32)] * 2
        scale = [jnp.broadcast_to(mine[:, branch * 3 + i : branch * 3 + i + 1], (each, length)) for i in range(3)]
        for p in range(positions):
            now = held[p // pieces, branch, p % pieces].astype(jnp.float32)
            total = scale[0] * now
            for back in (1, 2):
                rolled = pltpu.roll(now, back, 1)
                total = total + scale[back] * jnp.where(lane < back, last[back - 1], rolled)
                last[back - 1] = rolled
            filtered[branch, p] = total

    tiles = [(r, c) for r in range(0, each, chunk) for c in range(0, length, width)]
    step = max(each, min(blocks * each, 128))
    for order in range(2):
        for r, c in tiles:
            bins = forward_half([filtered[0, p, r : r + chunk, c : c + width] for p in range(positions)])
            for k in range(blocks):
                cos, sin = twist_ref[0, k : k + 1, c : c + width], twist_ref[1, k : k + 1, c : c + width]
                re, im = bins[min(k, blocks - k)]
                if im is None:
                    pair = (re * cos, re * sin)
                elif 2 * k < blocks:
                    pair = (re * cos - im * sin, re * sin + im * cos)
                else:
                    pair = (re * cos + im * sin, re * sin - im * cos)
                for part in range(2):
                    lines[k * each + r : k * each + r + chunk, part * length + c : part * length + c + width] = pair[part].astype(jnp.bfloat16)
        for start in range(0, blocks * each, step):
            spectrum = jnp.dot(lines[start : start + step], table_ref[...], preferred_element_type=jnp.float32)
            for k in range(start // each, (start + step) // each):
                at = k * each - start
                re, im = spectrum[at : at + each, :length], spectrum[at : at + each, length:]
                first = order * 2 * residues + k % residues
                gain_re = spectra_ref[k // residues, first].astype(jnp.float32)
                gain_im = spectra_ref[k // residues, first + residues].astype(jnp.float32)
                lines[k * each : (k + 1) * each, :length] = (re * gain_re - im * gain_im).astype(jnp.bfloat16)
                lines[k * each : (k + 1) * each, length:] = (-(re * gain_im) - im * gain_re).astype(jnp.bfloat16)
        for start in range(0, blocks * each, step):
            wave[start : start + step] = jnp.dot(lines[start : start + step], table_ref[...], preferred_element_type=jnp.float32)
        for r, c in tiles:
            turned = []
            for k in range(blocks):
                cos, sin = twist_ref[0, k : k + 1, c : c + width], twist_ref[1, k : k + 1, c : c + width]
                re = wave[k * each + r : k * each + r + chunk, c : c + width]
                im = wave[k * each + r : k * each + r + chunk, length + c : length + c + width]
                turned.append((re * cos - im * sin, re * sin + im * cos))
            bins = [(turned[0][0] * 2.0, None)]
            for k in range(1, blocks // 2):
                one, two = turned[k], turned[blocks - k]
                bins.append((one[0] + two[0], two[1] - one[1]))
            bins.append((turned[blocks // 2][0] * 2.0, None))
            values = inverse_half(bins)
            skip = columns[pl.ds(pl.multiple_of(me * each + r, chunk), chunk), 9 + order : 10 + order]
            for p in range(positions):
                here = (p, slice(r, r + chunk), slice(c, c + width))
                carried = filtered[(0,) + here]
                total = values[p] * (0.5 / (blocks * length)) + skip * carried
                filtered[(0,) + here] = filtered[(order + 1,) + here] * total

    share, across = out_ref.shape[3], out_ref.shape[1]
    for p in range(positions):
        for part in range(length // share):
            to = p % pieces * (length // share) + part
            out_ref[p // pieces, to] = filtered[0, p, :, part * share : (part + 1) * share].astype(jnp.bfloat16)


def convolve(arrived, spectra, taps, skip, across):
    count, slabs, each, length = spectra.shape
    branches, pieces = arrived[0].shape[:2]
    blocks = count * (slabs // 4)
    positions = count * pieces
    channels = taps.shape[2]
    share = pieces * length // across
    return pl.pallas_call(
        functools.partial(convolve_kernel, count),
        in_specs=[VMEM] * (count + 5),
        out_specs=VMEM,
        out_shape=jax.ShapeDtypeStruct((count, across, each, share), jnp.bfloat16),
        scratch_shapes=[
            pltpu.VMEM((count, branches, pieces, each, length), jnp.bfloat16),
            pltpu.VMEM((branches, positions, each, length), jnp.float32),
            pltpu.VMEM((blocks * each, 2 * length), jnp.bfloat16),
            pltpu.VMEM((blocks * each, 2 * length), jnp.float32),
            pltpu.VMEM((16, channels), jnp.float32),
            pltpu.VMEM((channels, 16), jnp.float32),
        ],
        compiler_params=pltpu.CompilerParams(vmem_limit_bytes=LIMIT),
    )(*arrived, spectra, taps, skip, line_table(length), twist_tables(blocks, length))


def finish_kernel(gated_ref, *refs):
    weights, out_ref = refs[:-1], refs[-1]
    count, across, each, share = gated_ref.shape
    me = lax.axis_index("tp")
    total = jnp.zeros(out_ref.shape, jnp.float32)
    for flip, weight in enumerate(weights):
        part = gated_ref[:, jnp.bitwise_xor(me, flip)].astype(jnp.float32)
        part = part.reshape(count * each, share).astype(jnp.bfloat16)
        total = total + lax.dot_general(
            part, weight[...], (((0,), (0,)), ((), ())), preferred_element_type=jnp.float32
        )
    out_ref[...] = total.astype(jnp.bfloat16)


def finish(gated, weights):
    across, share, width = gated.shape[1], gated.shape[3], weights[0].shape[1]
    return pl.pallas_call(
        finish_kernel,
        in_specs=[VMEM] * (1 + across),
        out_specs=VMEM,
        out_shape=jax.ShapeDtypeStruct((share, width), jnp.bfloat16),
        compiler_params=pltpu.CompilerParams(vmem_limit_bytes=LIMIT),
    )(gated, *weights)


def local(tokens, w_in, short_taps, skip_bias, filter_spectra, w_out):
    count, across = lax.axis_size("seq"), lax.axis_size("tp")
    length = filter_spectra.shape[3]
    spectra = send_spectra(filter_spectra, count)
    spectra = lax.all_to_all(spectra, "seq", split_axis=0, concat_axis=0, tiled=True)
    gathered = lax.all_gather(tokens, "tp", axis=0, tiled=True)
    outgoing = project(gathered, w_in, count, length)
    arrived = [outgoing[0]] + [
        lax.ppermute(outgoing[shift], "seq", [(i, (i + shift) % count) for i in range(count)])
        for shift in range(1, count)
    ]
    weights = [w_out] + [
        lax.ppermute(w_out, "tp", [(i, i ^ flip) for i in range(across)]) for flip in range(1, across)
    ]
    gated = convolve(arrived, spectra, short_taps, skip_bias, across)
    shape = gated.shape
    gated = gated.reshape((count * across,) + shape[2:])
    gated = lax.all_to_all(gated, ("seq", "tp"), split_axis=0, concat_axis=0, tiled=True)
    return finish(gated.reshape(shape), weights)


def solution(mesh):
    in_specs = (
        P(("seq", "tp"), None),
        P(None, None, "tp"),
        P(None, None, "tp"),
        P(None, "tp"),
        P(None, None, "seq", None, "tp"),
        P("tp", None),
    )
    out_specs = P(("seq", "tp"), None)
    return jax.shard_map(local, mesh=mesh, in_specs=in_specs, out_specs=out_specs, check_vma=False)
```

time: 387 us -> 96.3 us (0.25); the launches traced: 380 us -> 95.7 us
  waiting for transfers between devices: 192 us -> 39.4 us
  matrix products: 50.2 us -> 0 us
  blocking collectives: 44.4 us -> 8.6 us
  local copies, waits for them, and re-layouts: 31.9 us -> 8.51 us
  between operations: 14.8 us -> 0.09 us
  starting transfers between devices: 40 us -> 26.7 us
  Pallas kernels: 0 us -> 12.4 us
  other arithmetic: 6.57 us -> 0 us
    all_to_all x10 -> x2, waiting for transfers between devices: 161 us -> 10.6 us  [the longest x1 10.6 us: local(): lax.all_to_all(gated, ('seq', 'tp'), split_axis=0, concat_axis=0, tiled=T...]
    dot_general x42 -> x0, matrix products: 50.2 us -> none  [the longest x8 10.6 us: contract(): jnp.einsum(pattern, table_pair[1], value_pair[0], precision=PRECISE)]
    all_to_all x2 -> x0, blocking collectives: 34 us -> none  [local(): lax.all_to_all(carried[None], 'seq', split_axis=1, concat_axis=0, tiled=T...]
    reduce_scatter x1 -> x0, waiting for transfers between devices: 27 us -> none  [local(): lax.psum_scatter(jnp.dot(gated_out, w_out, preferred_element_type=jnp.flo...]
    all_to_all x10 -> x2, starting transfers between devices: 36.5 us -> 11.7 us  [the longest x1 7.41 us: local(): lax.all_to_all(spectra, 'seq', split_axis=0, concat_axis=0, tiled=True)]
    ppermute x1 -> x10, waiting for transfers between devices: 4.6 us -> 28.8 us  [the longest x7 28.8 us: local(): lax.ppermute(outgoing[shift], 'seq', [(i, (i + shift) % count) for i in r...]
    pallas_call x0 -> x4, Pallas kernels: none -> 12.4 us  [the longest x1 5.23 us: convolve(): pl.pallas_call(functools.partial(convolve_kernel, count), in_specs=[VMEM]...]
    ppermute x1 -> x10, starting transfers between devices: 3.43 us -> 15 us  [the longest x7 13.5 us: local(): lax.ppermute(outgoing[shift], 'seq', [(i, (i + shift) % count) for i in r...]
  transfers between devices with their start and end apart: 12 -> 12, of which waited for: 12 -> 5; matrix products, arithmetic and copies ran while one was open for 6% -> 0% of each run, Pallas kernels for 0% -> 7%
where the time goes in v1:
time: 96.3 us; the launch traced here: 95.7 us
  waiting for transfers between devices  39.4 us (41%)
  starting transfers between devices  26.7 us (28%)
  Pallas kernels  12.4 us (13%)
  blocking collectives  8.6 us (9%)
  local copies, waits for them, and re-layouts  8.51 us (9%)
    ppermute x7, waiting for transfers between devices, local(): lax.ppermute(outgoing[shift], 'seq', [(i, (i + shift) % count) for i in r...  28.8 us
    ppermute x7, starting transfers between devices, local(): lax.ppermute(outgoing[shift], 'seq', [(i, (i + shift) % count) for i in r...  13.5 us
    all_to_all x1, waiting for transfers between devices, local(): lax.all_to_all(gated, ('seq', 'tp'), split_axis=0, concat_axis=0, tiled=T...  10.6 us
    all_gather x1, blocking collectives, local(): gathered = lax.all_gather(tokens, 'tp', axis=0, tiled=True)  8.6 us
    unnamed x26, local copies, waits for them, and re-layouts  8.51 us
    all_to_all x1, starting transfers between devices, local(): lax.all_to_all(spectra, 'seq', split_axis=0, concat_axis=0, tiled=True)  7.41 us
    pallas_call x1, Pallas kernels, convolve(): pl.pallas_call(functools.partial(convolve_kernel, count), in_specs=[VMEM]...  5.23 us
    all_to_all x1, starting transfers between devices, local(): lax.all_to_all(gated, ('seq', 'tp'), split_axis=0, concat_axis=0, tiled=T...  4.33 us
  transfers between devices with their start and end apart: 12, of which 5 were waited for; matrix products, arithmetic and copies ran while one was open for 0% of the time, Pallas kernels for 7%

profile of v1, /device:TPU:0, one launch (start us, length us, event | category | flops | bytes accessed | tf_op | source)
XLA Modules:
  0.0 95.7 jit_solution(17103139913075104827)
XLA Ops:
  0.0 0.0 copy-start
  0.0 1.9 %copy-done = f32[2,2,2,384,256]{4,3,2,1,0:T(8,128)S(1)} copy-done((f32[2,2,2,384,256]{4,3,2,1,0:T(8,128)S(1)}, f32[2,2,2,384,256]{4,3,2,1,0:T(8,128)}, u32[]{:S(2)}) %copy-start) | copy-done | bytes 3145752
  1.9 3.5 %shard_map.83 = bf16[8,8,32,384]{3,2,1,0:T(8,128)(2,1)} custom-call(f32[2,2,2,384,256]{4,3,2,1,0:T(8,128)S(1)} %copy-done), custom_call_target="tpu_custom_call" | custom-call | tf_op jit(solution)/shard_map/pallas_call | solution.py:89
  5.4 0.0 copy-start.12
  5.4 0.0 copy-start.1
  5.4 7.4 %all-to-all-start = ((bf16[8,8,32,384]{3,2,1,0:T(8,128)(2,1)}), bf16[8,8,32,384]{3,2,1,0:T(8,128)(2,1)S(1)}, u32[]{:S(2)}, u32[]{:S(2)}) async-start(bf16[8,8,32,384]{3,2,1,0:T(8,128)(2,1)} %shard_map.83), calls=%async_computation | async-start | bytes 3145728 | tf_op jit(solution)/shard_map/all_to_all | solution.py:275
  12.8 0.0 copy-done.12
  12.8 0.0 copy-start.10
  12.8 0.0 copy-start.11
  12.9 8.6 %all_gather.3.tokens_ref = bf16[384,1024]{1,0:T(8,128)(2,1)S(1)} all-gather(bf16[96,1024]{1,0:T(8,128)(2,1)S(1)} %copy-done.12), channel_id=1, replica_groups=mesh['seq'=8,'tp'=4] {'tp'}, dimensions={0}, use_global_device_ids=true | all-gather | bytes 983040 | tf_op jit(solution)/shard_map/all_gather | solution.py:276
  21.5 0.0 copy-done.1
  21.5 1.4 %shard_map.82 = (bf16[3,1,32,384]{3,2,1,0:T(8,128)(2,1)S(1)}, bf16[3,1,32,384]{3,2,1,0:T(8,128)(2,1)S(1)}, bf16[3,1,32,384]{3,2,1,0:T(8,128)(2,1)S(1)}, bf16[3,1...) custom-call(bf16[384,1024]{1,0:T(8,128)(2,1)S(1)} %all_gather.3.toke, ...), custom_call_target="tpu_custom_call" | custom-call | tf_op jit(solution)/shard_map/pallas_call | solution.py:120
  22.9 2.2 %collective-permute-start = (bf16[3,1,32,384]{3,2,1,0:T(8,128)(2,1)S(1)}, bf16[3,1,32,384]{3,2,1,0:T(8,128)(2,1)S(1)}, u32[]{:S(2)}, u32[]{:S(2)}) collective-permute-start(bf16[3,1,32,384]{3,2,1,0:T(8,128)(2,1)S(1)} %get-tuple-element.14), channel_id=1, source_target_pairs={{0,4},{4,8},{8,12},{12,16},{16,20},{20,24},{24,28},{28,0},{1,5},{5... | collective-permute-start | bytes 221192 | tf_op jit(solution)/shard_map/ppermute | solution.py:279
  25.1 1.5 %collective-permute-start.1 = (bf16[3,1,32,384]{3,2,1,0:T(8,128)(2,1)S(1)}, bf16[3,1,32,384]{3,2,1,0:T(8,128)(2,1)S(1)}, u32[]{:S(2)}, u32[]{:S(2)}) collective-permute-start(bf16[3,1,32,384]{3,2,1,0:T(8,128)(2,1)S(1)} %get-tuple-element.15), channel_id=1, source_target_pairs={{0,8},{4,12},{8,16},{12,20},{16,24},{20,28},{24,0},{28,4},{1,9},{5... | collective-permute-start | bytes 221192 | tf_op jit(solution)/shard_map/ppermute | solution.py:279
  26.5 2.4 %collective-permute-start.2 = (bf16[3,1,32,384]{3,2,1,0:T(8,128)(2,1)S(1)}, bf16[3,1,32,384]{3,2,1,0:T(8,128)(2,1)S(1)}, u32[]{:S(2)}, u32[]{:S(2)}) collective-permute-start(bf16[3,1,32,384]{3,2,1,0:T(8,128)(2,1)S(1)} %get-tuple-element.16), channel_id=1, source_target_pairs={{0,12},{4,16},{8,20},{12,24},{16,28},{20,0},{24,4},{28,8},{1,13},{... | collective-permute-start | bytes 221192 | tf_op jit(solution)/shard_map/ppermute | solution.py:279
  28.9 1.5 %collective-permute-start.3 = (bf16[3,1,32,384]{3,2,1,0:T(8,128)(2,1)S(1)}, bf16[3,1,32,384]{3,2,1,0:T(8,128)(2,1)S(1)}, u32[]{:S(2)}, u32[]{:S(2)}) collective-permute-start(bf16[3,1,32,384]{3,2,1,0:T(8,128)(2,1)S(1)} %get-tuple-element.17), channel_id=1, source_target_pairs={{0,16},{4,20},{8,24},{12,28},{16,0},{20,4},{24,8},{28,12},{1,17},{... | collective-permute-start | bytes 221192 | tf_op jit(solution)/shard_map/ppermute | solution.py:279
  30.4 2.4 %collective-permute-start.4 = (bf16[3,1,32,384]{3,2,1,0:T(8,128)(2,1)S(1)}, bf16[3,1,32,384]{3,2,1,0:T(8,128)(2,1)S(1)}, u32[]{:S(2)}, u32[]{:S(2)}) collective-permute-start(bf16[3,1,32,384]{3,2,1,0:T(8,128)(2,1)S(1)} %get-tuple-element.18), channel_id=1, source_target_pairs={{0,20},{4,24},{8,28},{12,0},{16,4},{20,8},{24,12},{28,16},{1,21},{... | collective-permute-start | bytes 221192 | tf_op jit(solution)/shard_map/ppermute | solution.py:279
  32.7 13.6 %collective-permute-done.refs_1_ = bf16[3,1,32,384]{3,2,1,0:T(8,128)(2,1)S(1)} collective-permute-done((bf16[3,1,32,384]{3,2,1,0:T(8,128)(2,1)S(1)}, bf16[3,1,32,384]{3,2,1,0:T(8,128)(2,1)S(1)}, u32[]{:S(2)}, u32[]{:S(2)}) %collective-permute-start) | collective-permute-done | bytes 73760 | tf_op jit(solution)/shard_map/ppermute | solution.py:279
  46.3 0.0 collective-permute-start.7
  46.4 0.0 collective-permute-done.1.refs_2_
  46.4 1.5 %collective-permute-start.8 = (bf16[256,1024]{1,0:T(8,128)(2,1)}, bf16[256,1024]{1,0:T(8,128)(2,1)S(1)}, u32[]{:S(2)}, u32[]{:S(2)}) collective-permute-start(bf16[256,1024]{1,0:T(8,128)(2,1)} %refs_0_.1), channel_id=1, source_target_pairs={{0,2},{1,3},{2,0},{3,1},{4,6},{5,7},{6,4},{7,5},{8,10},{9,11},{10,... | collective-permute-start | bytes 1572872 | tf_op jit(solution)/shard_map/ppermute | solution.py:283
  47.8 11.8 %collective-permute-done.2.refs_3_ = bf16[3,1,32,384]{3,2,1,0:T(8,128)(2,1)S(1)} collective-permute-done((bf16[3,1,32,384]{3,2,1,0:T(8,128)(2,1)S(1)}, bf16[3,1,32,384]{3,2,1,0:T(8,128)(2,1)S(1)}, u32[]{:S(2)}, u32[]{:S(2)}) %collective-permute-start.2) | collective-permute-done | bytes 73760 | tf_op jit(solution)/shard_map/ppermute | solution.py:279
  59.6 0.0 collective-permute-start.9
  59.6 0.0 collective-permute-done.3.refs_4_
  59.6 3.1 %collective-permute-start.5 = (bf16[3,1,32,384]{3,2,1,0:T(8,128)(2,1)S(1)}, bf16[3,1,32,384]{3,2,1,0:T(8,128)(2,1)S(1)}, u32[]{:S(2)}, u32[]{:S(2)}) collective-permute-start(bf16[3,1,32,384]{3,2,1,0:T(8,128)(2,1)S(1)} %get-tuple-element.19), channel_id=1, source_target_pairs={{0,24},{4,28},{8,0},{12,4},{16,8},{20,12},{24,16},{28,20},{1,25},{... | collective-permute-start | bytes 221192 | tf_op jit(solution)/shard_map/ppermute | solution.py:279
  62.8 0.0 collective-permute-done.4.refs_5_
  62.8 0.0 copy-start.3
  62.8 0.6 copy-done.3
  63.4 0.5 collective-permute-start.6
  63.9 1.5 %collective-permute-done.5.refs_6_ = bf16[3,1,32,384]{3,2,1,0:T(8,128)(2,1)S(1)} collective-permute-done((bf16[3,1,32,384]{3,2,1,0:T(8,128)(2,1)S(1)}, bf16[3,1,32,384]{3,2,1,0:T(8,128)(2,1)S(1)}, u32[]{:S(2)}, u32[]{:S(2)}) %collective-permute-start.5) | collective-permute-done | bytes 73760 | tf_op jit(solution)/shard_map/ppermute | solution.py:279
  65.4 0.0 copy-start.5
  65.4 0.6 copy-done.5
  66.0 1.9 %collective-permute-done.6.refs_7_ = bf16[3,1,32,384]{3,2,1,0:T(8,128)(2,1)S(1)} collective-permute-done((bf16[3,1,32,384]{3,2,1,0:T(8,128)(2,1)S(1)}, bf16[3,1,32,384]{3,2,1,0:T(8,128)(2,1)S(1)}, u32[]{:S(2)}, u32[]{:S(2)}) %collective-permute-start.6) | collective-permute-done | bytes 73760 | tf_op jit(solution)/shard_map/ppermute | solution.py:279
  67.9 0.0 copy-start.7
  67.9 0.6 copy-done.7
  68.5 0.0 all-to-all-done.refs_8_
  68.5 0.0 copy-done.10
  68.5 0.0 copy-done.11
  68.5 0.0 copy-start.2
  68.6 1.3 %copy-done.2 = bf16[768,768]{1,0:T(8,128)(2,1)S(1)} copy-done((bf16[768,768]{1,0:T(8,128)(2,1)S(1)}, bf16[768,768]{1,0:T(8,128)(2,1)}, u32[]{:S(2)}) %copy-start.2) | copy-done | bytes 1179672
  69.8 0.0 copy-start.4
  69.8 0.9 copy-done.4
  70.7 0.0 copy-start.6
  70.7 0.9 copy-done.6
  71.6 0.0 copy-start.8
  71.6 0.9 copy-done.8
  72.5 0.0 copy-start.9
  72.5 0.8 copy-done.9
  73.3 5.2 %shard_map.84 = bf16[8,4,32,96]{3,2,1,0:T(8,128)(2,1)} custom-call(bf16[3,1,32,384]{3,2,1,0:T(8,128)(2,1)S(1)} %get-tuple-element.13.refs_0_, bf16[3,1,32,384]{3,2,1,0:T(8,128)(2,1)S(1)} %collective-permute-done.refs_1_, bf16[3,1,32,384]{3,2,1,0:T(8,128)(2,1)S(1)} %collective-permute-done.1.refs_2_, ...), custom_call_target="tpu_custom_call" | custom-call | tf_op jit(solution)/shard_map/pallas_call | solution.py:229
  78.5 4.3 %all-to-all-start.1 = ((bf16[32,32,96]{2,1,0:T(8,128)(2,1)}), bf16[32,32,96]{2,1,0:T(8,128)(2,1)S(1)}, u32[]{:S(2)}, u32[]{:S(2)}) async-start(bf16[32,32,96]{2,1,0:T(8,128)(2,1)} %bitcast), calls=%async_computation.1 | async-start | bytes 524288 | tf_op jit(solution)/shard_map/all_to_all | solution.py:288
  82.8 0.0 collective-permute-done.7.refs_1_
  82.9 0.0 collective-permute-done.8.refs_2_
  82.9 0.0 collective-permute-done.9.refs_3_
  82.9 10.6 %all-to-all-done.1 = bf16[32,32,96]{2,1,0:T(8,128)(2,1)S(1)} async-done(((bf16[32,32,96]{2,1,0:T(8,128)(2,1)}), bf16[32,32,96]{2,1,0:T(8,128)(2,1)S(1)}, u32[]{:S(2)}, u32[]{:S(2)}) %all-to-all-start.1) | async-done | bytes 196640 | tf_op jit(solution)/shard_map/all_to_all | solution.py:288
  93.4 2.2 %shard_map.85 = bf16[96,1024]{1,0:T(8,128)(2,1)} custom-call(bf16[8,4,32,96]{3,2,1,0:T(8,128)(2,1)S(1)} %bitcast.2, bf16[256,1024]{1,0:T(8,128)(2,1)} %refs_0_.1, bf16[256,1024]{1,0:T(8,128)(2,1)S(1)} %collective-permute-done.7.refs_1_, bf16[256,1024]{1,0:T(8,128)(2,1)S(1)} %collective-permute-done.8.refs_2_, ...), custom_call_target="tpu_custom_call" | custom-call | tf_op jit(solution)/shard_map/pallas_call | solution.py:262
Async XLA Ops:
  0.0 1.9 %copy-start = (f32[2,2,2,384,256]{4,3,2,1,0:T(8,128)S(1)}, f32[2,2,2,384,256]{4,3,2,1,0:T(8,128)}, u32[]{:S(2)}) copy-start(f32[2,2,2,384,256]{4,3,2,1,0:T(8,128)} %spectra_ref.1) | copy-start | bytes 9437188
  5.4 7.4 %copy-start.12 = (bf16[96,1024]{1,0:T(8,128)(2,1)S(1)}, bf16[96,1024]{1,0:T(8,128)(2,1)}, u32[]{:S(2)}) copy-start(bf16[96,1024]{1,0:T(8,128)(2,1)} %param.8) | copy-start | bytes 589828
  5.4 16.0 %copy-start.1 = (bf16[3,1024,256]{2,1,0:T(8,128)(2,1)S(1)}, bf16[3,1024,256]{2,1,0:T(8,128)(2,1)}, u32[]{:S(2)}) copy-start(bf16[3,1024,256]{2,1,0:T(8,128)(2,1)} %weight_ref.1) | copy-start | bytes 4718596
  5.4 63.1 %all-to-all-start = ((bf16[8,8,32,384]{3,2,1,0:T(8,128)(2,1)}), bf16[8,8,32,384]{3,2,1,0:T(8,128)(2,1)S(1)}, u32[]{:S(2)}, u32[]{:S(2)}) async-start(bf16[8,8,32,384]{3,2,1,0:T(8,128)(2,1)} %shard_map.83), calls=%async_computation | async-start | bytes 3145728 | tf_op jit(solution)/shard_map/all_to_all | solution.py:275
  12.8 55.7 %copy-start.10 = (f32[3,3,256]{2,1,0:T(4,128)S(1)}, f32[3,3,256]{2,1,0:T(4,128)}, u32[]{:S(2)}) copy-start(f32[3,3,256]{2,1,0:T(4,128)} %refs_9_.1) | copy-start | bytes 27652
  12.8 55.7 %copy-start.11 = (f32[2,256]{1,0:T(2,128)S(1)}, f32[2,256]{1,0:T(2,128)}, u32[]{:S(2)}) copy-start(f32[2,256]{1,0:T(2,128)} %refs_10_.1) | copy-start | bytes 6148
  22.9 23.5 %collective-permute-start = (bf16[3,1,32,384]{3,2,1,0:T(8,128)(2,1)S(1)}, bf16[3,1,32,384]{3,2,1,0:T(8,128)(2,1)S(1)}, u32[]{:S(2)}, u32[]{:S(2)}) collective-permute-start(bf16[3,1,32,384]{3,2,1,0:T(8,128)(2,1)S(1)} %get-tuple-element.14), channel_id=1, source_target_pairs={{0,4},{4,8},{8,12},{12,16},{16,20},{20,24},{24,28},{28,0},{1,5},{5... | collective-permute-start | bytes 221192 | tf_op jit(solution)/shard_map/ppermute | solution.py:279
  25.1 21.3 %collective-permute-start.1 = (bf16[3,1,32,384]{3,2,1,0:T(8,128)(2,1)S(1)}, bf16[3,1,32,384]{3,2,1,0:T(8,128)(2,1)S(1)}, u32[]{:S(2)}, u32[]{:S(2)}) collective-permute-start(bf16[3,1,32,384]{3,2,1,0:T(8,128)(2,1)S(1)} %get-tuple-element.15), channel_id=1, source_target_pairs={{0,8},{4,12},{8,16},{12,20},{16,24},{20,28},{24,0},{28,4},{1,9},{5... | collective-permute-start | bytes 221192 | tf_op jit(solution)/shard_map/ppermute | solution.py:279
  26.5 33.1 %collective-permute-start.2 = (bf16[3,1,32,384]{3,2,1,0:T(8,128)(2,1)S(1)}, bf16[3,1,32,384]{3,2,1,0:T(8,128)(2,1)S(1)}, u32[]{:S(2)}, u32[]{:S(2)}) collective-permute-start(bf16[3,1,32,384]{3,2,1,0:T(8,128)(2,1)S(1)} %get-tuple-element.16), channel_id=1, source_target_pairs={{0,12},{4,16},{8,20},{12,24},{16,28},{20,0},{24,4},{28,8},{1,13},{... | collective-permute-start | bytes 221192 | tf_op jit(solution)/shard_map/ppermute | solution.py:279
  28.9 30.7 %collective-permute-start.3 = (bf16[3,1,32,384]{3,2,1,0:T(8,128)(2,1)S(1)}, bf16[3,1,32,384]{3,2,1,0:T(8,128)(2,1)S(1)}, u32[]{:S(2)}, u32[]{:S(2)}) collective-permute-start(bf16[3,1,32,384]{3,2,1,0:T(8,128)(2,1)S(1)} %get-tuple-element.17), channel_id=1, source_target_pairs={{0,16},{4,20},{8,24},{12,28},{16,0},{20,4},{24,8},{28,12},{1,17},{... | collective-permute-start | bytes 221192 | tf_op jit(solution)/shard_map/ppermute | solution.py:279
  30.4 32.4 %collective-permute-start.4 = (bf16[3,1,32,384]{3,2,1,0:T(8,128)(2,1)S(1)}, bf16[3,1,32,384]{3,2,1,0:T(8,128)(2,1)S(1)}, u32[]{:S(2)}, u32[]{:S(2)}) collective-permute-start(bf16[3,1,32,384]{3,2,1,0:T(8,128)(2,1)S(1)} %get-tuple-element.18), channel_id=1, source_target_pairs={{0,20},{4,24},{8,28},{12,0},{16,4},{20,8},{24,12},{28,16},{1,21},{... | collective-permute-start | bytes 221192 | tf_op jit(solution)/shard_map/ppermute | solution.py:279
  46.3 36.5 %collective-permute-start.7 = (bf16[256,1024]{1,0:T(8,128)(2,1)}, bf16[256,1024]{1,0:T(8,128)(2,1)S(1)}, u32[]{:S(2)}, u32[]{:S(2)}) collective-permute-start(bf16[256,1024]{1,0:T(8,128)(2,1)} %refs_0_.1), channel_id=1, source_target_pairs={{0,1},{1,0},{2,3},{3,2},{4,5},{5,4},{6,7},{7,6},{8,9},{9,8},{10,11... | collective-permute-start | bytes 1572872 | tf_op jit(solution)/shard_map/ppermute | solution.py:283
  46.4 36.5 %collective-permute-start.8 = (bf16[256,1024]{1,0:T(8,128)(2,1)}, bf16[256,1024]{1,0:T(8,128)(2,1)S(1)}, u32[]{:S(2)}, u32[]{:S(2)}) collective-permute-start(bf16[256,1024]{1,0:T(8,128)(2,1)} %refs_0_.1), channel_id=1, source_target_pairs={{0,2},{1,3},{2,0},{3,1},{4,6},{5,7},{6,4},{7,5},{8,10},{9,11},{10,... | collective-permute-start | bytes 1572872 | tf_op jit(solution)/shard_map/ppermute | solution.py:283
  59.6 23.2 %collective-permute-start.9 = (bf16[256,1024]{1,0:T(8,128)(2,1)}, bf16[256,1024]{1,0:T(8,128)(2,1)S(1)}, u32[]{:S(2)}, u32[]{:S(2)}) collective-permute-start(bf16[256,1024]{1,0:T(8,128)(2,1)} %refs_0_.1), channel_id=1, source_target_pairs={{0,3},{1,2},{2,1},{3,0},{4,7},{5,6},{6,5},{7,4},{8,11},{9,10},{10,... | collective-permute-start | bytes 1572872 | tf_op jit(solution)/shard_map/ppermute | solution.py:283
  59.6 5.7 %collective-permute-start.5 = (bf16[3,1,32,384]{3,2,1,0:T(8,128)(2,1)S(1)}, bf16[3,1,32,384]{3,2,1,0:T(8,128)(2,1)S(1)}, u32[]{:S(2)}, u32[]{:S(2)}) collective-permute-start(bf16[3,1,32,384]{3,2,1,0:T(8,128)(2,1)S(1)} %get-tuple-element.19), channel_id=1, source_target_pairs={{0,24},{4,28},{8,0},{12,4},{16,8},{20,12},{24,16},{28,20},{1,25},{... | collective-permute-start | bytes 221192 | tf_op jit(solution)/shard_map/ppermute | solution.py:279
  62.8 0.6 copy-start.3
  63.4 4.5 %collective-permute-start.6 = (bf16[3,1,32,384]{3,2,1,0:T(8,128)(2,1)S(1)}, bf16[3,1,32,384]{3,2,1,0:T(8,128)(2,1)S(1)}, u32[]{:S(2)}, u32[]{:S(2)}) collective-permute-start(bf16[3,1,32,384]{3,2,1,0:T(8,128)(2,1)S(1)} %get-tuple-element.20), channel_id=1, source_target_pairs={{0,28},{4,0},{8,4},{12,8},{16,12},{20,16},{24,20},{28,24},{1,29},{... | collective-permute-start | bytes 221192 | tf_op jit(solution)/shard_map/ppermute | solution.py:279
  65.4 0.6 copy-start.5
  67.9 0.6 copy-start.7
  68.5 1.3 %copy-start.2 = (bf16[768,768]{1,0:T(8,128)(2,1)S(1)}, bf16[768,768]{1,0:T(8,128)(2,1)}, u32[]{:S(2)}) copy-start(bf16[768,768]{1,0:T(8,128)(2,1)} %constant.4.clone.refs_11_) | copy-start | bytes 3538948
  69.8 0.9 copy-start.4
  70.7 0.9 copy-start.6
  71.6 0.9 copy-start.8
  72.5 0.8 copy-start.9
  78.5 14.9 %all-to-all-start.1 = ((bf16[32,32,96]{2,1,0:T(8,128)(2,1)}), bf16[32,32,96]{2,1,0:T(8,128)(2,1)S(1)}, u32[]{:S(2)}, u32[]{:S(2)}) async-start(bf16[32,32,96]{2,1,0:T(8,128)(2,1)} %bitcast), calls=%async_computation.1 | async-start | bytes 524288 | tf_op jit(solution)/shard_map/all_to_all | solution.py:288

commit v2 on v1

v2 whole, which is shorter than its diff:
```python
import functools
import math

import jax
import jax.numpy as jnp
import numpy as np
from jax import lax
from jax.experimental import pallas as pl
from jax.experimental.pallas import tpu as pltpu
from jax.sharding import PartitionSpec as P

VMEM = pl.BlockSpec(memory_space=pltpu.VMEM)
ANY = pl.BlockSpec(memory_space=pl.ANY)
MOST = 63 * 1024 * 1024
LANES = 128
INNER = 16
LIMIT = 20 * 1024 * 1024


def phase_rows(blocks, length):
    line = np.arange(length)
    angles = [
        2.0 * np.pi / (blocks * length) * np.outer(np.arange(blocks), line),
        2.0 * np.pi / length * (np.outer(INNER * np.arange(length // INNER), line) % length),
        2.0 * np.pi / length * (np.outer(np.arange(INNER), line) % length),
    ]
    return jnp.asarray(np.concatenate([part for a in angles for part in (np.cos(a), -np.sin(a))]), jnp.float32)


def build_table(phases_ref, top, table_ref):
    length = phases_ref.shape[1]
    outer = length // INNER
    cos_j, sin_j = phases_ref[top + 2 * outer : top + 2 * outer + INNER], phases_ref[top + 2 * outer + INNER :]
    for i in range(outer):
        cos_i, sin_i = phases_ref[top + i : top + i + 1], phases_ref[top + outer + i : top + outer + i + 1]
        cos = (cos_i * cos_j - sin_i * sin_j).astype(jnp.bfloat16)
        sin = (cos_i * sin_j + sin_i * cos_j).astype(jnp.bfloat16)
        table_ref[i * INNER : (i + 1) * INNER, :length] = cos
        table_ref[i * INNER : (i + 1) * INNER, length:] = sin
        table_ref[length + i * INNER : length + (i + 1) * INNER, :length] = -sin
        table_ref[length + i * INNER : length + (i + 1) * INNER, length:] = cos


def window_width(share, count):
    return -(-(share + 2 * count) // LANES) * LANES


def share_table(length, share, wide):
    columns = np.arange(length)
    table = np.zeros((length, length // share * wide))
    table[columns, columns // share * wide + columns % share] = 1.0
    return jnp.asarray(table, jnp.bfloat16)


def times(pair, k, size, direction):
    re, im = pair
    cos, sin = math.cos(2 * math.pi * k / size), direction * math.sin(2 * math.pi * k / size)
    return re * cos - im * sin, re * sin + im * cos


def forward_half(values):
    if len(values) == 1:
        return [(values[0], None), (values[0], None)]
    even, odd = forward_half(values[0::2]), forward_half(values[1::2])
    half = len(values)
    quarter = half // 2
    out = [None] * (half + 1)
    out[0] = (even[0][0] + odd[0][0], None)
    out[half] = (even[0][0] - odd[0][0], None)
    out[quarter] = (even[quarter][0], -odd[quarter][0])
    for k in range(1, quarter):
        re, im = times(odd[k], k, 2 * half, -1.0)
        out[k] = (even[k][0] + re, even[k][1] + im)
        out[half - k] = (even[k][0] - re, im - even[k][1])
    return out


def inverse_half(bins):
    half = len(bins) - 1
    if half == 1:
        return [bins[0][0] + bins[1][0]]
    quarter = half // 2
    even = [(bins[0][0] + bins[half][0], None)]
    odd = [(bins[0][0] - bins[half][0], None)]
    for k in range(1, quarter):
        (a, b), (c, d) = bins[k], bins[half - k]
        even.append((a + c, b - d))
        odd.append(times((a - c, b + d), k, 2 * half, 1.0))
    even.append((2.0 * bins[quarter][0], None))
    odd.append((-2.0 * bins[quarter][1], None))
    out = [None] * half
    out[0::2] = inverse_half(even)
    out[1::2] = inverse_half(odd)
    return out


def spectra_kernel(spectra_ref, out_ref, arriving, leaving, sems_in, sems_out):
    orders, parts, residues = spectra_ref.shape[:3]
    count, slabs, each, length = out_ref.shape
    fetches, stores = [], []
    for i in range(slabs):
        order, part, residue = i // (parts * residues), i // residues % parts, i % residues
        fetches.append(
            pltpu.make_async_copy(spectra_ref.at[order, part, residue], arriving.at[i], sems_in.at[i])
        )
        stores.append(pltpu.make_async_copy(leaving.at[i], out_ref.at[:, i], sems_out.at[i]))
    for fetch in fetches:
        fetch.start()
    for i, (fetch, store) in enumerate(zip(fetches, stores)):
        fetch.wait()
        leaving[i] = arriving[i].T.reshape(count, each, length).astype(jnp.bfloat16)
        store.start()
    for store in stores:
        store.wait()


def send_spectra(spectra, count):
    orders, parts, residues, length, channels = spectra.shape
    each = channels // count
    slabs = orders * parts * residues
    return pl.pallas_call(
        spectra_kernel,
        in_specs=[ANY],
        out_specs=ANY,
        out_shape=jax.ShapeDtypeStruct((count, slabs, each, length), jnp.bfloat16),
        scratch_shapes=[
            pltpu.VMEM((slabs, length, channels), jnp.float32),
            pltpu.VMEM((slabs, count, each, length), jnp.bfloat16),
            pltpu.SemaphoreType.DMA((slabs,)),
            pltpu.SemaphoreType.DMA((slabs,)),
        ],
        compiler_params=pltpu.CompilerParams(vmem_limit_bytes=MOST),
    )(spectra)


def tap_columns(taps_ref, skip_ref, gathered):
    branches = taps_ref.shape[0]
    for branch in range(branches):
        gathered[branch * 3 : branch * 3 + 3] = taps_ref[branch]
    gathered[9:11] = skip_ref[...]
    return gathered[...].T


def filter_lines(now, last, scale, lane):
    total = scale[0] * now
    rolls = []
    for back in (1, 2):
        rolled = pltpu.roll(now, back, 1)
        total = total + scale[back] * jnp.where(lane < back, last[back - 1], rolled)
        rolls.append(rolled)
    return total, rolls


def project_kernel(tokens_ref, weight_ref, taps_ref, skip_ref, *refs):
    mine_ref, other_ref, edge_ref = refs[:3]
    outs, (held, gathered, windows) = refs[3:-3], refs[-3:]
    count, pieces, each, length = held.shape
    across, channels, wide = windows.shape
    share = pieces * length // across
    branch = pl.program_id(0)
    me = lax.axis_index("seq")
    rows = jnp.dot(tokens_ref[...], weight_ref[0], preferred_element_type=jnp.float32)
    turned = [rows[piece * length : (piece + 1) * length].T for piece in range(pieces)]

    @pl.when(branch < 2)
    def _():
        for piece in range(pieces):
            held[:, piece] = turned[piece].reshape(count, each, length).astype(jnp.bfloat16)
        for shift in range(count // 2):
            to = lax.rem(me + 2 * shift, count)
            mine_ref[shift, 0] = held[to]
            other_ref[shift, 0] = held[jnp.bitwise_xor(to, 1)]

    @pl.when(branch == 2)
    def _():
        columns = tap_columns(taps_ref, skip_ref, gathered)
        scale = [jnp.broadcast_to(columns[:, 6 + i : 7 + i], (channels, length)) for i in range(3)]
        lane = lax.broadcasted_iota(jnp.int32, (channels, length), 1)
        last = [jnp.zeros((channels, length), jnp.float32)] * 2
        windows[...] = jnp.zeros_like(windows)
        for piece in range(pieces):
            now = turned[piece].astype(jnp.bfloat16).astype(jnp.float32)
            total, last = filter_lines(now, last, scale, lane)
            for part in range(length // share):
                window = total[:, part * share : (part + 1) * share]
                windows[piece * (length // share) + part, :, :share] = window.astype(jnp.bfloat16)
        for flip, out in enumerate(outs):
            out[...] = windows[jnp.bitwise_xor(lax.axis_index("tp"), flip)]
        edge = jnp.where(lane < 1, scale[1] * last[0], 0.0) + jnp.where(lane < 2, scale[2] * last[1], 0.0)
        edge = edge[:, :LANES] * (me < count - 1).astype(jnp.float32)
        if wide > LANES:
            edge = jnp.concatenate([edge, jnp.zeros((channels, wide - LANES), jnp.float32)], axis=1)
        total = jnp.zeros((each, wide), jnp.float32)
        for block in range(count):
            total = total + pltpu.roll(edge[block * each : (block + 1) * each], share + 2 * block, 1)
        edge_ref[...] = total.astype(jnp.bfloat16)


def project(tokens, weights, taps, skip, count, across, length):
    rows, depth = tokens.shape
    branches, _, channels = weights.shape
    each, pieces = channels // count, rows // length
    wide = window_width(rows // across, count)
    half = (count // 2, 1, pieces, each, length)
    return pl.pallas_call(
        project_kernel,
        grid=(branches,),
        in_specs=[
            pl.BlockSpec((rows, depth), lambda b: (0, 0)),
            pl.BlockSpec((1, depth, channels), lambda b: (b, 0, 0)),
            pl.BlockSpec(taps.shape, lambda b: (0, 0, 0)),
            pl.BlockSpec(skip.shape, lambda b: (0, 0)),
        ],
        out_specs=[
            pl.BlockSpec(half, lambda b: (0, jnp.minimum(b, 1), 0, 0, 0)),
            pl.BlockSpec(half, lambda b: (0, jnp.minimum(b, 1), 0, 0, 0)),
            pl.BlockSpec((each, wide), lambda b: (0, 0)),
        ]
        + [pl.BlockSpec((channels, wide), lambda b: (0, 0))] * across,
        out_shape=[
            jax.ShapeDtypeStruct((count // 2, 2) + half[2:], jnp.bfloat16),
            jax.ShapeDtypeStruct((count // 2, 2) + half[2:], jnp.bfloat16),
            jax.ShapeDtypeStruct((each, wide), jnp.bfloat16),
        ]
        + [jax.ShapeDtypeStruct((channels, wide), jnp.bfloat16)] * across,
        scratch_shapes=[
            pltpu.VMEM((count, pieces, each, length), jnp.bfloat16),
            pltpu.VMEM((16, channels), jnp.float32),
            pltpu.VMEM((across, channels, wide), jnp.bfloat16),
        ],
        compiler_params=pltpu.CompilerParams(vmem_limit_bytes=LIMIT),
    )(tokens, weights, taps, skip)


def pack_kernel(weight_ref, *refs):
    windows, outs = refs[: len(refs) // 2], refs[len(refs) // 2 :]
    for window, out in zip(windows, outs):
        wide = window.shape[1]
        out[:, :wide] = window[...]
        out[:, wide:] = weight_ref[...]


def pack(windows, weight):
    channels, wide = windows[0].shape
    shape = jax.ShapeDtypeStruct((channels, wide + weight.shape[1]), jnp.bfloat16)
    return pl.pallas_call(
        pack_kernel,
        in_specs=[VMEM] * (1 + len(windows)),
        out_specs=[VMEM] * len(windows),
        out_shape=[shape] * len(windows),
        compiler_params=pltpu.CompilerParams(vmem_limit_bytes=LIMIT),
    )(weight, *windows)


def relay_kernel(mine_ref, came_ref, *outs):
    for shift, out in enumerate(outs, 1):
        out[0] = mine_ref[shift]
        out[1] = came_ref[shift]


def relay(mine, came):
    shape = (2,) + mine.shape[1:]
    return pl.pallas_call(
        relay_kernel,
        in_specs=[VMEM] * 2,
        out_specs=[VMEM] * (mine.shape[0] - 1),
        out_shape=[jax.ShapeDtypeStruct(shape, jnp.bfloat16)] * (mine.shape[0] - 1),
        compiler_params=pltpu.CompilerParams(vmem_limit_bytes=LIMIT),
    )(mine, came)


def tiles_of(each, length):
    chunk, width = min(16, each), 128
    return [(slice(r, r + chunk), slice(c, c + width)) for r in range(0, each, chunk) for c in range(0, length, width)]


def part_of(cols, length, part):
    return slice(part * length + cols.start, part * length + cols.stop)


def twist_of(phases_ref, k, blocks, cols):
    return phases_ref[k : k + 1, cols], phases_ref[blocks + k : blocks + k + 1, cols]


def forward_tile(values, tile, lines, phases_ref, each, length):
    rows, cols = tile
    blocks = 2 * len(values)
    bins = forward_half(values)
    for k in range(blocks):
        cos, sin = twist_of(phases_ref, k, blocks, cols)
        re, im = bins[min(k, blocks - k)]
        if im is None:
            pair = (re * cos, re * sin)
        elif 2 * k < blocks:
            pair = (re * cos - im * sin, re * sin + im * cos)
        else:
            pair = (re * cos + im * sin, re * sin - im * cos)
        at = slice(k * each + rows.start, k * each + rows.stop)
        for part in range(2):
            lines[at, part_of(cols, length, part)] = pair[part].astype(jnp.bfloat16)


def respond(spectrum, start, order, spectra_ref, lines, each, length):
    residues = spectra_ref.shape[1] // 4
    for k in range(start // each, (start + spectrum.shape[0]) // each):
        at = k * each - start
        re, im = spectrum[at : at + each, :length], spectrum[at : at + each, length:]
        first = order * 2 * residues + k % residues
        gain_re = spectra_ref[k // residues, first].astype(jnp.float32)
        gain_im = spectra_ref[k // residues, first + residues].astype(jnp.float32)
        lines[k * each : (k + 1) * each, :length] = (re * gain_re - im * gain_im).astype(jnp.bfloat16)
        lines[k * each : (k + 1) * each, length:] = (-(re * gain_im) - im * gain_re).astype(jnp.bfloat16)


def inverse_tile(wave, tile, phases_ref, positions, each, length):
    rows, cols = tile
    blocks = 2 * positions
    turned = []
    for k in range(blocks):
        cos, sin = twist_of(phases_ref, k, blocks, cols)
        at = slice(k * each + rows.start, k * each + rows.stop)
        re, im = wave[at, cols], wave[at, part_of(cols, length, 1)]
        turned.append((re * cos - im * sin, re * sin + im * cos))
    bins = [(turned[0][0] * 2.0, None)]
    for k in range(1, positions):
        one, two = turned[k], turned[blocks - k]
        bins.append((one[0] + two[0], two[1] - one[1]))
    bins.append((turned[positions][0] * 2.0, None))
    return [value * (0.5 / (blocks * length)) for value in inverse_half(bins)]


def row_steps(blocks, each):
    step = max(each, min(blocks * each, 128))
    return [slice(start, start + step) for start in range(0, blocks * each, step)]


def flipped(array, flip, size):
    return lax.ppermute(array, "tp", [(i, i ^ flip) for i in range(size)])


def convolve_kernel(*refs):
    mine_in, came_in, spectra_in, phases_in, shares_in, taps_ref, skip_ref, edge_ref = refs[:8]
    shifted, refs = refs[8:-14], refs[-14:]
    out_ref, held, spectra_ref, phases_ref, shares_ref, table_ref, filtered, lines, wave = refs[:9]
    gathered, columns, leaving, sems, some = refs[9:]
    branches, positions, each, length = filtered.shape
    blocks = 2 * positions
    count = held.shape[0]
    pieces = positions // count
    slabs = spectra_ref.shape[1]
    me = lax.axis_index("seq")
    other = jnp.bitwise_xor(me, 1)

    inward = [
        pltpu.make_async_copy(mine_in.at[0], held.at[me], some.at[0]),
        pltpu.make_async_copy(came_in.at[0], held.at[other], some.at[1]),
    ]
    for shift, ref in enumerate(shifted, 1):
        for i, one in enumerate((me, other)):
            source = lax.rem(one + count - 2 * shift, count)
            inward.append(pltpu.make_async_copy(ref.at[i], held.at[source], some.at[2 * shift + i]))
    halves = [slice(0, slabs // 2), slice(slabs // 2, slabs)]
    phases = pltpu.make_async_copy(phases_in, phases_ref, sems.at[0])
    spectra = [
        pltpu.make_async_copy(spectra_in.at[:, half], spectra_ref.at[:, half], sems.at[1 + i])
        for i, half in enumerate(halves)
    ]
    shares = pltpu.make_async_copy(shares_in, shares_ref, sems.at[3])
    for copy in [phases] + inward:
        copy.start()
    columns[...] = tap_columns(taps_ref, skip_ref, gathered)
    mine = columns[pl.ds(pl.multiple_of(me * each, each), each), :]
    lane = lax.broadcasted_iota(jnp.int32, (each, length), 1)
    phases.wait()
    for copy in inward:
        copy.wait()
    for copy in spectra + [shares]:
        copy.start()
    build_table(phases_ref, 2 * blocks, table_ref)
    for branch in range(branches):
        last = [jnp.zeros((each, length), jnp.float32)] * 2
        scale = [jnp.broadcast_to(mine[:, branch * 3 + i : branch * 3 + i + 1], (each, length)) for i in range(3)]
        for p in range(positions):
            now = held[p // pieces, branch, p % pieces].astype(jnp.float32)
            filtered[branch, p], last = filter_lines(now, last, scale, lane)
    skips = [jnp.broadcast_to(mine[:, 9 + order : 10 + order], (each, LANES)) for order in range(2)]

    def through(order):
        spectra[order].wait()
        for rows in row_steps(blocks, each):
            spectrum = jnp.dot(lines[rows], table_ref[...], preferred_element_type=jnp.float32)
            respond(spectrum, rows.start, order, spectra_ref, lines, each, length)
        for rows in row_steps(blocks, each):
            wave[rows] = jnp.dot(lines[rows], table_ref[...], preferred_element_type=jnp.float32)

    tiles = tiles_of(each, length)
    for tile in tiles:
        forward_tile([filtered[(0, p) + tile] for p in range(positions)], tile, lines, phases_ref, each, length)
    through(0)
    for tile in tiles:
        values = inverse_tile(wave, tile, phases_ref, positions, each, length)
        for p, value in enumerate(values):
            values[p] = filtered[(1, p) + tile] * (value + skips[0][tile[0]] * filtered[(0, p) + tile])
            filtered[(0, p) + tile] = values[p]
        forward_tile(values, tile, lines, phases_ref, each, length)
    through(1)
    for tile in tiles:
        for p, value in enumerate(inverse_tile(wave, tile, phases_ref, positions, each, length)):
            filtered[(0, p) + tile] = value + skips[1][tile[0]] * filtered[(0, p) + tile]
    shares.wait()
    wide = out_ref.shape[3]
    parts = shares_ref.shape[1] // wide
    flat = filtered[0].reshape(positions * each, length).astype(jnp.bfloat16)
    spread_out = jnp.dot(flat, shares_ref[...], preferred_element_type=jnp.float32)
    for p in range(positions):
        for part in range(parts):
            block = spread_out[p * each : (p + 1) * each, part * wide : (part + 1) * wide]
            leaving[p // pieces, p % pieces * parts + part] = block.astype(jnp.bfloat16)
    following = lax.rem(me + 1, count)
    leaving[following, 0] = leaving[following, 0] + edge_ref[...]
    store = pltpu.make_async_copy(leaving, out_ref, sems.at[4])
    store.start()
    store.wait()


def convolve(mine, came, shifted, spectra, taps, skip, edge, across):
    count, slabs, each, length = spectra.shape
    branches, pieces = mine.shape[1:3]
    positions = count * pieces
    blocks = 2 * positions
    channels = taps.shape[2]
    phases = phase_rows(blocks, length)
    share = pieces * length // across
    wide = window_width(share, count)
    shares = share_table(length, share, wide)
    return pl.pallas_call(
        convolve_kernel,
        in_specs=[ANY] * 5 + [VMEM] * 3 + [ANY] * len(shifted),
        out_specs=ANY,
        out_shape=jax.ShapeDtypeStruct((count, across, each, wide), jnp.bfloat16),
        scratch_shapes=[
            pltpu.VMEM((count, branches, pieces, each, length), jnp.bfloat16),
            pltpu.VMEM(spectra.shape, spectra.dtype),
            pltpu.VMEM(phases.shape, phases.dtype),
            pltpu.VMEM(shares.shape, shares.dtype),
            pltpu.VMEM((2 * length, 2 * length), jnp.bfloat16),
            pltpu.VMEM((branches, positions, each, length), jnp.float32),
            pltpu.VMEM((blocks * each, 2 * length), jnp.bfloat16),
            pltpu.VMEM((blocks * each, 2 * length), jnp.float32),
            pltpu.VMEM((16, channels), jnp.float32),
            pltpu.VMEM((channels, 16), jnp.float32),
            pltpu.VMEM((count, across, each, wide), jnp.bfloat16),
            pltpu.SemaphoreType.DMA((5,)),
            pltpu.SemaphoreType.DMA((count,)),
        ],
        compiler_params=pltpu.CompilerParams(vmem_limit_bytes=MOST),
    )(mine, came, spectra, phases, shares, taps, skip, edge, *shifted)


def finish_kernel(share, carried_ref, own_ref, weight_ref, *refs):
    came, out_ref = refs[:-1], refs[-1]
    count, across, each, wide = carried_ref.shape
    me = lax.axis_index("tp")
    before = lax.rem(lax.axis_index("seq") + count - 1, count)
    first = (me == 0).astype(jnp.float32)
    lane = lax.broadcasted_iota(jnp.int32, (each, wide), 1)
    pairs = [(own_ref[...], weight_ref[...])] + [(ref[:, :wide], ref[:, wide:]) for ref in came]
    total = jnp.zeros((wide, out_ref.shape[1]), jnp.float32)
    for flip, (gate, weight) in enumerate(pairs):
        source = jnp.bitwise_xor(me, flip)
        edge = carried_ref[before, source].astype(jnp.float32) * first
        edges = [
            jnp.where(lane < 2, pltpu.roll(edge, wide - share - 2 * block, 1), 0.0) for block in range(count)
        ]
        gate = gate.astype(jnp.float32) + jnp.concatenate(edges, axis=0)
        part = carried_ref[:, source].astype(jnp.float32).reshape(count * each, wide)
        total = total + lax.dot_general(
            (part * gate).astype(jnp.bfloat16), weight, (((0,), (0,)), ((), ())), preferred_element_type=jnp.float32
        )
    out_ref[...] = total[:share].astype(jnp.bfloat16)


def finish(carried, own, weight, came, share):
    return pl.pallas_call(
        functools.partial(finish_kernel, share),
        in_specs=[VMEM] * (3 + len(came)),
        out_specs=VMEM,
        out_shape=jax.ShapeDtypeStruct((share, weight.shape[1]), jnp.bfloat16),
        compiler_params=pltpu.CompilerParams(vmem_limit_bytes=LIMIT),
    )(carried, own, weight, *came)


def spread(array, axes):
    return lax.all_to_all(array, axes, split_axis=0, concat_axis=0, tiled=True)


def local(tokens, w_in, short_taps, skip_bias, filter_spectra, w_out):
    count, across = lax.axis_size("seq"), lax.axis_size("tp")
    length = filter_spectra.shape[3]
    spectra = spread(send_spectra(filter_spectra, count), "seq")
    gathered = lax.all_gather(tokens, "tp", axis=0, tiled=True)
    mine, other, edge, own, *windows = project(gathered, w_in, short_taps, skip_bias, count, across, length)
    came = lax.ppermute(other, "seq", [(i, i ^ 1) for i in range(count)])
    onward = relay(mine, came)
    shifted = [
        lax.ppermute(array, "seq", [(i, (i + 2 * shift) % count) for i in range(count)])
        for shift, array in enumerate(onward, 1)
    ]
    packed = [flipped(array, flip, across) for flip, array in enumerate(pack(windows, w_out), 1)]
    carried = convolve(mine, came, shifted, spectra, short_taps, skip_bias, edge, across)
    shape = carried.shape
    carried = spread(carried.reshape((count * across,) + shape[2:]), ("seq", "tp"))
    return finish(carried.reshape(shape), own, w_out, packed, tokens.shape[0])


def solution(mesh):
    in_specs = (
        P(("seq", "tp"), None),
        P(None, None, "tp"),
        P(None, None, "tp"),
        P(None, "tp"),
        P(None, None, "seq", None, "tp"),
        P("tp", None),
    )
    out_specs = P(("seq", "tp"), None)
    return jax.shard_map(local, mesh=mesh, in_specs=in_specs, out_specs=out_specs, check_vma=False)
```

time: 96.3 us -> 81.8 us (0.85)
  waiting for transfers between devices: 39.4 us -> 29.7 us
  local copies, waits for them, and re-layouts: 8.51 us -> 0.68 us
  Pallas kernels: 12.4 us -> 17.2 us
  starting transfers between devices: 26.7 us -> 25.1 us
    unnamed x26 -> x20, local copies, waits for them, and re-layouts: 8.51 us -> 0.68 us
    ppermute x10 -> x7, waiting for transfers between devices: 28.8 us -> 22.2 us  [the longest x3 10.5 us: local(): lax.ppermute(array, 'seq', [(i, (i + 2 * shift) % count) for i in range(c...]
    pallas_call x3 -> x5, Pallas kernels: 11 us -> 14.9 us  [the longest x1 7.77 us: convolve(): pl.pallas_call(convolve_kernel, in_specs=[ANY] * 5 + [VMEM] * 3 + [ANY] *...]
    all_to_all x2, waiting for transfers between devices: 10.6 us -> 7.58 us  [spread(): return lax.all_to_all(array, axes, split_axis=0, concat_axis=0, tiled=True)]
    ppermute x10 -> x7, starting transfers between devices: 15 us -> 12.9 us  [the longest x3 9.23 us: local(): lax.ppermute(array, 'seq', [(i, (i + 2 * shift) % count) for i in range(c...]
  transfers between devices with their start and end apart: 12 -> 9, of which waited for: 5 -> 5; matrix products, arithmetic and copies ran while one was open for 0% -> 0% of each run, Pallas kernels for 7% -> 14%
where the time goes in v2:
time: 81.8 us; the launch traced here: 81.4 us
  waiting for transfers between devices  29.7 us (36%)
  starting transfers between devices  25.1 us (31%)
  Pallas kernels  17.2 us (21%)
  blocking collectives  8.6 us (11%)
    all_to_all x2, starting transfers between devices, spread(): return lax.all_to_all(array, axes, split_axis=0, concat_axis=0, tiled=True)  12.2 us
    ppermute x3, waiting for transfers between devices, local(): lax.ppermute(array, 'seq', [(i, (i + 2 * shift) % count) for i in range(c...  10.5 us
    ppermute x3, starting transfers between devices, local(): lax.ppermute(array, 'seq', [(i, (i + 2 * shift) % count) for i in range(c...  9.23 us
    ppermute x1, waiting for transfers between devices, local(): came = lax.ppermute(other, 'seq', [(i, i ^ 1) for i in range(count)])  8.67 us
    all_gather x1, blocking collectives, local(): gathered = lax.all_gather(tokens, 'tp', axis=0, tiled=True)  8.6 us
    pallas_call x1, Pallas kernels, convolve(): pl.pallas_call(convolve_kernel, in_specs=[ANY] * 5 + [VMEM] * 3 + [ANY] *...  7.77 us
    all_to_all x2, waiting for transfers between devices, spread(): return lax.all_to_all(array, axes, split_axis=0, concat_axis=0, tiled=True)  7.58 us
    ppermute x3, waiting for transfers between devices, flipped(): return lax.ppermute(array, 'tp', [(i, i ^ flip) for i in range(size)])  3 us
  transfers between devices with their start and end apart: 9, of which 5 were waited for; matrix products, arithmetic and copies ran while one was open for 0% of the time, Pallas kernels for 14%

profile of v2, /device:TPU:0, one launch (start us, length us, event | category | flops | bytes accessed | tf_op | source)
XLA Modules:
  0.0 81.4 jit_solution(2653687080546744732)
XLA Ops:
  0.0 2.9 %shard_map.83 = bf16[8,8,32,384]{3,2,1,0:T(8,128)(2,1)} custom-call(f32[2,2,2,384,256]{4,3,2,1,0:T(8,128)} %spectra_ref.1), custom_call_target="tpu_custom_call" | custom-call | tf_op jit(solution)/shard_map/pallas_call | solution.py:121
  2.9 0.0 copy-start.7
  2.9 0.0 copy-start.1
  2.9 0.0 copy-start.4
  3.0 0.0 copy-start.6
  3.0 7.4 %all-to-all-start = ((bf16[8,8,32,384]{3,2,1,0:T(8,128)(2,1)}), bf16[8,8,32,384]{3,2,1,0:T(8,128)(2,1)}, u32[]{:S(2)}, u32[]{:S(2)}) async-start(bf16[8,8,32,384]{3,2,1,0:T(8,128)(2,1)} %shard_map.83), calls=%async_computation | async-start | bytes 3145728 | tf_op jit(solution)/shard_map/all_to_all | solution.py:494
  10.4 0.0 copy-done.7
  10.4 8.6 %all_gather.3.tokens_ref = bf16[384,1024]{1,0:T(8,128)(2,1)S(1)} all-gather(bf16[96,1024]{1,0:T(8,128)(2,1)S(1)} %copy-done.7), channel_id=1, replica_groups=mesh['seq'=8,'tp'=4] {'tp'}, dimensions={0}, use_global_device_ids=true | all-gather | bytes 983040 | tf_op jit(solution)/shard_map/all_gather | solution.py:501
  19.0 0.0 copy-done.1
  19.0 0.0 copy-done.4
  19.0 0.0 copy-done.6
  19.0 0.0 copy-start
  19.0 2.2 %shard_map.82 = (bf16[4,2,1,32,384]{4,3,2,1,0:T(8,128)(2,1)S(1)}, bf16[4,2,1,32,384]{4,3,2,1,0:T(8,128)(2,1)S(1)}, bf16[32,128]{1,0:T(8,128)(2,1)S(1)}, bf16[256...) custom-call(bf16[384,1024]{1,0:T(8,128)(2,1)S(1)} %all_gather.3.toke, ...), custom_call_target="tpu_custom_call" | custom-call | tf_op jit(solution)/shard_map/pallas_call | solution.py:205
  21.3 0.0 copy-start.5
  21.3 0.0 copy-start.2
  21.3 2.1 %collective-permute-start = (bf16[4,2,1,32,384]{4,3,2,1,0:T(8,128)(2,1)S(1)}, bf16[4,2,1,32,384]{4,3,2,1,0:T(8,128)(2,1)S(1)}, u32[]{:S(2)}, u32[]{:S(2)}) collective-permute-start(bf16[4,2,1,32,384]{4,3,2,1,0:T(8,128)(2,1)S(1)} %get-tuple-element.19), channel_id=1, source_target_pairs={{0,4},{4,0},{8,12},{12,8},{16,20},{20,16},{24,28},{28,24},{1,5},{5... | collective-permute-start | bytes 589832 | tf_op jit(solution)/shard_map/ppermute | solution.py:503
  23.4 8.7 %collective-permute-done.came_ref.refs_1_ = bf16[4,2,1,32,384]{4,3,2,1,0:T(8,128)(2,1)S(1)} collective-permute-done((bf16[4,2,1,32,384]{4,3,2,1,0:T(8,128)(2,1)S(1)}, bf16[4,2,1,32,384]{4,3,2,1,0:T(8,128)(2,1)S(1)}, u32[]{:S(2)}, u32[]{:S(2)}) %collective-permute-start) | collective-permute-done | bytes 196640 | tf_op jit(solution)/shard_map/ppermute | solution.py:503
  32.0 0.0 copy-start.3
  32.1 0.5 collective-permute-start.1
  32.5 8.8 %collective-permute-start.2 = (bf16[2,2,1,32,384]{4,3,2,1,0:T(8,128)(2,1)S(1)}, bf16[2,2,1,32,384]{4,3,2,1,0:T(8,128)(2,1)S(1)}, u32[]{:S(2)}, u32[]{:S(2)}) collective-permute-start(bf16[2,2,1,32,384]{4,3,2,1,0:T(8,128)(2,1)S(1)} %get-tuple-element.22), channel_id=1, source_target_pairs={{0,16},{4,20},{8,24},{12,28},{16,0},{20,4},{24,8},{28,12},{1,17},{... | collective-permute-start | bytes 294920 | tf_op jit(solution)/shard_map/ppermute | solution.py:506
  41.3 0.0 collective-permute-start.3
  41.3 0.0 copy-done
  41.3 1.4 %shard_map.86 = (bf16[256,1152]{1,0:T(8,128)(2,1)}, bf16[256,1152]{1,0:T(8,128)(2,1)}, bf16[256,1152]{1,0:T(8,128)(2,1)}) custom-call(bf16[256,1024]{1,0:T(8,128)(2,1)S(1)} %copy-done, bf16[256,128]{1,0:T(8,128)(2,1)S(1)} %get-tuple-element.25.refs_0_, bf16[256,128]{1,0:T(8,128)(2,1)S(1)} %get-tuple-element.26.refs_1_, ...), custom_call_target="tpu_custom_call" | custom-call | tf_op jit(solution)/shard_map/pallas_call | solution.py:246
  42.7 0.0 copy-done.5
  42.7 0.0 collective-permute-start.4
  42.7 1.5 %collective-permute-start.5 = (bf16[256,1152]{1,0:T(8,128)(2,1)}, bf16[256,1152]{1,0:T(8,128)(2,1)}, u32[]{:S(2)}, u32[]{:S(2)}) collective-permute-start(bf16[256,1152]{1,0:T(8,128)(2,1)} %get-tuple-element.29), channel_id=1, source_target_pairs={{0,2},{1,3},{2,0},{3,1},{4,6},{5,7},{6,4},{7,5},{8,10},{9,11},{10,... | collective-permute-start | bytes 1769480 | tf_op jit(solution)/shard_map/ppermute | solution.py:338
  44.2 0.3 collective-permute-done.1.refs_8_
  44.4 0.0 copy-start.8
  44.4 0.1 collective-permute-start.6
  44.5 10.2 %collective-permute-done.2.refs_9_ = bf16[2,2,1,32,384]{4,3,2,1,0:T(8,128)(2,1)S(1)} collective-permute-done((bf16[2,2,1,32,384]{4,3,2,1,0:T(8,128)(2,1)S(1)}, bf16[2,2,1,32,384]{4,3,2,1,0:T(8,128)(2,1)S(1)}, u32[]{:S(2)}, u32[]{:S(2)}) %collective-permute-start.2) | collective-permute-done | bytes 98336 | tf_op jit(solution)/shard_map/ppermute | solution.py:506
  54.8 0.0 copy-done.8
  54.8 0.0 copy-start.9
  54.8 0.6 copy-done.9
  55.4 0.0 collective-permute-done.3.refs_10_
  55.4 0.0 all-to-all-done.refs_2_
  55.4 0.0 copy-done.2
  55.4 0.0 copy-done.3
  55.4 7.8 %shard_map.85 = bf16[8,4,32,128]{3,2,1,0:T(8,128)(2,1)} custom-call(bf16[4,2,1,32,384]{4,3,2,1,0:T(8,128)(2,1)} %copy-done.2, bf16[4,2,1,32,384]{4,3,2,1,0:T(8,128)(2,1)} %copy-done.3, bf16[8,8,32,384]{3,2,1,0:T(8,128)(2,1)} %all-to-all-done.refs_2_, f32[112,384]{1,0:T(8,128)} %constant.4.clone.refs_3_, bf16[384,512]{1,0:T(8,128)(2,1)} %constant.5.clone.refs_4_, ...), custom_call_target="tpu_custom_call" | custom-call | tf_op jit(solution)/shard_map/pallas_call | solution.py:436
  63.2 4.8 %all-to-all-start.1 = ((bf16[32,32,128]{2,1,0:T(8,128)(2,1)}), bf16[32,32,128]{2,1,0:T(8,128)(2,1)S(1)}, u32[]{:S(2)}, u32[]{:S(2)}) async-start(bf16[32,32,128]{2,1,0:T(8,128)(2,1)} %bitcast.3), calls=%async_computation.1 | async-start | bytes 524288 | tf_op jit(solution)/shard_map/all_to_all | solution.py:494
  68.0 0.0 collective-permute-done.4.refs_0_
  68.0 0.0 collective-permute-done.5.refs_1_
  68.0 3.0 %collective-permute-done.6.refs_2_ = bf16[256,1152]{1,0:T(8,128)(2,1)} collective-permute-done((bf16[256,1152]{1,0:T(8,128)(2,1)}, bf16[256,1152]{1,0:T(8,128)(2,1)}, u32[]{:S(2)}, u32[]{:S(2)}) %collective-permute-start.6) | collective-permute-done | bytes 589856 | tf_op jit(solution)/shard_map/ppermute | solution.py:338
  71.0 7.6 %all-to-all-done.1 = bf16[32,32,128]{2,1,0:T(8,128)(2,1)S(1)} async-done(((bf16[32,32,128]{2,1,0:T(8,128)(2,1)}), bf16[32,32,128]{2,1,0:T(8,128)(2,1)S(1)}, u32[]{:S(2)}, u32[]{:S(2)}) %all-to-all-start.1) | async-done | bytes 262176 | tf_op jit(solution)/shard_map/all_to_all | solution.py:494
  78.6 2.8 %shard_map.87 = bf16[96,1024]{1,0:T(8,128)(2,1)} custom-call(bf16[8,4,32,128]{3,2,1,0:T(8,128)(2,1)S(1)} %bitcast.2, bf16[256,128]{1,0:T(8,128)(2,1)S(1)} %get-tuple-element.24.own_ref, bf16[256,1024]{1,0:T(8,128)(2,1)S(1)} %copy-done, bf16[256,1152]{1,0:T(8,128)(2,1)} %collective-permute-done.4.refs_0_, bf16[256,1152]{1,0:T(8,128)(2,1)} %collective-permute-done.5.refs_1_, ...), custom_call_target="tpu_custom_call" | custom-call | tf_op jit(solution)/shard_map/pallas_call | solution.py:484
  (1 shorter events, 0.0 us)
Async XLA Ops:
  2.9 7.5 %copy-start.7 = (bf16[96,1024]{1,0:T(8,128)(2,1)S(1)}, bf16[96,1024]{1,0:T(8,128)(2,1)}, u32[]{:S(2)}) copy-start(bf16[96,1024]{1,0:T(8,128)(2,1)} %param.8) | copy-start | bytes 589828
  2.9 16.1 %copy-start.1 = (bf16[3,1024,256]{2,1,0:T(8,128)(2,1)S(1)}, bf16[3,1024,256]{2,1,0:T(8,128)(2,1)}, u32[]{:S(2)}) copy-start(bf16[3,1024,256]{2,1,0:T(8,128)(2,1)} %weight_ref.3) | copy-start | bytes 4718596
  2.9 16.1 %copy-start.4 = (f32[3,3,256]{2,1,0:T(4,128)S(1)}, f32[3,3,256]{2,1,0:T(4,128)}, u32[]{:S(2)}) copy-start(f32[3,3,256]{2,1,0:T(4,128)} %refs_5_.1) | copy-start | bytes 27652
  3.0 16.0 %copy-start.6 = (f32[2,256]{1,0:T(2,128)S(1)}, f32[2,256]{1,0:T(2,128)}, u32[]{:S(2)}) copy-start(f32[2,256]{1,0:T(2,128)} %refs_6_.1) | copy-start | bytes 6148
  3.0 52.4 %all-to-all-start = ((bf16[8,8,32,384]{3,2,1,0:T(8,128)(2,1)}), bf16[8,8,32,384]{3,2,1,0:T(8,128)(2,1)}, u32[]{:S(2)}, u32[]{:S(2)}) async-start(bf16[8,8,32,384]{3,2,1,0:T(8,128)(2,1)} %shard_map.83), calls=%async_computation | async-start | bytes 3145728 | tf_op jit(solution)/shard_map/all_to_all | solution.py:494
  19.0 22.3 %copy-start = (bf16[256,1024]{1,0:T(8,128)(2,1)S(1)}, bf16[256,1024]{1,0:T(8,128)(2,1)}, u32[]{:S(2)}) copy-start(bf16[256,1024]{1,0:T(8,128)(2,1)} %weight_ref.5) | copy-start | bytes 1572868
  21.3 21.4 %copy-start.5 = (bf16[32,128]{1,0:T(8,128)(2,1)}, bf16[32,128]{1,0:T(8,128)(2,1)S(1)}, u32[]{:S(2)}) copy-start(bf16[32,128]{1,0:T(8,128)(2,1)S(1)} %get-tuple-element.20.refs_7_) | copy-start | bytes 24580
  21.3 34.1 %copy-start.2 = (bf16[4,2,1,32,384]{4,3,2,1,0:T(8,128)(2,1)}, bf16[4,2,1,32,384]{4,3,2,1,0:T(8,128)(2,1)S(1)}, u32[]{:S(2)}) copy-start(bf16[4,2,1,32,384]{4,3,2,1,0:T(8,128)(2,1)S(1)} %get-tuple-element.18.mine_ref.refs_0_) | copy-start | bytes 589828
  21.3 10.8 %collective-permute-start = (bf16[4,2,1,32,384]{4,3,2,1,0:T(8,128)(2,1)S(1)}, bf16[4,2,1,32,384]{4,3,2,1,0:T(8,128)(2,1)S(1)}, u32[]{:S(2)}, u32[]{:S(2)}) collective-permute-start(bf16[4,2,1,32,384]{4,3,2,1,0:T(8,128)(2,1)S(1)} %get-tuple-element.19), channel_id=1, source_target_pairs={{0,4},{4,0},{8,12},{12,8},{16,20},{20,16},{24,28},{28,24},{1,5},{5... | collective-permute-start | bytes 589832 | tf_op jit(solution)/shard_map/ppermute | solution.py:503
  32.0 23.4 %copy-start.3 = (bf16[4,2,1,32,384]{4,3,2,1,0:T(8,128)(2,1)}, bf16[4,2,1,32,384]{4,3,2,1,0:T(8,128)(2,1)S(1)}, u32[]{:S(2)}) copy-start(bf16[4,2,1,32,384]{4,3,2,1,0:T(8,128)(2,1)S(1)} %collective-permute-done.came_ref.refs_1_) | copy-start | bytes 589828
  32.1 12.4 %collective-permute-start.1 = (bf16[2,2,1,32,384]{4,3,2,1,0:T(8,128)(2,1)S(1)}, bf16[2,2,1,32,384]{4,3,2,1,0:T(8,128)(2,1)S(1)}, u32[]{:S(2)}, u32[]{:S(2)}) collective-permute-start(bf16[2,2,1,32,384]{4,3,2,1,0:T(8,128)(2,1)S(1)} %get-tuple-element.21), channel_id=1, source_target_pairs={{0,8},{4,12},{8,16},{12,20},{16,24},{20,28},{24,0},{28,4},{1,9},{5... | collective-permute-start | bytes 294920 | tf_op jit(solution)/shard_map/ppermute | solution.py:506
  32.5 22.2 %collective-permute-start.2 = (bf16[2,2,1,32,384]{4,3,2,1,0:T(8,128)(2,1)S(1)}, bf16[2,2,1,32,384]{4,3,2,1,0:T(8,128)(2,1)S(1)}, u32[]{:S(2)}, u32[]{:S(2)}) collective-permute-start(bf16[2,2,1,32,384]{4,3,2,1,0:T(8,128)(2,1)S(1)} %get-tuple-element.22), channel_id=1, source_target_pairs={{0,16},{4,20},{8,24},{12,28},{16,0},{20,4},{24,8},{28,12},{1,17},{... | collective-permute-start | bytes 294920 | tf_op jit(solution)/shard_map/ppermute | solution.py:506
  41.3 14.1 %collective-permute-start.3 = (bf16[2,2,1,32,384]{4,3,2,1,0:T(8,128)(2,1)S(1)}, bf16[2,2,1,32,384]{4,3,2,1,0:T(8,128)(2,1)}, u32[]{:S(2)}, u32[]{:S(2)}) collective-permute-start(bf16[2,2,1,32,384]{4,3,2,1,0:T(8,128)(2,1)S(1)} %get-tuple-element.23), channel_id=1, source_target_pairs={{0,24},{4,28},{8,0},{12,4},{16,8},{20,12},{24,16},{28,20},{1,25},{... | collective-permute-start | bytes 294920 | tf_op jit(solution)/shard_map/ppermute | solution.py:506
  42.7 25.3 %collective-permute-start.4 = (bf16[256,1152]{1,0:T(8,128)(2,1)}, bf16[256,1152]{1,0:T(8,128)(2,1)}, u32[]{:S(2)}, u32[]{:S(2)}) collective-permute-start(bf16[256,1152]{1,0:T(8,128)(2,1)} %get-tuple-element.28), channel_id=1, source_target_pairs={{0,1},{1,0},{2,3},{3,2},{4,5},{5,4},{6,7},{7,6},{8,9},{9,8},{10,11... | collective-permute-start | bytes 1769480 | tf_op jit(solution)/shard_map/ppermute | solution.py:338
  42.7 25.3 %collective-permute-start.5 = (bf16[256,1152]{1,0:T(8,128)(2,1)}, bf16[256,1152]{1,0:T(8,128)(2,1)}, u32[]{:S(2)}, u32[]{:S(2)}) collective-permute-start(bf16[256,1152]{1,0:T(8,128)(2,1)} %get-tuple-element.29), channel_id=1, source_target_pairs={{0,2},{1,3},{2,0},{3,1},{4,6},{5,7},{6,4},{7,5},{8,10},{9,11},{10,... | collective-permute-start | bytes 1769480 | tf_op jit(solution)/shard_map/ppermute | solution.py:338
  44.4 10.3 %copy-start.8 = (bf16[2,2,1,32,384]{4,3,2,1,0:T(8,128)(2,1)}, bf16[2,2,1,32,384]{4,3,2,1,0:T(8,128)(2,1)S(1)}, u32[]{:S(2)}) copy-start(bf16[2,2,1,32,384]{4,3,2,1,0:T(8,128)(2,1)S(1)} %collective-permute-done.1.refs_8_) | copy-start | bytes 294916
  44.4 26.6 %collective-permute-start.6 = (bf16[256,1152]{1,0:T(8,128)(2,1)}, bf16[256,1152]{1,0:T(8,128)(2,1)}, u32[]{:S(2)}, u32[]{:S(2)}) collective-permute-start(bf16[256,1152]{1,0:T(8,128)(2,1)} %get-tuple-element.30), channel_id=1, source_target_pairs={{0,3},{1,2},{2,1},{3,0},{4,7},{5,6},{6,5},{7,4},{8,11},{9,10},{10,... | collective-permute-start | bytes 1769480 | tf_op jit(solution)/shard_map/ppermute | solution.py:338
  54.8 0.6 copy-start.9
  63.2 15.4 %all-to-all-start.1 = ((bf16[32,32,128]{2,1,0:T(8,128)(2,1)}), bf16[32,32,128]{2,1,0:T(8,128)(2,1)S(1)}, u32[]{:S(2)}, u32[]{:S(2)}) async-start(bf16[32,32,128]{2,1,0:T(8,128)(2,1)} %bitcast.3), calls=%async_computation.1 | async-start | bytes 524288 | tf_op jit(solution)/shard_map/all_to_all | solution.py:494

commit v3 on v2

--- a/solution.py
+++ b/solution.py
@@ -13,32 +13,19 @@
 ANY = pl.BlockSpec(memory_space=pl.ANY)
 MOST = 63 * 1024 * 1024
 LANES = 128
-INNER = 16
+HALF_ROOT = math.sqrt(0.75)
 LIMIT = 20 * 1024 * 1024
 
 
-def phase_rows(blocks, length):
-    line = np.arange(length)
-    angles = [
-        2.0 * np.pi / (blocks * length) * np.outer(np.arange(blocks), line),
-        2.0 * np.pi / length * (np.outer(INNER * np.arange(length // INNER), line) % length),
-        2.0 * np.pi / length * (np.outer(np.arange(INNER), line) % length),
-    ]
-    return jnp.asarray(np.concatenate([part for a in angles for part in (np.cos(a), -np.sin(a))]), jnp.float32)
-
-
-def build_table(phases_ref, top, table_ref):
-    length = phases_ref.shape[1]
-    outer = length // INNER
-    cos_j, sin_j = phases_ref[top + 2 * outer : top + 2 * outer + INNER], phases_ref[top + 2 * outer + INNER :]
-    for i in range(outer):
-        cos_i, sin_i = phases_ref[top + i : top + i + 1], phases_ref[top + outer + i : top + outer + i + 1]
-        cos = (cos_i * cos_j - sin_i * sin_j).astype(jnp.bfloat16)
-        sin = (cos_i * sin_j + sin_i * cos_j).astype(jnp.bfloat16)
-        table_ref[i * INNER : (i + 1) * INNER, :length] = cos
-        table_ref[i * INNER : (i + 1) * INNER, length:] = sin
-        table_ref[length + i * INNER : length + (i + 1) * INNER, :length] = -sin
-        table_ref[length + i * INNER : length + (i + 1) * INNER, length:] = cos
+def lanes_table():
+    angles = 2.0 * np.pi / LANES * (np.outer(np.arange(LANES), np.arange(LANES)) % LANES)
+    cos, sin = np.cos(angles), np.sin(angles)
+    return jnp.asarray(np.block([[cos, -sin], [sin, cos]]), jnp.bfloat16)
+
+
+def twist_rows(bins):
+    angles = 2.0 * np.pi / (bins * LANES) * np.outer(np.arange(bins), np.arange(LANES))
+    return jnp.asarray(np.concatenate([np.cos(angles), -np.sin(angles)]), jnp.float32)
 
 
 def window_width(share, count):
@@ -61,6 +48,14 @@
 def forward_half(values):
     if len(values) == 1:
         return [(values[0], None), (values[0], None)]
+    if len(values) == 3:
+        both, gap = values[1] + values[2], values[1] - values[2]
+        return [
+            (values[0] + both, None),
+            (values[0] + 0.5 * gap, -HALF_ROOT * both),
+            (values[0] - 0.5 * both, -HALF_ROOT * gap),
+            (values[0] - gap, None),
+        ]
     even, odd = forward_half(values[0::2]), forward_half(values[1::2])
     half = len(values)
     quarter = half // 2
@@ -79,6 +74,14 @@
     half = len(bins) - 1
     if half == 1:
         return [bins[0][0] + bins[1][0]]
+    if half == 3:
+        (zero, _), (re, im), (re_two, im_two), (three, _) = bins
+        both, gap = zero + three, zero - three
+        return [
+            both + 2.0 * (re + re_two),
+            gap + (re - re_two) - 2.0 * HALF_ROOT * (im + im_two),
+            both - (re + re_two) - 2.0 * HALF_ROOT * (im - im_two),
+        ]
     quarter = half // 2
     even = [(bins[0][0] + bins[half][0], None)]
     odd = [(bins[0][0] - bins[half][0], None)]
@@ -97,18 +100,23 @@
 def spectra_kernel(spectra_ref, out_ref, arriving, leaving, sems_in, sems_out):
     orders, parts, residues = spectra_ref.shape[:3]
     count, slabs, each, length = out_ref.shape
+    steps, groups = length // LANES, arriving.shape[1]
     fetches, stores = [], []
     for i in range(slabs):
         order, part, residue = i // (parts * residues), i // residues % parts, i % residues
-        fetches.append(
-            pltpu.make_async_copy(spectra_ref.at[order, part, residue], arriving.at[i], sems_in.at[i])
-        )
+        for group in range(groups):
+            source = spectra_ref.at[order, part, residue, :, pl.ds(group * LANES, LANES)]
+            fetches.append(pltpu.make_async_copy(source, arriving.at[i, group], sems_in.at[i, group]))
         stores.append(pltpu.make_async_copy(leaving.at[i], out_ref.at[:, i], sems_out.at[i]))
     for fetch in fetches:
         fetch.start()
-    for i, (fetch, store) in enumerate(zip(fetches, stores)):
-        fetch.wait()
-        leaving[i] = arriving[i].T.reshape(count, each, length).astype(jnp.bfloat16)
+    some = count // groups
+    for i, store in enumerate(stores):
+        runs = []
+        for group in range(groups):
+            fetches[i * groups + group].wait()
+            runs.append(jnp.concatenate([arriving[i, group, pl.ds(start, LANES, stride=steps), :] for start in range(steps)], axis=0))
+        leaving[i] = jnp.concatenate(runs, axis=1).astype(jnp.bfloat16).T.reshape(count, each, length)
         store.start()
     for store in stores:
         store.wait()
@@ -124,9 +132,9 @@
         out_specs=ANY,
         out_shape=jax.ShapeDtypeStruct((count, slabs, each, length), jnp.bfloat16),
         scratch_shapes=[
-            pltpu.VMEM((slabs, length, channels), jnp.float32),
+            pltpu.VMEM((slabs, channels // LANES, length, LANES), jnp.float32),
             pltpu.VMEM((slabs, count, each, length), jnp.bfloat16),
-            pltpu.SemaphoreType.DMA((slabs,)),
+            pltpu.SemaphoreType.DMA((slabs, channels // LANES)),
             pltpu.SemaphoreType.DMA((slabs,)),
         ],
         compiler_params=pltpu.CompilerParams(vmem_limit_bytes=MOST),
@@ -269,69 +277,55 @@
     )(mine, came)
 
 
-def tiles_of(each, length):
-    chunk, width = min(16, each), 128
-    return [(slice(r, r + chunk), slice(c, c + width)) for r in range(0, each, chunk) for c in range(0, length, width)]
-
-
-def part_of(cols, length, part):
-    return slice(part * length + cols.start, part * length + cols.stop)
-
-
-def twist_of(phases_ref, k, blocks, cols):
-    return phases_ref[k : k + 1, cols], phases_ref[blocks + k : blocks + k + 1, cols]
-
-
-def forward_tile(values, tile, lines, phases_ref, each, length):
-    rows, cols = tile
-    blocks = 2 * len(values)
+def forward_tile(values, rows, lines, twist_ref, each):
+    count = 2 * len(values)
     bins = forward_half(values)
-    for k in range(blocks):
-        cos, sin = twist_of(phases_ref, k, blocks, cols)
-        re, im = bins[min(k, blocks - k)]
+    for k in range(count):
+        cos, sin = twist_ref[k : k + 1], twist_ref[count + k : count + k + 1]
+        re, im = bins[min(k, count - k)]
         if im is None:
             pair = (re * cos, re * sin)
-        elif 2 * k < blocks:
+        elif 2 * k < count:
             pair = (re * cos - im * sin, re * sin + im * cos)
         else:
             pair = (re * cos + im * sin, re * sin - im * cos)
         at = slice(k * each + rows.start, k * each + rows.stop)
         for part in range(2):
-            lines[at, part_of(cols, length, part)] = pair[part].astype(jnp.bfloat16)
-
-
-def respond(spectrum, start, order, spectra_ref, lines, each, length):
+            lines[at, part * LANES : (part + 1) * LANES] = pair[part].astype(jnp.bfloat16)
+
+
+def respond(spectrum, start, order, spectra_ref, lines, each, blocks):
     residues = spectra_ref.shape[1] // 4
     for k in range(start // each, (start + spectrum.shape[0]) // each):
         at = k * each - start
-        re, im = spectrum[at : at + each, :length], spectrum[at : at + each, length:]
-        first = order * 2 * residues + k % residues
-        gain_re = spectra_ref[k // residues, first].astype(jnp.float32)
-        gain_im = spectra_ref[k // residues, first + residues].astype(jnp.float32)
-        lines[k * each : (k + 1) * each, :length] = (re * gain_re - im * gain_im).astype(jnp.bfloat16)
-        lines[k * each : (k + 1) * each, length:] = (-(re * gain_im) - im * gain_re).astype(jnp.bfloat16)
-
-
-def inverse_tile(wave, tile, phases_ref, positions, each, length):
-    rows, cols = tile
-    blocks = 2 * positions
+        re, im = spectrum[at : at + each, :LANES], spectrum[at : at + each, LANES:]
+        block, cols = k % blocks, slice(k // blocks * LANES, (k // blocks + 1) * LANES)
+        first = order * 2 * residues + block % residues
+        gain_re = spectra_ref[block // residues, first, :, cols].astype(jnp.float32)
+        gain_im = spectra_ref[block // residues, first + residues, :, cols].astype(jnp.float32)
+        lines[k * each : (k + 1) * each, :LANES] = (re * gain_re - im * gain_im).astype(jnp.bfloat16)
+        lines[k * each : (k + 1) * each, LANES:] = (-(re * gain_im) - im * gain_re).astype(jnp.bfloat16)
+
+
+def inverse_tile(wave, rows, twist_ref, half, each):
+    count = 2 * half
     turned = []
-    for k in range(blocks):
-        cos, sin = twist_of(phases_ref, k, blocks, cols)
+    for k in range(count):
+        cos, sin = twist_ref[k : k + 1], twist_ref[count + k : count + k + 1]
         at = slice(k * each + rows.start, k * each + rows.stop)
-        re, im = wave[at, cols], wave[at, part_of(cols, length, 1)]
+        re, im = wave[at, :LANES], wave[at, LANES:]
         turned.append((re * cos - im * sin, re * sin + im * cos))
     bins = [(turned[0][0] * 2.0, None)]
-    for k in range(1, positions):
-        one, two = turned[k], turned[blocks - k]
+    for k in range(1, half):
+        one, two = turned[k], turned[count - k]
         bins.append((one[0] + two[0], two[1] - one[1]))
-    bins.append((turned[positions][0] * 2.0, None))
-    return [value * (0.5 / (blocks * length)) for value in inverse_half(bins)]
-
-
-def row_steps(blocks, each):
-    step = max(each, min(blocks * each, 128))
-    return [slice(start, start + step) for start in range(0, blocks * each, step)]
+    bins.append((turned[half][0] * 2.0, None))
+    return [value * (0.5 / (count * LANES)) for value in inverse_half(bins)]
+
+
+def row_steps(total, most):
+    step = math.gcd(total, most)
+    return [slice(start, start + step) for start in range(0, total, step)]
 
 
 def flipped(array, flip, size):
@@ -339,12 +333,13 @@
 
 
 def convolve_kernel(*refs):
-    mine_in, came_in, spectra_in, phases_in, shares_in, taps_ref, skip_ref, edge_ref = refs[:8]
-    shifted, refs = refs[8:-14], refs[-14:]
-    out_ref, held, spectra_ref, phases_ref, shares_ref, table_ref, filtered, lines, wave = refs[:9]
+    mine_in, came_in, spectra_in, twist_in, table_in, shares_in, taps_ref, skip_ref, edge_ref = refs[:9]
+    shifted, refs = refs[9:-14], refs[-14:]
+    out_ref, held, spectra_ref, twist_ref, table_ref, shares_ref, filtered, lines, wave = refs[:9]
     gathered, columns, leaving, sems, some = refs[9:]
     branches, positions, each, length = filtered.shape
     blocks = 2 * positions
+    runs = length // LANES
     count = held.shape[0]
     pieces = positions // count
     slabs = spectra_ref.shape[1]
@@ -360,23 +355,22 @@
             source = lax.rem(one + count - 2 * shift, count)
             inward.append(pltpu.make_async_copy(ref.at[i], held.at[source], some.at[2 * shift + i]))
     halves = [slice(0, slabs // 2), slice(slabs // 2, slabs)]
-    phases = pltpu.make_async_copy(phases_in, phases_ref, sems.at[0])
+    twist = pltpu.make_async_copy(twist_in, twist_ref, sems.at[0])
+    table = pltpu.make_async_copy(table_in, table_ref, sems.at[5])
     spectra = [
         pltpu.make_async_copy(spectra_in.at[:, half], spectra_ref.at[:, half], sems.at[1 + i])
         for i, half in enumerate(halves)
     ]
     shares = pltpu.make_async_copy(shares_in, shares_ref, sems.at[3])
-    for copy in [phases] + inward:
+    for copy in inward + [twist]:
         copy.start()
     columns[...] = tap_columns(taps_ref, skip_ref, gathered)
     mine = columns[pl.ds(pl.multiple_of(me * each, each), each), :]
     lane = lax.broadcasted_iota(jnp.int32, (each, length), 1)
-    phases.wait()
     for copy in inward:
         copy.wait()
-    for copy in spectra + [shares]:
+    for copy in [table] + spectra + [shares]:
         copy.start()
-    build_table(phases_ref, 2 * blocks, table_ref)
     for branch in range(branches):
         last = [jnp.zeros((each, length), jnp.float32)] * 2
         scale = [jnp.broadcast_to(mine[:, branch * 3 + i : branch * 3 + i + 1], (each, length)) for i in range(3)]
@@ -387,26 +381,31 @@
 
     def through(order):
         spectra[order].wait()
-        for rows in row_steps(blocks, each):
+        for rows in row_steps(runs * blocks * each, 512):
             spectrum = jnp.dot(lines[rows], table_ref[...], preferred_element_type=jnp.float32)
-            respond(spectrum, rows.start, order, spectra_ref, lines, each, length)
-        for rows in row_steps(blocks, each):
+            respond(spectrum, rows.start, order, spectra_ref, lines, each, blocks)
+        for rows in row_steps(runs * blocks * each, 512):
             wave[rows] = jnp.dot(lines[rows], table_ref[...], preferred_element_type=jnp.float32)
 
-    tiles = tiles_of(each, length)
-    for tile in tiles:
-        forward_tile([filtered[(0, p) + tile] for p in range(positions)], tile, lines, phases_ref, each, length)
+    chunk = min(16, each)
+    tiles = [slice(row, row + chunk) for row in range(0, each, chunk)]
+    places = [(p, slice(run * LANES, (run + 1) * LANES)) for p in range(positions) for run in range(runs)]
+    twist.wait()
+    for rows in tiles:
+        forward_tile([filtered[0, p, rows, cols] for p, cols in places], rows, lines, twist_ref, each)
+    table.wait()
     through(0)
-    for tile in tiles:
-        values = inverse_tile(wave, tile, phases_ref, positions, each, length)
-        for p, value in enumerate(values):
-            values[p] = filtered[(1, p) + tile] * (value + skips[0][tile[0]] * filtered[(0, p) + tile])
-            filtered[(0, p) + tile] = values[p]
-        forward_tile(values, tile, lines, phases_ref, each, length)
+    for rows in tiles:
+        values = inverse_tile(wave, rows, twist_ref, len(places), each)
+        for i, (p, cols) in enumerate(places):
+            values[i] = filtered[1, p, rows, cols] * (values[i] + skips[0][rows] * filtered[0, p, rows, cols])
+            filtered[0, p, rows, cols] = values[i]
+        forward_tile(values, rows, lines, twist_ref, each)
     through(1)
-    for tile in tiles:
-        for p, value in enumerate(inverse_tile(wave, tile, phases_ref, positions, each, length)):
-            filtered[(0, p) + tile] = value + skips[1][tile[0]] * filtered[(0, p) + tile]
+    for rows in tiles:
+        values = inverse_tile(wave, rows, twist_ref, len(places), each)
+        for value, (p, cols) in zip(values, places):
+            filtered[0, p, rows, cols] = value + skips[1][rows] * filtered[0, p, rows, cols]
     shares.wait()
     wide = out_ref.shape[3]
     parts = shares_ref.shape[1] // wide
@@ -429,32 +428,32 @@
     positions = count * pieces
     blocks = 2 * positions
     channels = taps.shape[2]
-    phases = phase_rows(blocks, length)
+    twist, table = twist_rows(length // LANES * blocks), lanes_table()
     share = pieces * length // across
     wide = window_width(share, count)
     shares = share_table(length, share, wide)
     return pl.pallas_call(
         convolve_kernel,
-        in_specs=[ANY] * 5 + [VMEM] * 3 + [ANY] * len(shifted),
+        in_specs=[ANY] * 6 + [VMEM] * 3 + [ANY] * len(shifted),
         out_specs=ANY,
         out_shape=jax.ShapeDtypeStruct((count, across, each, wide), jnp.bfloat16),
         scratch_shapes=[
             pltpu.VMEM((count, branches, pieces, each, length), jnp.bfloat16),
             pltpu.VMEM(spectra.shape, spectra.dtype),
-            pltpu.VMEM(phases.shape, phases.dtype),
+            pltpu.VMEM(twist.shape, twist.dtype),
+            pltpu.VMEM(table.shape, table.dtype),
             pltpu.VMEM(shares.shape, shares.dtype),
-            pltpu.VMEM((2 * length, 2 * length), jnp.bfloat16),
             pltpu.VMEM((branches, positions, each, length), jnp.float32),
-            pltpu.VMEM((blocks * each, 2 * length), jnp.bfloat16),
-            pltpu.VMEM((blocks * each, 2 * length), jnp.float32),
+            pltpu.VMEM((length // LANES * blocks * each, 2 * LANES), jnp.bfloat16),
+            pltpu.VMEM((length // LANES * blocks * each, 2 * LANES), jnp.float32),
             pltpu.VMEM((16, channels), jnp.float32),
             pltpu.VMEM((channels, 16), jnp.float32),
             pltpu.VMEM((count, across, each, wide), jnp.bfloat16),
-            pltpu.SemaphoreType.DMA((5,)),
+            pltpu.SemaphoreType.DMA((6,)),
             pltpu.SemaphoreType.DMA((count,)),
         ],
-        compiler_params=pltpu.CompilerParams(vmem_limit_bytes=MOST),
-    )(mine, came, spectra, phases, shares, taps, skip, edge, *shifted)
+        compiler_params=pltpu.CompilerParams(vmem_limit_bytes=56 * 1024 * 1024),
+    )(mine, came, spectra, twist, table, shares, taps, skip, edge, *shifted)
 
 
 def finish_kernel(share, carried_ref, own_ref, weight_ref, *refs):

time: 81.8 us -> 79.1 us (0.967)
  Pallas kernels: 17.2 us -> 14.2 us
    ppermute x3, waiting for transfers between devices: 3 us -> 4.9 us  [flipped(): return lax.ppermute(array, 'tp', [(i, i ^ flip) for i in range(size)])]
    all_to_all x2, waiting for transfers between devices: 7.58 us -> 5.68 us  [spread(): return lax.all_to_all(array, axes, split_axis=0, concat_axis=0, tiled=True)]
    pallas_call x1, Pallas kernels: 2.84 us -> 1.42 us  [finish(): pl.pallas_call(functools.partial(finish_kernel, share), in_specs=[VMEM] *...]
    pallas_call x1, Pallas kernels: 7.77 us -> 6.51 us  [convolve(): pl.pallas_call(convolve_kernel, in_specs=[ANY] * 6 + [VMEM] * 3 + [ANY] *...]
  transfers between devices with their start and end apart: 9 -> 9, of which waited for: 5 -> 5; matrix products, arithmetic and copies ran while one was open for 0% -> 0% of each run, Pallas kernels for 14% -> 13%
where the time goes in v3:
time: 79.1 us; the launch traced here: 78.7 us
  waiting for transfers between devices  30.1 us (38%)
  starting transfers between devices  25 us (32%)
  Pallas kernels  14.2 us (18%)
  blocking collectives  8.6 us (11%)
    all_to_all x2, starting transfers between devices, spread(): return lax.all_to_all(array, axes, split_axis=0, concat_axis=0, tiled=True)  12.2 us
    ppermute x3, waiting for transfers between devices, local(): lax.ppermute(array, 'seq', [(i, (i + 2 * shift) % count) for i in range(c...  10.8 us
    ppermute x3, starting transfers between devices, local(): lax.ppermute(array, 'seq', [(i, (i + 2 * shift) % count) for i in range(c...  9.22 us
    ppermute x1, waiting for transfers between devices, local(): came = lax.ppermute(other, 'seq', [(i, i ^ 1) for i in range(count)])  8.67 us
    all_gather x1, blocking collectives, local(): gathered = lax.all_gather(tokens, 'tp', axis=0, tiled=True)  8.6 us
    pallas_call x1, Pallas kernels, convolve(): pl.pallas_call(convolve_kernel, in_specs=[ANY] * 6 + [VMEM] * 3 + [ANY] *...  6.51 us
    all_to_all x2, waiting for transfers between devices, spread(): return lax.all_to_all(array, axes, split_axis=0, concat_axis=0, tiled=True)  5.68 us
    ppermute x3, waiting for transfers between devices, flipped(): return lax.ppermute(array, 'tp', [(i, i ^ flip) for i in range(size)])  4.9 us
  transfers between devices with their start and end apart: 9, of which 5 were waited for; matrix products, arithmetic and copies ran while one was open for 0% of the time, Pallas kernels for 13%

profile of v3, /device:TPU:0, one launch (start us, length us, event | category | flops | bytes accessed | tf_op | source)
XLA Modules:
  0.0 78.7 jit_solution(414504854323672619)
XLA Ops:
  0.0 2.9 %shard_map.92 = bf16[8,8,32,384]{3,2,1,0:T(8,128)(2,1)} custom-call(f32[2,2,2,384,256]{4,3,2,1,0:T(8,128)} %spectra_ref.1), custom_call_target="tpu_custom_call" | custom-call | tf_op jit(solution)/shard_map/pallas_call | solution.py:129
  2.9 0.0 copy-start.7
  2.9 0.0 copy-start.1
  2.9 0.0 copy-start.4
  3.0 0.0 copy-start.6
  3.0 7.4 %all-to-all-start = ((bf16[8,8,32,384]{3,2,1,0:T(8,128)(2,1)}), bf16[8,8,32,384]{3,2,1,0:T(8,128)(2,1)}, u32[]{:S(2)}, u32[]{:S(2)}) async-start(bf16[8,8,32,384]{3,2,1,0:T(8,128)(2,1)} %shard_map.92), calls=%async_computation | async-start | bytes 3145728 | tf_op jit(solution)/shard_map/all_to_all | solution.py:493
  10.4 0.0 copy-done.7
  10.4 8.6 %all_gather.3.tokens_ref = bf16[384,1024]{1,0:T(8,128)(2,1)S(1)} all-gather(bf16[96,1024]{1,0:T(8,128)(2,1)S(1)} %copy-done.7), channel_id=1, replica_groups=mesh['seq'=8,'tp'=4] {'tp'}, dimensions={0}, use_global_device_ids=true | all-gather | bytes 983040 | tf_op jit(solution)/shard_map/all_gather | solution.py:500
  19.0 0.0 copy-done.1
  19.0 0.0 copy-done.4
  19.0 0.0 copy-done.6
  19.0 0.0 copy-start
  19.0 2.3 %shard_map.91 = (bf16[4,2,1,32,384]{4,3,2,1,0:T(8,128)(2,1)S(1)}, bf16[4,2,1,32,384]{4,3,2,1,0:T(8,128)(2,1)S(1)}, bf16[32,128]{1,0:T(8,128)(2,1)S(1)}, bf16[256...) custom-call(bf16[384,1024]{1,0:T(8,128)(2,1)S(1)} %all_gather.3.toke, ...), custom_call_target="tpu_custom_call" | custom-call | tf_op jit(solution)/shard_map/pallas_call | solution.py:213
  21.3 0.0 copy-start.5
  21.3 0.0 copy-start.2
  21.3 2.1 %collective-permute-start = (bf16[4,2,1,32,384]{4,3,2,1,0:T(8,128)(2,1)S(1)}, bf16[4,2,1,32,384]{4,3,2,1,0:T(8,128)(2,1)S(1)}, u32[]{:S(2)}, u32[]{:S(2)}) collective-permute-start(bf16[4,2,1,32,384]{4,3,2,1,0:T(8,128)(2,1)S(1)} %get-tuple-element.19), channel_id=1, source_target_pairs={{0,4},{4,0},{8,12},{12,8},{16,20},{20,16},{24,28},{28,24},{1,5},{5... | collective-permute-start | bytes 589832 | tf_op jit(solution)/shard_map/ppermute | solution.py:502
  23.4 8.7 %collective-permute-done.came_ref.refs_1_ = bf16[4,2,1,32,384]{4,3,2,1,0:T(8,128)(2,1)S(1)} collective-permute-done((bf16[4,2,1,32,384]{4,3,2,1,0:T(8,128)(2,1)S(1)}, bf16[4,2,1,32,384]{4,3,2,1,0:T(8,128)(2,1)S(1)}, u32[]{:S(2)}, u32[]{:S(2)}) %collective-permute-start) | collective-permute-done | bytes 196640 | tf_op jit(solution)/shard_map/ppermute | solution.py:502
  32.1 0.0 copy-start.3
  32.1 0.5 collective-permute-start.1
  32.6 8.7 %collective-permute-start.2 = (bf16[2,2,1,32,384]{4,3,2,1,0:T(8,128)(2,1)S(1)}, bf16[2,2,1,32,384]{4,3,2,1,0:T(8,128)(2,1)S(1)}, u32[]{:S(2)}, u32[]{:S(2)}) collective-permute-start(bf16[2,2,1,32,384]{4,3,2,1,0:T(8,128)(2,1)S(1)} %get-tuple-element.22), channel_id=1, source_target_pairs={{0,16},{4,20},{8,24},{12,28},{16,0},{20,4},{24,8},{28,12},{1,17},{... | collective-permute-start | bytes 294920 | tf_op jit(solution)/shard_map/ppermute | solution.py:505
  41.3 0.0 collective-permute-start.3
  41.3 0.0 copy-done
  41.3 1.1 %shard_map.95 = (bf16[256,1152]{1,0:T(8,128)(2,1)}, bf16[256,1152]{1,0:T(8,128)(2,1)}, bf16[256,1152]{1,0:T(8,128)(2,1)S(1)}) custom-call(bf16[256,1024]{1,0:T(8,128)(2,1)S(1)} %copy-done, bf16[256,128]{1,0:T(8,128)(2,1)S(1)} %get-tuple-element.25.refs_0_, bf16[256,128]{1,0:T(8,128)(2,1)S(1)} %get-tuple-element.26.refs_1_, ...), custom_call_target="tpu_custom_call" | custom-call | tf_op jit(solution)/shard_map/pallas_call | solution.py:254
  42.4 0.0 collective-permute-start.4
  42.4 1.5 %collective-permute-start.5 = (bf16[256,1152]{1,0:T(8,128)(2,1)}, bf16[256,1152]{1,0:T(8,128)(2,1)S(1)}, u32[]{:S(2)}, u32[]{:S(2)}) collective-permute-start(bf16[256,1152]{1,0:T(8,128)(2,1)} %get-tuple-element.29), channel_id=1, source_target_pairs={{0,2},{1,3},{2,0},{3,1},{4,6},{5,7},{6,4},{7,5},{8,10},{9,11},{10,... | collective-permute-start | bytes 1769480 | tf_op jit(solution)/shard_map/ppermute | solution.py:332
  43.9 0.5 collective-permute-done.1.refs_9_
  44.4 0.0 copy-done.5
  44.4 0.0 copy-start.8
  44.4 0.0 collective-permute-start.6
  44.4 10.3 %collective-permute-done.2.refs_10_ = bf16[2,2,1,32,384]{4,3,2,1,0:T(8,128)(2,1)S(1)} collective-permute-done((bf16[2,2,1,32,384]{4,3,2,1,0:T(8,128)(2,1)S(1)}, bf16[2,2,1,32,384]{4,3,2,1,0:T(8,128)(2,1)S(1)}, u32[]{:S(2)}, u32[]{:S(2)}) %collective-permute-start.2) | collective-permute-done | bytes 98336 | tf_op jit(solution)/shard_map/ppermute | solution.py:505
  54.8 0.0 copy-start.9
  54.8 0.0 collective-permute-done.3.refs_11_
  54.8 0.0 all-to-all-done.refs_2_
  54.8 0.0 copy-done.2
  54.8 0.0 copy-done.3
  54.8 0.0 copy-done.8
  54.8 0.6 copy-done.9
  55.4 6.5 %shard_map.94 = bf16[8,4,32,128]{3,2,1,0:T(8,128)(2,1)} custom-call(bf16[4,2,1,32,384]{4,3,2,1,0:T(8,128)(2,1)} %copy-done.2, bf16[4,2,1,32,384]{4,3,2,1,0:T(8,128)(2,1)} %copy-done.3, bf16[8,8,32,384]{3,2,1,0:T(8,128)(2,1)} %all-to-all-done.refs_2_, f32[96,128]{1,0:T(8,128)} %constant.6.clone.refs_3_, bf16[256,256]{1,0:T(8,128)(2,1)} %constant.7.clone.refs_4_, ...), custom_call_target="tpu_custom_call" | custom-call | tf_op jit(solution)/shard_map/pallas_call | solution.py:435
  61.9 4.8 %all-to-all-start.1 = ((bf16[32,32,128]{2,1,0:T(8,128)(2,1)}), bf16[32,32,128]{2,1,0:T(8,128)(2,1)S(1)}, u32[]{:S(2)}, u32[]{:S(2)}) async-start(bf16[32,32,128]{2,1,0:T(8,128)(2,1)} %bitcast.3), calls=%async_computation.1 | async-start | bytes 524288 | tf_op jit(solution)/shard_map/all_to_all | solution.py:493
  66.7 0.0 collective-permute-done.4.refs_0_
  66.7 0.0 collective-permute-done.5.refs_1_
  66.7 4.9 %collective-permute-done.6.refs_2_ = bf16[256,1152]{1,0:T(8,128)(2,1)S(1)} collective-permute-done((bf16[256,1152]{1,0:T(8,128)(2,1)S(1)}, bf16[256,1152]{1,0:T(8,128)(2,1)S(1)}, u32[]{:S(2)}, u32[]{:S(2)}) %collective-permute-start.6) | collective-permute-done | bytes 589856 | tf_op jit(solution)/shard_map/ppermute | solution.py:332
  71.6 5.7 %all-to-all-done.1 = bf16[32,32,128]{2,1,0:T(8,128)(2,1)S(1)} async-done(((bf16[32,32,128]{2,1,0:T(8,128)(2,1)}), bf16[32,32,128]{2,1,0:T(8,128)(2,1)S(1)}, u32[]{:S(2)}, u32[]{:S(2)}) %all-to-all-start.1) | async-done | bytes 262176 | tf_op jit(solution)/shard_map/all_to_all | solution.py:493
  77.3 1.4 %shard_map.96 = bf16[96,1024]{1,0:T(8,128)(2,1)} custom-call(bf16[8,4,32,128]{3,2,1,0:T(8,128)(2,1)S(1)} %bitcast.2, bf16[256,128]{1,0:T(8,128)(2,1)S(1)} %get-tuple-element.24.own_ref, bf16[256,1024]{1,0:T(8,128)(2,1)S(1)} %copy-done, bf16[256,1152]{1,0:T(8,128)(2,1)S(1)} %collective-permute-done.4.refs_0_, ...), custom_call_target="tpu_custom_call" | custom-call | tf_op jit(solution)/shard_map/pallas_call | solution.py:483
  (1 shorter events, 0.0 us)
Async XLA Ops:
  2.9 7.5 %copy-start.7 = (bf16[96,1024]{1,0:T(8,128)(2,1)S(1)}, bf16[96,1024]{1,0:T(8,128)(2,1)}, u32[]{:S(2)}) copy-start(bf16[96,1024]{1,0:T(8,128)(2,1)} %param.9) | copy-start | bytes 589828
  2.9 16.1 %copy-start.1 = (bf16[3,1024,256]{2,1,0:T(8,128)(2,1)S(1)}, bf16[3,1024,256]{2,1,0:T(8,128)(2,1)}, u32[]{:S(2)}) copy-start(bf16[3,1024,256]{2,1,0:T(8,128)(2,1)} %weight_ref.3) | copy-start | bytes 4718596
  2.9 16.1 %copy-start.4 = (f32[3,3,256]{2,1,0:T(4,128)S(1)}, f32[3,3,256]{2,1,0:T(4,128)}, u32[]{:S(2)}) copy-start(f32[3,3,256]{2,1,0:T(4,128)} %refs_6_.1) | copy-start | bytes 27652
  3.0 16.0 %copy-start.6 = (f32[2,256]{1,0:T(2,128)S(1)}, f32[2,256]{1,0:T(2,128)}, u32[]{:S(2)}) copy-start(f32[2,256]{1,0:T(2,128)} %refs_7_.1) | copy-start | bytes 6148
  3.0 51.8 %all-to-all-start = ((bf16[8,8,32,384]{3,2,1,0:T(8,128)(2,1)}), bf16[8,8,32,384]{3,2,1,0:T(8,128)(2,1)}, u32[]{:S(2)}, u32[]{:S(2)}) async-start(bf16[8,8,32,384]{3,2,1,0:T(8,128)(2,1)} %shard_map.92), calls=%async_computation | async-start | bytes 3145728 | tf_op jit(solution)/shard_map/all_to_all | solution.py:493
  19.0 22.3 %copy-start = (bf16[256,1024]{1,0:T(8,128)(2,1)S(1)}, bf16[256,1024]{1,0:T(8,128)(2,1)}, u32[]{:S(2)}) copy-start(bf16[256,1024]{1,0:T(8,128)(2,1)} %weight_ref.5) | copy-start | bytes 1572868
  21.3 23.2 %copy-start.5 = (bf16[32,128]{1,0:T(8,128)(2,1)}, bf16[32,128]{1,0:T(8,128)(2,1)S(1)}, u32[]{:S(2)}) copy-start(bf16[32,128]{1,0:T(8,128)(2,1)S(1)} %get-tuple-element.20.refs_8_) | copy-start | bytes 24580
  21.3 33.5 %copy-start.2 = (bf16[4,2,1,32,384]{4,3,2,1,0:T(8,128)(2,1)}, bf16[4,2,1,32,384]{4,3,2,1,0:T(8,128)(2,1)S(1)}, u32[]{:S(2)}) copy-start(bf16[4,2,1,32,384]{4,3,2,1,0:T(8,128)(2,1)S(1)} %get-tuple-element.18.mine_ref.refs_0_) | copy-start | bytes 589828
  21.3 10.8 %collective-permute-start = (bf16[4,2,1,32,384]{4,3,2,1,0:T(8,128)(2,1)S(1)}, bf16[4,2,1,32,384]{4,3,2,1,0:T(8,128)(2,1)S(1)}, u32[]{:S(2)}, u32[]{:S(2)}) collective-permute-start(bf16[4,2,1,32,384]{4,3,2,1,0:T(8,128)(2,1)S(1)} %get-tuple-element.19), channel_id=1, source_target_pairs={{0,4},{4,0},{8,12},{12,8},{16,20},{20,16},{24,28},{28,24},{1,5},{5... | collective-permute-start | bytes 589832 | tf_op jit(solution)/shard_map/ppermute | solution.py:502
  32.1 22.7 %copy-start.3 = (bf16[4,2,1,32,384]{4,3,2,1,0:T(8,128)(2,1)}, bf16[4,2,1,32,384]{4,3,2,1,0:T(8,128)(2,1)S(1)}, u32[]{:S(2)}) copy-start(bf16[4,2,1,32,384]{4,3,2,1,0:T(8,128)(2,1)S(1)} %collective-permute-done.came_ref.refs_1_) | copy-start | bytes 589828
  32.1 12.3 %collective-permute-start.1 = (bf16[2,2,1,32,384]{4,3,2,1,0:T(8,128)(2,1)S(1)}, bf16[2,2,1,32,384]{4,3,2,1,0:T(8,128)(2,1)S(1)}, u32[]{:S(2)}, u32[]{:S(2)}) collective-permute-start(bf16[2,2,1,32,384]{4,3,2,1,0:T(8,128)(2,1)S(1)} %get-tuple-element.21), channel_id=1, source_target_pairs={{0,8},{4,12},{8,16},{12,20},{16,24},{20,28},{24,0},{28,4},{1,9},{5... | collective-permute-start | bytes 294920 | tf_op jit(solution)/shard_map/ppermute | solution.py:505
  32.6 22.2 %collective-permute-start.2 = (bf16[2,2,1,32,384]{4,3,2,1,0:T(8,128)(2,1)S(1)}, bf16[2,2,1,32,384]{4,3,2,1,0:T(8,128)(2,1)S(1)}, u32[]{:S(2)}, u32[]{:S(2)}) collective-permute-start(bf16[2,2,1,32,384]{4,3,2,1,0:T(8,128)(2,1)S(1)} %get-tuple-element.22), channel_id=1, source_target_pairs={{0,16},{4,20},{8,24},{12,28},{16,0},{20,4},{24,8},{28,12},{1,17},{... | collective-permute-start | bytes 294920 | tf_op jit(solution)/shard_map/ppermute | solution.py:505
  41.3 13.5 %collective-permute-start.3 = (bf16[2,2,1,32,384]{4,3,2,1,0:T(8,128)(2,1)S(1)}, bf16[2,2,1,32,384]{4,3,2,1,0:T(8,128)(2,1)}, u32[]{:S(2)}, u32[]{:S(2)}) collective-permute-start(bf16[2,2,1,32,384]{4,3,2,1,0:T(8,128)(2,1)S(1)} %get-tuple-element.23), channel_id=1, source_target_pairs={{0,24},{4,28},{8,0},{12,4},{16,8},{20,12},{24,16},{28,20},{1,25},{... | collective-permute-start | bytes 294920 | tf_op jit(solution)/shard_map/ppermute | solution.py:505
  42.4 24.2 %collective-permute-start.4 = (bf16[256,1152]{1,0:T(8,128)(2,1)}, bf16[256,1152]{1,0:T(8,128)(2,1)S(1)}, u32[]{:S(2)}, u32[]{:S(2)}) collective-permute-start(bf16[256,1152]{1,0:T(8,128)(2,1)} %get-tuple-element.28), channel_id=1, source_target_pairs={{0,1},{1,0},{2,3},{3,2},{4,5},{5,4},{6,7},{7,6},{8,9},{9,8},{10,11... | collective-permute-start | bytes 1769480 | tf_op jit(solution)/shard_map/ppermute | solution.py:332
  42.4 24.3 %collective-permute-start.5 = (bf16[256,1152]{1,0:T(8,128)(2,1)}, bf16[256,1152]{1,0:T(8,128)(2,1)S(1)}, u32[]{:S(2)}, u32[]{:S(2)}) collective-permute-start(bf16[256,1152]{1,0:T(8,128)(2,1)} %get-tuple-element.29), channel_id=1, source_target_pairs={{0,2},{1,3},{2,0},{3,1},{4,6},{5,7},{6,4},{7,5},{8,10},{9,11},{10,... | collective-permute-start | bytes 1769480 | tf_op jit(solution)/shard_map/ppermute | solution.py:332
  44.4 10.4 %copy-start.8 = (bf16[2,2,1,32,384]{4,3,2,1,0:T(8,128)(2,1)}, bf16[2,2,1,32,384]{4,3,2,1,0:T(8,128)(2,1)S(1)}, u32[]{:S(2)}) copy-start(bf16[2,2,1,32,384]{4,3,2,1,0:T(8,128)(2,1)S(1)} %collective-permute-done.1.refs_9_) | copy-start | bytes 294916
  44.4 27.2 %collective-permute-start.6 = (bf16[256,1152]{1,0:T(8,128)(2,1)S(1)}, bf16[256,1152]{1,0:T(8,128)(2,1)S(1)}, u32[]{:S(2)}, u32[]{:S(2)}) collective-permute-start(bf16[256,1152]{1,0:T(8,128)(2,1)S(1)} %get-tuple-element.30), channel_id=1, source_target_pairs={{0,3},{1,2},{2,1},{3,0},{4,7},{5,6},{6,5},{7,4},{8,11},{9,10},{10,... | collective-permute-start | bytes 1769480 | tf_op jit(solution)/shard_map/ppermute | solution.py:332
  54.8 0.6 copy-start.9
  61.9 15.4 %all-to-all-start.1 = ((bf16[32,32,128]{2,1,0:T(8,128)(2,1)}), bf16[32,32,128]{2,1,0:T(8,128)(2,1)S(1)}, u32[]{:S(2)}, u32[]{:S(2)}) async-start(bf16[32,32,128]{2,1,0:T(8,128)(2,1)} %bitcast.3), calls=%async_computation.1 | async-start | bytes 524288 | tf_op jit(solution)/shard_map/all_to_all | solution.py:493

commit v4 on v3

--- a/solution.py
+++ b/solution.py
@@ -17,14 +17,23 @@
 LIMIT = 20 * 1024 * 1024
 
 
-def lanes_table():
+def lanes_waves():
     angles = 2.0 * np.pi / LANES * (np.outer(np.arange(LANES), np.arange(LANES)) % LANES)
-    cos, sin = np.cos(angles), np.sin(angles)
-    return jnp.asarray(np.block([[cos, -sin], [sin, cos]]), jnp.bfloat16)
-
-
-def twist_rows(bins):
-    angles = 2.0 * np.pi / (bins * LANES) * np.outer(np.arange(bins), np.arange(LANES))
+    return jnp.asarray(np.stack([np.cos(angles), np.sin(angles)]), jnp.bfloat16)
+
+
+def fill_tables(waves_ref, table_ref, back_ref):
+    cos, sin = waves_ref[0], waves_ref[1]
+    for row, parts in enumerate([(cos, -sin, cos, -sin), (sin, cos, -sin, -cos)]):
+        for col, part in enumerate(parts):
+            table_ref[row * LANES : (row + 1) * LANES, col * LANES : (col + 1) * LANES] = part
+    for row, parts in enumerate([(cos, sin), (sin, -cos), (cos, -sin), (sin, cos)]):
+        for col, part in enumerate(parts):
+            back_ref[row * LANES : (row + 1) * LANES, col * LANES : (col + 1) * LANES] = part
+
+
+def twist_rows(half):
+    angles = np.pi / (half * LANES) * np.outer(np.arange(half + 1), np.arange(LANES))
     return jnp.asarray(np.concatenate([np.cos(angles), -np.sin(angles)]), jnp.float32)
 
 
@@ -32,11 +41,13 @@
     return -(-(share + 2 * count) // LANES) * LANES
 
 
-def share_table(length, share, wide):
-    columns = np.arange(length)
-    table = np.zeros((length, length // share * wide))
-    table[columns, columns // share * wide + columns % share] = 1.0
-    return jnp.asarray(table, jnp.bfloat16)
+def fill_shares(shares_ref, share, wide):
+    length, columns = shares_ref.shape
+    line = lax.broadcasted_iota(jnp.int32, (length, wide), 0)
+    lane = lax.broadcasted_iota(jnp.int32, (length, wide), 1)
+    for part in range(columns // wide):
+        chosen = jnp.logical_and(lane < share, line == lane + part * share)
+        shares_ref[:, part * wide : (part + 1) * wide] = chosen.astype(jnp.bfloat16)
 
 
 def times(pair, k, size, direction):
@@ -278,54 +289,49 @@
 
 
 def forward_tile(values, rows, lines, twist_ref, each):
-    count = 2 * len(values)
     bins = forward_half(values)
-    for k in range(count):
-        cos, sin = twist_ref[k : k + 1], twist_ref[count + k : count + k + 1]
-        re, im = bins[min(k, count - k)]
-        if im is None:
-            pair = (re * cos, re * sin)
-        elif 2 * k < count:
-            pair = (re * cos - im * sin, re * sin + im * cos)
-        else:
-            pair = (re * cos + im * sin, re * sin - im * cos)
+    for k, (re, im) in enumerate(bins):
+        cos, sin = twist_ref[k : k + 1], twist_ref[len(bins) + k : len(bins) + k + 1]
+        pair = (re * cos, re * sin) if im is None else (re * cos - im * sin, re * sin + im * cos)
         at = slice(k * each + rows.start, k * each + rows.stop)
         for part in range(2):
             lines[at, part * LANES : (part + 1) * LANES] = pair[part].astype(jnp.bfloat16)
 
 
-def respond(spectrum, start, order, spectra_ref, lines, each, blocks):
+def respond(spectrum, start, order, spectra_ref, answers, each, blocks, half):
     residues = spectra_ref.shape[1] // 4
     for k in range(start // each, (start + spectrum.shape[0]) // each):
         at = k * each - start
-        re, im = spectrum[at : at + each, :LANES], spectrum[at : at + each, LANES:]
-        block, cols = k % blocks, slice(k // blocks * LANES, (k // blocks + 1) * LANES)
-        first = order * 2 * residues + block % residues
-        gain_re = spectra_ref[block // residues, first, :, cols].astype(jnp.float32)
-        gain_im = spectra_ref[block // residues, first + residues, :, cols].astype(jnp.float32)
-        lines[k * each : (k + 1) * each, :LANES] = (re * gain_re - im * gain_im).astype(jnp.bfloat16)
-        lines[k * each : (k + 1) * each, LANES:] = (-(re * gain_im) - im * gain_re).astype(jnp.bfloat16)
+        for mirror in range(2 if 0 < k < half else 1):
+            col = 2 * mirror * LANES
+            re, im = spectrum[at : at + each, col : col + LANES], spectrum[at : at + each, col + LANES : col + 2 * LANES]
+            bin_at = 2 * half - k if mirror else k
+            block, cols = bin_at % blocks, slice(bin_at // blocks * LANES, (bin_at // blocks + 1) * LANES)
+            first = order * 2 * residues + block % residues
+            gain_re = spectra_ref[block // residues, first, :, cols].astype(jnp.float32)
+            gain_im = spectra_ref[block // residues, first + residues, :, cols].astype(jnp.float32)
+            if mirror:
+                gain_re, gain_im = pltpu.roll(gain_re, 1, 1), pltpu.roll(gain_im, 1, 1)
+            rows = slice(k * each, (k + 1) * each)
+            answers[rows, col : col + LANES] = (re * gain_re - im * gain_im).astype(jnp.bfloat16)
+            answers[rows, col + LANES : col + 2 * LANES] = (-(re * gain_im) - im * gain_re).astype(jnp.bfloat16)
 
 
 def inverse_tile(wave, rows, twist_ref, half, each):
-    count = 2 * half
-    turned = []
-    for k in range(count):
-        cos, sin = twist_ref[k : k + 1], twist_ref[count + k : count + k + 1]
+    bins = []
+    for k in range(half + 1):
+        cos, sin = twist_ref[k : k + 1], twist_ref[half + 1 + k : half + 2 + k]
         at = slice(k * each + rows.start, k * each + rows.stop)
         re, im = wave[at, :LANES], wave[at, LANES:]
-        turned.append((re * cos - im * sin, re * sin + im * cos))
-    bins = [(turned[0][0] * 2.0, None)]
-    for k in range(1, half):
-        one, two = turned[k], turned[count - k]
-        bins.append((one[0] + two[0], two[1] - one[1]))
-    bins.append((turned[half][0] * 2.0, None))
-    return [value * (0.5 / (count * LANES)) for value in inverse_half(bins)]
-
-
-def row_steps(total, most):
-    step = math.gcd(total, most)
-    return [slice(start, start + step) for start in range(0, total, step)]
+        if k in (0, half):
+            bins.append((2.0 * (re * cos + im * sin), None))
+        else:
+            bins.append((re * cos + im * sin, im * cos - re * sin))
+    return [value * (0.25 / (half * LANES)) for value in inverse_half(bins)]
+
+
+def row_steps(total, step):
+    return [slice(start, min(start + step, total)) for start in range(0, total, step)]
 
 
 def flipped(array, flip, size):
@@ -333,10 +339,10 @@
 
 
 def convolve_kernel(*refs):
-    mine_in, came_in, spectra_in, twist_in, table_in, shares_in, taps_ref, skip_ref, edge_ref = refs[:9]
-    shifted, refs = refs[9:-14], refs[-14:]
-    out_ref, held, spectra_ref, twist_ref, table_ref, shares_ref, filtered, lines, wave = refs[:9]
-    gathered, columns, leaving, sems, some = refs[9:]
+    mine_in, came_in, spectra_in, twist_ref, waves_ref, taps_ref, skip_ref, edge_ref = refs[:8]
+    shifted, refs = refs[8:-14], refs[-14:]
+    out_ref, held, spectra_ref, table_ref, back_ref, shares_ref, filtered, lines, answers, wave = refs[:10]
+    gathered, columns, leaving, sems = refs[10:]
     branches, positions, each, length = filtered.shape
     blocks = 2 * positions
     runs = length // LANES
@@ -346,31 +352,24 @@
     me = lax.axis_index("seq")
     other = jnp.bitwise_xor(me, 1)
 
-    inward = [
-        pltpu.make_async_copy(mine_in.at[0], held.at[me], some.at[0]),
-        pltpu.make_async_copy(came_in.at[0], held.at[other], some.at[1]),
-    ]
+    held[me] = mine_in[0]
+    held[other] = came_in[0]
     for shift, ref in enumerate(shifted, 1):
         for i, one in enumerate((me, other)):
-            source = lax.rem(one + count - 2 * shift, count)
-            inward.append(pltpu.make_async_copy(ref.at[i], held.at[source], some.at[2 * shift + i]))
+            held[lax.rem(one + count - 2 * shift, count)] = ref[i]
     halves = [slice(0, slabs // 2), slice(slabs // 2, slabs)]
-    twist = pltpu.make_async_copy(twist_in, twist_ref, sems.at[0])
-    table = pltpu.make_async_copy(table_in, table_ref, sems.at[5])
     spectra = [
         pltpu.make_async_copy(spectra_in.at[:, half], spectra_ref.at[:, half], sems.at[1 + i])
         for i, half in enumerate(halves)
     ]
-    shares = pltpu.make_async_copy(shares_in, shares_ref, sems.at[3])
-    for copy in inward + [twist]:
+    for copy in spectra:
         copy.start()
     columns[...] = tap_columns(taps_ref, skip_ref, gathered)
     mine = columns[pl.ds(pl.multiple_of(me * each, each), each), :]
     lane = lax.broadcasted_iota(jnp.int32, (each, length), 1)
-    for copy in inward:
-        copy.wait()
-    for copy in [table] + spectra + [shares]:
-        copy.start()
+    fill_tables(waves_ref, table_ref, back_ref)
+    wide = out_ref.shape[3]
+    fill_shares(shares_ref, pieces * length // out_ref.shape[1], wide)
     for branch in range(branches):
         last = [jnp.zeros((each, length), jnp.float32)] * 2
         scale = [jnp.broadcast_to(mine[:, branch * 3 + i : branch * 3 + i + 1], (each, length)) for i in range(3)]
@@ -379,21 +378,24 @@
             filtered[branch, p], last = filter_lines(now, last, scale, lane)
     skips = [jnp.broadcast_to(mine[:, 9 + order : 10 + order], (each, LANES)) for order in range(2)]
 
+    half = runs * positions
+    steps = row_steps((half + 1) * each, max(1, 160 // each) * each)
+    for k in (0, half):
+        answers[k * each : (k + 1) * each, 2 * LANES :] = jnp.zeros((each, 2 * LANES), jnp.bfloat16)
+
     def through(order):
         spectra[order].wait()
-        for rows in row_steps(runs * blocks * each, 512):
+        for rows in steps:
             spectrum = jnp.dot(lines[rows], table_ref[...], preferred_element_type=jnp.float32)
-            respond(spectrum, rows.start, order, spectra_ref, lines, each, blocks)
-        for rows in row_steps(runs * blocks * each, 512):
-            wave[rows] = jnp.dot(lines[rows], table_ref[...], preferred_element_type=jnp.float32)
+            respond(spectrum, rows.start, order, spectra_ref, answers, each, blocks, half)
+        for rows in steps:
+            wave[rows] = jnp.dot(answers[rows], back_ref[...], preferred_element_type=jnp.float32)
 
     chunk = min(16, each)
     tiles = [slice(row, row + chunk) for row in range(0, each, chunk)]
     places = [(p, slice(run * LANES, (run + 1) * LANES)) for p in range(positions) for run in range(runs)]
-    twist.wait()
     for rows in tiles:
         forward_tile([filtered[0, p, rows, cols] for p, cols in places], rows, lines, twist_ref, each)
-    table.wait()
     through(0)
     for rows in tiles:
         values = inverse_tile(wave, rows, twist_ref, len(places), each)
@@ -406,20 +408,27 @@
         values = inverse_tile(wave, rows, twist_ref, len(places), each)
         for value, (p, cols) in zip(values, places):
             filtered[0, p, rows, cols] = value + skips[1][rows] * filtered[0, p, rows, cols]
-    shares.wait()
-    wide = out_ref.shape[3]
     parts = shares_ref.shape[1] // wide
-    flat = filtered[0].reshape(positions * each, length).astype(jnp.bfloat16)
-    spread_out = jnp.dot(flat, shares_ref[...], preferred_element_type=jnp.float32)
-    for p in range(positions):
-        for part in range(parts):
-            block = spread_out[p * each : (p + 1) * each, part * wide : (part + 1) * wide]
-            leaving[p // pieces, p % pieces * parts + part] = block.astype(jnp.bfloat16)
     following = lax.rem(me + 1, count)
-    leaving[following, 0] = leaving[following, 0] + edge_ref[...]
-    store = pltpu.make_async_copy(leaving, out_ref, sems.at[4])
-    store.start()
-    store.wait()
+    stores = []
+    for i, some_p in enumerate((range(positions // 2), range(positions // 2, positions))):
+        flat = filtered[0, some_p.start : some_p.stop].reshape(len(some_p) * each, length).astype(jnp.bfloat16)
+        spread_out = jnp.dot(flat, shares_ref[...], preferred_element_type=jnp.float32)
+        for at, p in enumerate(some_p):
+            for part in range(parts):
+                block = spread_out[at * each : (at + 1) * each, part * wide : (part + 1) * wide]
+                leaving[p // pieces, p % pieces * parts + part] = block.astype(jnp.bfloat16)
+        half_count = slice(some_p.start // pieces, some_p.stop // pieces)
+        here = jnp.logical_and(following >= half_count.start, following < half_count.stop)
+
+        @pl.when(here)
+        def _():
+            leaving[following, 0] = leaving[following, 0] + edge_ref[...]
+
+        stores.append(pltpu.make_async_copy(leaving.at[half_count], out_ref.at[half_count], sems.at[2 + i]))
+        stores[-1].start()
+    for store in stores:
+        store.wait()
 
 
 def convolve(mine, came, shifted, spectra, taps, skip, edge, across):
@@ -428,32 +437,32 @@
     positions = count * pieces
     blocks = 2 * positions
     channels = taps.shape[2]
-    twist, table = twist_rows(length // LANES * blocks), lanes_table()
+    half = length // LANES * positions
+    twist, waves = twist_rows(half), lanes_waves()
     share = pieces * length // across
     wide = window_width(share, count)
-    shares = share_table(length, share, wide)
     return pl.pallas_call(
         convolve_kernel,
-        in_specs=[ANY] * 6 + [VMEM] * 3 + [ANY] * len(shifted),
+        in_specs=[VMEM] * 2 + [ANY] + [VMEM] * 5 + [VMEM] * len(shifted),
         out_specs=ANY,
         out_shape=jax.ShapeDtypeStruct((count, across, each, wide), jnp.bfloat16),
         scratch_shapes=[
             pltpu.VMEM((count, branches, pieces, each, length), jnp.bfloat16),
             pltpu.VMEM(spectra.shape, spectra.dtype),
-            pltpu.VMEM(twist.shape, twist.dtype),
-            pltpu.VMEM(table.shape, table.dtype),
-            pltpu.VMEM(shares.shape, shares.dtype),
+            pltpu.VMEM((2 * LANES, 4 * LANES), jnp.bfloat16),
+            pltpu.VMEM((4 * LANES, 2 * LANES), jnp.bfloat16),
+            pltpu.VMEM((length, length // share * wide), jnp.bfloat16),
             pltpu.VMEM((branches, positions, each, length), jnp.float32),
-            pltpu.VMEM((length // LANES * blocks * each, 2 * LANES), jnp.bfloat16),
-            pltpu.VMEM((length // LANES * blocks * each, 2 * LANES), jnp.float32),
+            pltpu.VMEM(((half + 1) * each, 2 * LANES), jnp.bfloat16),
+            pltpu.VMEM(((half + 1) * each, 4 * LANES), jnp.bfloat16),
+            pltpu.VMEM(((half + 1) * each, 2 * LANES), jnp.float32),
             pltpu.VMEM((16, channels), jnp.float32),
             pltpu.VMEM((channels, 16), jnp.float32),
             pltpu.VMEM((count, across, each, wide), jnp.bfloat16),
-            pltpu.SemaphoreType.DMA((6,)),
-            pltpu.SemaphoreType.DMA((count,)),
+            pltpu.SemaphoreType.DMA((4,)),
         ],
-        compiler_params=pltpu.CompilerParams(vmem_limit_bytes=56 * 1024 * 1024),
-    )(mine, came, spectra, twist, table, shares, taps, skip, edge, *shifted)
+        compiler_params=pltpu.CompilerParams(vmem_limit_bytes=52 * 1024 * 1024),
+    )(mine, came, spectra, twist, waves, taps, skip, edge, *shifted)
 
 
 def finish_kernel(share, carried_ref, own_ref, weight_ref, *refs):

time: 79.1 us -> 77.2 us (0.976)
  Pallas kernels: 14.2 us -> 13.3 us
    ppermute x3, waiting for transfers between devices: 4.9 us -> 7.78 us  [flipped(): return lax.ppermute(array, 'tp', [(i, i ^ flip) for i in range(size)])]
    all_to_all x2, waiting for transfers between devices: 5.68 us -> 2.81 us  [spread(): return lax.all_to_all(array, axes, split_axis=0, concat_axis=0, tiled=True)]
    pallas_call x1, Pallas kernels: 6.51 us -> 5.23 us  [convolve(): pl.pallas_call(convolve_kernel, in_specs=[VMEM] * 2 + [ANY] + [VMEM] * 5...]
  transfers between devices with their start and end apart: 9 -> 9, of which waited for: 5 -> 5; matrix products, arithmetic and copies ran while one was open for 0% -> 0% of each run, Pallas kernels for 13% -> 12%
where the time goes in v4:
time: 77.2 us; the launch traced here: 76.9 us
  waiting for transfers between devices  29.7 us (38%)
  starting transfers between devices  25.1 us (33%)
  Pallas kernels  13.3 us (17%)
  blocking collectives  8.6 us (11%)
    all_to_all x2, starting transfers between devices, spread(): return lax.all_to_all(array, axes, split_axis=0, concat_axis=0, tiled=True)  12.2 us
    ppermute x3, waiting for transfers between devices, local(): lax.ppermute(array, 'seq', [(i, (i + 2 * shift) % count) for i in range(c...  10.4 us
    ppermute x3, starting transfers between devices, local(): lax.ppermute(array, 'seq', [(i, (i + 2 * shift) % count) for i in range(c...  9.21 us
    ppermute x1, waiting for transfers between devices, local(): came = lax.ppermute(other, 'seq', [(i, i ^ 1) for i in range(count)])  8.68 us
    all_gather x1, blocking collectives, local(): gathered = lax.all_gather(tokens, 'tp', axis=0, tiled=True)  8.6 us
    ppermute x3, waiting for transfers between devices, flipped(): return lax.ppermute(array, 'tp', [(i, i ^ flip) for i in range(size)])  7.78 us
    pallas_call x1, Pallas kernels, convolve(): pl.pallas_call(convolve_kernel, in_specs=[VMEM] * 2 + [ANY] + [VMEM] * 5...  5.23 us
    pallas_call x1, Pallas kernels, send_spectra(): pl.pallas_call(spectra_kernel, in_specs=[ANY], out_specs=ANY, out_shape=j...  2.94 us
  transfers between devices with their start and end apart: 9, of which 5 were waited for; matrix products, arithmetic and copies ran while one was open for 0% of the time, Pallas kernels for 12%

profile of v4, /device:TPU:0, one launch (start us, length us, event | category | flops | bytes accessed | tf_op | source)
XLA Modules:
  0.0 76.9 jit_solution(4424181255397545724)
XLA Ops:
  0.0 2.9 %shard_map.83 = bf16[8,8,32,384]{3,2,1,0:T(8,128)(2,1)} custom-call(f32[2,2,2,384,256]{4,3,2,1,0:T(8,128)} %spectra_ref.1), custom_call_target="tpu_custom_call" | custom-call | tf_op jit(solution)/shard_map/pallas_call | solution.py:140
  2.9 0.0 copy-start.6
  3.0 0.0 copy-start.1
  3.0 0.0 copy-start.3
  3.0 0.0 copy-start.5
  3.0 7.4 %all-to-all-start = ((bf16[8,8,32,384]{3,2,1,0:T(8,128)(2,1)}), bf16[8,8,32,384]{3,2,1,0:T(8,128)(2,1)}, u32[]{:S(2)}, u32[]{:S(2)}) async-start(bf16[8,8,32,384]{3,2,1,0:T(8,128)(2,1)} %shard_map.83), calls=%async_computation | async-start | bytes 3145728 | tf_op jit(solution)/shard_map/all_to_all | solution.py:502
  10.4 0.0 copy-done.6
  10.4 8.6 %all_gather.3.tokens_ref = bf16[384,1024]{1,0:T(8,128)(2,1)S(1)} all-gather(bf16[96,1024]{1,0:T(8,128)(2,1)S(1)} %copy-done.6), channel_id=1, replica_groups=mesh['seq'=8,'tp'=4] {'tp'}, dimensions={0}, use_global_device_ids=true | all-gather | bytes 983040 | tf_op jit(solution)/shard_map/all_gather | solution.py:509
  19.0 0.0 copy-done.1
  19.0 0.0 copy-done.3
  19.0 0.0 copy-done.5
  19.0 0.0 copy-start
  19.0 0.0 copy-start.2
  19.1 0.0 copy-start.4
  19.1 2.3 %shard_map.82 = (bf16[4,2,1,32,384]{4,3,2,1,0:T(8,128)(2,1)S(1)}, bf16[4,2,1,32,384]{4,3,2,1,0:T(8,128)(2,1)S(1)}, bf16[32,128]{1,0:T(8,128)(2,1)S(1)}, bf16[256...) custom-call(bf16[384,1024]{1,0:T(8,128)(2,1)S(1)} %all_gather.3.toke, ...), custom_call_target="tpu_custom_call" | custom-call | tf_op jit(solution)/shard_map/pallas_call | solution.py:224
  21.3 2.1 %collective-permute-start = (bf16[4,2,1,32,384]{4,3,2,1,0:T(8,128)(2,1)S(1)}, bf16[4,2,1,32,384]{4,3,2,1,0:T(8,128)(2,1)S(1)}, u32[]{:S(2)}, u32[]{:S(2)}) collective-permute-start(bf16[4,2,1,32,384]{4,3,2,1,0:T(8,128)(2,1)S(1)} %get-tuple-element.19), channel_id=1, source_target_pairs={{0,4},{4,0},{8,12},{12,8},{16,20},{20,16},{24,28},{28,24},{1,5},{5... | collective-permute-start | bytes 589832 | tf_op jit(solution)/shard_map/ppermute | solution.py:511
  23.4 8.7 %collective-permute-done.came_ref.refs_1_ = bf16[4,2,1,32,384]{4,3,2,1,0:T(8,128)(2,1)S(1)} collective-permute-done((bf16[4,2,1,32,384]{4,3,2,1,0:T(8,128)(2,1)S(1)}, bf16[4,2,1,32,384]{4,3,2,1,0:T(8,128)(2,1)S(1)}, u32[]{:S(2)}, u32[]{:S(2)}) %collective-permute-start) | collective-permute-done | bytes 196640 | tf_op jit(solution)/shard_map/ppermute | solution.py:511
  32.1 0.5 collective-permute-start.1
  32.6 8.7 %collective-permute-start.2 = (bf16[2,2,1,32,384]{4,3,2,1,0:T(8,128)(2,1)S(1)}, bf16[2,2,1,32,384]{4,3,2,1,0:T(8,128)(2,1)S(1)}, u32[]{:S(2)}, u32[]{:S(2)}) collective-permute-start(bf16[2,2,1,32,384]{4,3,2,1,0:T(8,128)(2,1)S(1)} %get-tuple-element.22), channel_id=1, source_target_pairs={{0,16},{4,20},{8,24},{12,28},{16,0},{20,4},{24,8},{28,12},{1,17},{... | collective-permute-start | bytes 294920 | tf_op jit(solution)/shard_map/ppermute | solution.py:514
  41.3 0.0 collective-permute-start.3
  41.3 0.0 copy-done
  41.3 1.4 %shard_map.86 = (bf16[256,1152]{1,0:T(8,128)(2,1)}, bf16[256,1152]{1,0:T(8,128)(2,1)}, bf16[256,1152]{1,0:T(8,128)(2,1)}) custom-call(bf16[256,1024]{1,0:T(8,128)(2,1)S(1)} %copy-done, bf16[256,128]{1,0:T(8,128)(2,1)S(1)} %get-tuple-element.25.refs_0_, bf16[256,128]{1,0:T(8,128)(2,1)S(1)} %get-tuple-element.26.refs_1_, ...), custom_call_target="tpu_custom_call" | custom-call | tf_op jit(solution)/shard_map/pallas_call | solution.py:265
  42.7 0.0 collective-permute-start.4
  42.7 1.5 %collective-permute-start.5 = (bf16[256,1152]{1,0:T(8,128)(2,1)}, bf16[256,1152]{1,0:T(8,128)(2,1)S(1)}, u32[]{:S(2)}, u32[]{:S(2)}) collective-permute-start(bf16[256,1152]{1,0:T(8,128)(2,1)} %get-tuple-element.29), channel_id=1, source_target_pairs={{0,2},{1,3},{2,0},{3,1},{4,6},{5,7},{6,4},{7,5},{8,10},{9,11},{10,... | collective-permute-start | bytes 1769480 | tf_op jit(solution)/shard_map/ppermute | solution.py:338
  44.2 0.2 collective-permute-done.1.refs_8_
  44.5 0.1 collective-permute-start.6
  44.6 10.2 %collective-permute-done.2.refs_9_ = bf16[2,2,1,32,384]{4,3,2,1,0:T(8,128)(2,1)S(1)} collective-permute-done((bf16[2,2,1,32,384]{4,3,2,1,0:T(8,128)(2,1)S(1)}, bf16[2,2,1,32,384]{4,3,2,1,0:T(8,128)(2,1)S(1)}, u32[]{:S(2)}, u32[]{:S(2)}) %collective-permute-start.2) | collective-permute-done | bytes 98336 | tf_op jit(solution)/shard_map/ppermute | solution.py:514
  54.8 0.0 collective-permute-done.3.refs_10_
  54.8 0.0 all-to-all-done.refs_2_
  54.8 0.0 copy-done.2
  54.8 0.0 copy-done.4
  54.8 5.2 %shard_map.85 = bf16[8,4,32,128]{3,2,1,0:T(8,128)(2,1)} custom-call(bf16[4,2,1,32,384]{4,3,2,1,0:T(8,128)(2,1)S(1)} %get-tuple-element.18.mine_ref.refs_0_, bf16[4,2,1,32,384]{4,3,2,1,0:T(8,128)(2,1)S(1)} %collective-permute-done.came_ref.refs_1_, bf16[8,8,32,384]{3,2,1,0:T(8,128)(2,1)} %all-to-all-done.refs_2_, f32[50,128]{1,0:T(8,128)S(1)} %copy-done.4, ...), custom_call_target="tpu_custom_call" | custom-call | tf_op jit(solution)/shard_map/pallas_call | solution.py:444
  60.1 4.8 %all-to-all-start.1 = ((bf16[32,32,128]{2,1,0:T(8,128)(2,1)}), bf16[32,32,128]{2,1,0:T(8,128)(2,1)S(1)}, u32[]{:S(2)}, u32[]{:S(2)}) async-start(bf16[32,32,128]{2,1,0:T(8,128)(2,1)} %bitcast), calls=%async_computation.1 | async-start | bytes 524288 | tf_op jit(solution)/shard_map/all_to_all | solution.py:502
  64.8 0.0 collective-permute-done.4.refs_0_
  64.9 0.0 collective-permute-done.5.refs_1_
  64.9 7.8 %collective-permute-done.6.refs_2_ = bf16[256,1152]{1,0:T(8,128)(2,1)S(1)} collective-permute-done((bf16[256,1152]{1,0:T(8,128)(2,1)}, bf16[256,1152]{1,0:T(8,128)(2,1)S(1)}, u32[]{:S(2)}, u32[]{:S(2)}) %collective-permute-start.6) | collective-permute-done | bytes 589856 | tf_op jit(solution)/shard_map/ppermute | solution.py:338
  72.6 2.8 %all-to-all-done.1 = bf16[32,32,128]{2,1,0:T(8,128)(2,1)S(1)} async-done(((bf16[32,32,128]{2,1,0:T(8,128)(2,1)}), bf16[32,32,128]{2,1,0:T(8,128)(2,1)S(1)}, u32[]{:S(2)}, u32[]{:S(2)}) %all-to-all-start.1) | async-done | bytes 262176 | tf_op jit(solution)/shard_map/all_to_all | solution.py:502
  75.4 1.4 %shard_map.87 = bf16[96,1024]{1,0:T(8,128)(2,1)} custom-call(bf16[8,4,32,128]{3,2,1,0:T(8,128)(2,1)S(1)} %bitcast.2, bf16[256,128]{1,0:T(8,128)(2,1)S(1)} %get-tuple-element.24.own_ref, bf16[256,1024]{1,0:T(8,128)(2,1)S(1)} %copy-done, bf16[256,1152]{1,0:T(8,128)(2,1)S(1)} %collective-permute-done.4.refs_0_, ...), custom_call_target="tpu_custom_call" | custom-call | tf_op jit(solution)/shard_map/pallas_call | solution.py:492
  (1 shorter events, 0.0 us)
Async XLA Ops:
  2.9 7.5 %copy-start.6 = (bf16[96,1024]{1,0:T(8,128)(2,1)S(1)}, bf16[96,1024]{1,0:T(8,128)(2,1)}, u32[]{:S(2)}) copy-start(bf16[96,1024]{1,0:T(8,128)(2,1)} %param.8) | copy-start | bytes 589828
  3.0 16.1 %copy-start.1 = (bf16[3,1024,256]{2,1,0:T(8,128)(2,1)S(1)}, bf16[3,1024,256]{2,1,0:T(8,128)(2,1)}, u32[]{:S(2)}) copy-start(bf16[3,1024,256]{2,1,0:T(8,128)(2,1)} %weight_ref.3) | copy-start | bytes 4718596
  3.0 16.1 %copy-start.3 = (f32[3,3,256]{2,1,0:T(4,128)S(1)}, f32[3,3,256]{2,1,0:T(4,128)}, u32[]{:S(2)}) copy-start(f32[3,3,256]{2,1,0:T(4,128)} %refs_5_.1) | copy-start | bytes 27652
  3.0 16.0 %copy-start.5 = (f32[2,256]{1,0:T(2,128)S(1)}, f32[2,256]{1,0:T(2,128)}, u32[]{:S(2)}) copy-start(f32[2,256]{1,0:T(2,128)} %refs_6_.1) | copy-start | bytes 6148
  3.0 51.8 %all-to-all-start = ((bf16[8,8,32,384]{3,2,1,0:T(8,128)(2,1)}), bf16[8,8,32,384]{3,2,1,0:T(8,128)(2,1)}, u32[]{:S(2)}, u32[]{:S(2)}) async-start(bf16[8,8,32,384]{3,2,1,0:T(8,128)(2,1)} %shard_map.83), calls=%async_computation | async-start | bytes 3145728 | tf_op jit(solution)/shard_map/all_to_all | solution.py:502
  19.0 22.3 %copy-start = (bf16[256,1024]{1,0:T(8,128)(2,1)S(1)}, bf16[256,1024]{1,0:T(8,128)(2,1)}, u32[]{:S(2)}) copy-start(bf16[256,1024]{1,0:T(8,128)(2,1)} %weight_ref.5) | copy-start | bytes 1572868
  19.0 35.8 %copy-start.2 = (bf16[2,128,128]{2,1,0:T(8,128)(2,1)S(1)}, bf16[2,128,128]{2,1,0:T(8,128)(2,1)}, u32[]{:S(2)}) copy-start(bf16[2,128,128]{2,1,0:T(8,128)(2,1)} %constant.5.clone.refs_4_) | copy-start | bytes 196612
  19.1 35.8 %copy-start.4 = (f32[50,128]{1,0:T(8,128)S(1)}, f32[50,128]{1,0:T(8,128)}, u32[]{:S(2)}) copy-start(f32[50,128]{1,0:T(8,128)} %constant.4.clone.refs_3_) | copy-start | bytes 76804
  21.3 10.8 %collective-permute-start = (bf16[4,2,1,32,384]{4,3,2,1,0:T(8,128)(2,1)S(1)}, bf16[4,2,1,32,384]{4,3,2,1,0:T(8,128)(2,1)S(1)}, u32[]{:S(2)}, u32[]{:S(2)}) collective-permute-start(bf16[4,2,1,32,384]{4,3,2,1,0:T(8,128)(2,1)S(1)} %get-tuple-element.19), channel_id=1, source_target_pairs={{0,4},{4,0},{8,12},{12,8},{16,20},{20,16},{24,28},{28,24},{1,5},{5... | collective-permute-start | bytes 589832 | tf_op jit(solution)/shard_map/ppermute | solution.py:511
  32.1 12.3 %collective-permute-start.1 = (bf16[2,2,1,32,384]{4,3,2,1,0:T(8,128)(2,1)S(1)}, bf16[2,2,1,32,384]{4,3,2,1,0:T(8,128)(2,1)S(1)}, u32[]{:S(2)}, u32[]{:S(2)}) collective-permute-start(bf16[2,2,1,32,384]{4,3,2,1,0:T(8,128)(2,1)S(1)} %get-tuple-element.21), channel_id=1, source_target_pairs={{0,8},{4,12},{8,16},{12,20},{16,24},{20,28},{24,0},{28,4},{1,9},{5... | collective-permute-start | bytes 294920 | tf_op jit(solution)/shard_map/ppermute | solution.py:514
  32.6 22.2 %collective-permute-start.2 = (bf16[2,2,1,32,384]{4,3,2,1,0:T(8,128)(2,1)S(1)}, bf16[2,2,1,32,384]{4,3,2,1,0:T(8,128)(2,1)S(1)}, u32[]{:S(2)}, u32[]{:S(2)}) collective-permute-start(bf16[2,2,1,32,384]{4,3,2,1,0:T(8,128)(2,1)S(1)} %get-tuple-element.22), channel_id=1, source_target_pairs={{0,16},{4,20},{8,24},{12,28},{16,0},{20,4},{24,8},{28,12},{1,17},{... | collective-permute-start | bytes 294920 | tf_op jit(solution)/shard_map/ppermute | solution.py:514
  41.3 13.5 %collective-permute-start.3 = (bf16[2,2,1,32,384]{4,3,2,1,0:T(8,128)(2,1)S(1)}, bf16[2,2,1,32,384]{4,3,2,1,0:T(8,128)(2,1)S(1)}, u32[]{:S(2)}, u32[]{:S(2)}) collective-permute-start(bf16[2,2,1,32,384]{4,3,2,1,0:T(8,128)(2,1)S(1)} %get-tuple-element.23), channel_id=1, source_target_pairs={{0,24},{4,28},{8,0},{12,4},{16,8},{20,12},{24,16},{28,20},{1,25},{... | collective-permute-start | bytes 294920 | tf_op jit(solution)/shard_map/ppermute | solution.py:514
  42.7 22.1 %collective-permute-start.4 = (bf16[256,1152]{1,0:T(8,128)(2,1)}, bf16[256,1152]{1,0:T(8,128)(2,1)S(1)}, u32[]{:S(2)}, u32[]{:S(2)}) collective-permute-start(bf16[256,1152]{1,0:T(8,128)(2,1)} %get-tuple-element.28), channel_id=1, source_target_pairs={{0,1},{1,0},{2,3},{3,2},{4,5},{5,4},{6,7},{7,6},{8,9},{9,8},{10,11... | collective-permute-start | bytes 1769480 | tf_op jit(solution)/shard_map/ppermute | solution.py:338
  42.7 22.1 %collective-permute-start.5 = (bf16[256,1152]{1,0:T(8,128)(2,1)}, bf16[256,1152]{1,0:T(8,128)(2,1)S(1)}, u32[]{:S(2)}, u32[]{:S(2)}) collective-permute-start(bf16[256,1152]{1,0:T(8,128)(2,1)} %get-tuple-element.29), channel_id=1, source_target_pairs={{0,2},{1,3},{2,0},{3,1},{4,6},{5,7},{6,4},{7,5},{8,10},{9,11},{10,... | collective-permute-start | bytes 1769480 | tf_op jit(solution)/shard_map/ppermute | solution.py:338
  44.5 28.2 %collective-permute-start.6 = (bf16[256,1152]{1,0:T(8,128)(2,1)}, bf16[256,1152]{1,0:T(8,128)(2,1)S(1)}, u32[]{:S(2)}, u32[]{:S(2)}) collective-permute-start(bf16[256,1152]{1,0:T(8,128)(2,1)} %get-tuple-element.30), channel_id=1, source_target_pairs={{0,3},{1,2},{2,1},{3,0},{4,7},{5,6},{6,5},{7,4},{8,11},{9,10},{10,... | collective-permute-start | bytes 1769480 | tf_op jit(solution)/shard_map/ppermute | solution.py:338
  60.1 15.4 %all-to-all-start.1 = ((bf16[32,32,128]{2,1,0:T(8,128)(2,1)}), bf16[32,32,128]{2,1,0:T(8,128)(2,1)S(1)}, u32[]{:S(2)}, u32[]{:S(2)}) async-start(bf16[32,32,128]{2,1,0:T(8,128)(2,1)} %bitcast), calls=%async_computation.1 | async-start | bytes 524288 | tf_op jit(solution)/shard_map/all_to_all | solution.py:502

commit v5 on v4

--- a/solution.py
+++ b/solution.py
@@ -340,9 +340,9 @@
 
 def convolve_kernel(*refs):
     mine_in, came_in, spectra_in, twist_ref, waves_ref, taps_ref, skip_ref, edge_ref = refs[:8]
-    shifted, refs = refs[8:-14], refs[-14:]
+    shifted, refs = refs[8:-13], refs[-13:]
     out_ref, held, spectra_ref, table_ref, back_ref, shares_ref, filtered, lines, answers, wave = refs[:10]
-    gathered, columns, leaving, sems = refs[10:]
+    gathered, columns, sems = refs[10:]
     branches, positions, each, length = filtered.shape
     blocks = 2 * positions
     runs = length // LANES
@@ -410,8 +410,8 @@
             filtered[0, p, rows, cols] = value + skips[1][rows] * filtered[0, p, rows, cols]
     parts = shares_ref.shape[1] // wide
     following = lax.rem(me + 1, count)
-    stores = []
-    for i, some_p in enumerate((range(positions // 2), range(positions // 2, positions))):
+    leaving = out_ref
+    for some_p in (range(positions // 2), range(positions // 2, positions)):
         flat = filtered[0, some_p.start : some_p.stop].reshape(len(some_p) * each, length).astype(jnp.bfloat16)
         spread_out = jnp.dot(flat, shares_ref[...], preferred_element_type=jnp.float32)
         for at, p in enumerate(some_p):
@@ -424,11 +424,6 @@
         @pl.when(here)
         def _():
             leaving[following, 0] = leaving[following, 0] + edge_ref[...]
-
-        stores.append(pltpu.make_async_copy(leaving.at[half_count], out_ref.at[half_count], sems.at[2 + i]))
-        stores[-1].start()
-    for store in stores:
-        store.wait()
 
 
 def convolve(mine, came, shifted, spectra, taps, skip, edge, across):
@@ -444,7 +439,7 @@
     return pl.pallas_call(
         convolve_kernel,
         in_specs=[VMEM] * 2 + [ANY] + [VMEM] * 5 + [VMEM] * len(shifted),
-        out_specs=ANY,
+        out_specs=VMEM,
         out_shape=jax.ShapeDtypeStruct((count, across, each, wide), jnp.bfloat16),
         scratch_shapes=[
             pltpu.VMEM((count, branches, pieces, each, length), jnp.bfloat16),
@@ -458,7 +453,6 @@
             pltpu.VMEM(((half + 1) * each, 2 * LANES), jnp.float32),
             pltpu.VMEM((16, channels), jnp.float32),
             pltpu.VMEM((channels, 16), jnp.float32),
-            pltpu.VMEM((count, across, each, wide), jnp.bfloat16),
             pltpu.SemaphoreType.DMA((4,)),
         ],
         compiler_params=pltpu.CompilerParams(vmem_limit_bytes=52 * 1024 * 1024),
@@ -509,12 +503,13 @@
     gathered = lax.all_gather(tokens, "tp", axis=0, tiled=True)
     mine, other, edge, own, *windows = project(gathered, w_in, short_taps, skip_bias, count, across, length)
     came = lax.ppermute(other, "seq", [(i, i ^ 1) for i in range(count)])
+    came, *packed = lax.optimization_barrier((came, *pack(windows, w_out)))
     onward = relay(mine, came)
     shifted = [
         lax.ppermute(array, "seq", [(i, (i + 2 * shift) % count) for i in range(count)])
         for shift, array in enumerate(onward, 1)
     ]
-    packed = [flipped(array, flip, across) for flip, array in enumerate(pack(windows, w_out), 1)]
+    packed = [flipped(array, flip, across) for flip, array in enumerate(packed, 1)]
     carried = convolve(mine, came, shifted, spectra, short_taps, skip_bias, edge, across)
     shape = carried.shape
     carried = spread(carried.reshape((count * across,) + shape[2:]), ("seq", "tp"))

time: 77.2 us -> 76.5 us (level)
    ppermute x3, waiting for transfers between devices: 10.4 us -> 12 us  [local(): lax.ppermute(array, 'seq', [(i, (i + 2 * shift) % count) for i in range(c...]
    ppermute x1, waiting for transfers between devices: 8.68 us -> 7.28 us  [local(): came = lax.ppermute(other, 'seq', [(i, i ^ 1) for i in range(count)])]
    ppermute x3, waiting for transfers between devices: 7.78 us -> 6.65 us  [flipped(): return lax.ppermute(array, 'tp', [(i, i ^ flip) for i in range(size)])]
    all_to_all x2, waiting for transfers between devices: 2.81 us -> 3.94 us  [spread(): return lax.all_to_all(array, axes, split_axis=0, concat_axis=0, tiled=True)]
  transfers between devices with their start and end apart: 9 -> 9, of which waited for: 5 -> 5; matrix products, arithmetic and copies ran while one was open for 0% -> 0% of each run, Pallas kernels for 12% -> 11%
where the time goes in v5:
time: 76.5 us; the launch traced here: 76.2 us
  waiting for transfers between devices  29.8 us (39%)
  starting transfers between devices  24.8 us (32%)
  Pallas kernels  12.7 us (17%)
  blocking collectives  8.73 us (11%)
    all_to_all x2, starting transfers between devices, spread(): return lax.all_to_all(array, axes, split_axis=0, concat_axis=0, tiled=True)  12.2 us
    ppermute x3, waiting for transfers between devices, local(): lax.ppermute(array, 'seq', [(i, (i + 2 * shift) % count) for i in range(c...  12 us
    ppermute x3, starting transfers between devices, local(): lax.ppermute(array, 'seq', [(i, (i + 2 * shift) % count) for i in range(c...  9.07 us
    all_gather x1, blocking collectives, local(): gathered = lax.all_gather(tokens, 'tp', axis=0, tiled=True)  8.73 us
    ppermute x1, waiting for transfers between devices, local(): came = lax.ppermute(other, 'seq', [(i, i ^ 1) for i in range(count)])  7.28 us
    ppermute x3, waiting for transfers between devices, flipped(): return lax.ppermute(array, 'tp', [(i, i ^ flip) for i in range(size)])  6.65 us
    pallas_call x1, Pallas kernels, convolve(): pl.pallas_call(convolve_kernel, in_specs=[VMEM] * 2 + [ANY] + [VMEM] * 5...  4.61 us
    all_to_all x2, waiting for transfers between devices, spread(): return lax.all_to_all(array, axes, split_axis=0, concat_axis=0, tiled=True)  3.94 us
  transfers between devices with their start and end apart: 9, of which 5 were waited for; matrix products, arithmetic and copies ran while one was open for 0% of the time, Pallas kernels for 11%

profile of v5, /device:TPU:0, one launch (start us, length us, event | category | flops | bytes accessed | tf_op | source)
XLA Modules:
  0.0 76.2 jit_solution(6910419186756901943)
XLA Ops:
  0.0 2.9 %shard_map.84 = bf16[8,8,32,384]{3,2,1,0:T(8,128)(2,1)} custom-call(f32[2,2,2,384,256]{4,3,2,1,0:T(8,128)} %spectra_ref.1), custom_call_target="tpu_custom_call" | custom-call | tf_op jit(solution)/shard_map/pallas_call | solution.py:140
  2.9 0.0 copy-start.6
  3.0 0.0 copy-start.1
  3.0 0.0 copy-start.3
  3.0 0.0 copy-start.5
  3.0 7.4 %all-to-all-start = ((bf16[8,8,32,384]{3,2,1,0:T(8,128)(2,1)}), bf16[8,8,32,384]{3,2,1,0:T(8,128)(2,1)}, u32[]{:S(2)}, u32[]{:S(2)}) async-start(bf16[8,8,32,384]{3,2,1,0:T(8,128)(2,1)} %shard_map.84), calls=%async_computation | async-start | bytes 3145728 | tf_op jit(solution)/shard_map/all_to_all | solution.py:496
  10.4 0.0 copy-done.6
  10.4 0.0 copy-start
  10.4 8.7 %all_gather.3.tokens_ref = bf16[384,1024]{1,0:T(8,128)(2,1)S(1)} all-gather(bf16[96,1024]{1,0:T(8,128)(2,1)S(1)} %copy-done.6), channel_id=1, replica_groups=mesh['seq'=8,'tp'=4] {'tp'}, dimensions={0}, use_global_device_ids=true | all-gather | bytes 983040 | tf_op jit(solution)/shard_map/all_gather | solution.py:503
  19.2 0.0 copy-done.1
  19.2 0.0 copy-done.3
  19.2 0.0 copy-done.5
  19.2 0.0 copy-start.2
  19.2 0.0 copy-start.4
  19.2 2.3 %shard_map.82 = (bf16[4,2,1,32,384]{4,3,2,1,0:T(8,128)(2,1)S(1)}, bf16[4,2,1,32,384]{4,3,2,1,0:T(8,128)(2,1)S(1)}, bf16[32,128]{1,0:T(8,128)(2,1)S(1)}, bf16[256...) custom-call(bf16[384,1024]{1,0:T(8,128)(2,1)S(1)} %all_gather.3.toke, ...), custom_call_target="tpu_custom_call" | custom-call | tf_op jit(solution)/shard_map/pallas_call | solution.py:224
  21.5 2.1 %collective-permute-start = (bf16[4,2,1,32,384]{4,3,2,1,0:T(8,128)(2,1)S(1)}, bf16[4,2,1,32,384]{4,3,2,1,0:T(8,128)(2,1)S(1)}, u32[]{:S(2)}, u32[]{:S(2)}) collective-permute-start(bf16[4,2,1,32,384]{4,3,2,1,0:T(8,128)(2,1)S(1)} %get-tuple-element.23), channel_id=1, source_target_pairs={{0,4},{4,0},{8,12},{12,8},{16,20},{20,16},{24,28},{28,24},{1,5},{5... | collective-permute-start | bytes 589832 | tf_op jit(solution)/shard_map/ppermute | solution.py:505
  23.5 0.0 copy-done
  23.5 1.4 %shard_map.83 = (bf16[256,1152]{1,0:T(8,128)(2,1)}, bf16[256,1152]{1,0:T(8,128)(2,1)}, bf16[256,1152]{1,0:T(8,128)(2,1)}) custom-call(bf16[256,1024]{1,0:T(8,128)(2,1)S(1)} %copy-done, bf16[256,128]{1,0:T(8,128)(2,1)S(1)} %get-tuple-element.24.refs_0_, bf16[256,128]{1,0:T(8,128)(2,1)S(1)} %get-tuple-element.25.refs_1_, ...), custom_call_target="tpu_custom_call" | custom-call | tf_op jit(solution)/shard_map/pallas_call | solution.py:265
  24.9 7.3 %collective-permute-done.came_ref.refs_1_ = bf16[4,2,1,32,384]{4,3,2,1,0:T(8,128)(2,1)S(1)} collective-permute-done((bf16[4,2,1,32,384]{4,3,2,1,0:T(8,128)(2,1)S(1)}, bf16[4,2,1,32,384]{4,3,2,1,0:T(8,128)(2,1)S(1)}, u32[]{:S(2)}, u32[]{:S(2)}) %collective-permute-start) | collective-permute-done | bytes 196640 | tf_op jit(solution)/shard_map/ppermute | solution.py:505
  32.3 3.0 %collective-permute-start.1 = (bf16[2,2,1,32,384]{4,3,2,1,0:T(8,128)(2,1)S(1)}, bf16[2,2,1,32,384]{4,3,2,1,0:T(8,128)(2,1)S(1)}, u32[]{:S(2)}, u32[]{:S(2)}) collective-permute-start(bf16[2,2,1,32,384]{4,3,2,1,0:T(8,128)(2,1)S(1)} %get-tuple-element.32), channel_id=1, source_target_pairs={{0,8},{4,12},{8,16},{12,20},{16,24},{20,28},{24,0},{28,4},{1,9},{5... | collective-permute-start | bytes 294920 | tf_op jit(solution)/shard_map/ppermute | solution.py:509
  35.3 6.1 %collective-permute-start.2 = (bf16[2,2,1,32,384]{4,3,2,1,0:T(8,128)(2,1)S(1)}, bf16[2,2,1,32,384]{4,3,2,1,0:T(8,128)(2,1)S(1)}, u32[]{:S(2)}, u32[]{:S(2)}) collective-permute-start(bf16[2,2,1,32,384]{4,3,2,1,0:T(8,128)(2,1)S(1)} %get-tuple-element.33), channel_id=1, source_target_pairs={{0,16},{4,20},{8,24},{12,28},{16,0},{20,4},{24,8},{28,12},{1,17},{... | collective-permute-start | bytes 294920 | tf_op jit(solution)/shard_map/ppermute | solution.py:509
  41.3 0.0 collective-permute-start.3
  41.3 0.0 collective-permute-start.4
  41.3 1.5 %collective-permute-start.5 = (bf16[256,1152]{1,0:T(8,128)(2,1)}, bf16[256,1152]{1,0:T(8,128)(2,1)S(1)}, u32[]{:S(2)}, u32[]{:S(2)}) collective-permute-start(bf16[256,1152]{1,0:T(8,128)(2,1)} %get-tuple-element.37), channel_id=1, source_target_pairs={{0,2},{1,3},{2,0},{3,1},{4,6},{5,7},{6,4},{7,5},{8,10},{9,11},{10,... | collective-permute-start | bytes 1769480 | tf_op jit(solution)/shard_map/ppermute | solution.py:338
  42.8 1.6 %collective-permute-done.1.refs_8_ = bf16[2,2,1,32,384]{4,3,2,1,0:T(8,128)(2,1)S(1)} collective-permute-done((bf16[2,2,1,32,384]{4,3,2,1,0:T(8,128)(2,1)S(1)}, bf16[2,2,1,32,384]{4,3,2,1,0:T(8,128)(2,1)S(1)}, u32[]{:S(2)}, u32[]{:S(2)}) %collective-permute-start.1) | collective-permute-done | bytes 98336 | tf_op jit(solution)/shard_map/ppermute | solution.py:509
  44.5 0.0 collective-permute-start.6
  44.5 10.3 %collective-permute-done.2.refs_9_ = bf16[2,2,1,32,384]{4,3,2,1,0:T(8,128)(2,1)S(1)} collective-permute-done((bf16[2,2,1,32,384]{4,3,2,1,0:T(8,128)(2,1)S(1)}, bf16[2,2,1,32,384]{4,3,2,1,0:T(8,128)(2,1)S(1)}, u32[]{:S(2)}, u32[]{:S(2)}) %collective-permute-start.2) | collective-permute-done | bytes 98336 | tf_op jit(solution)/shard_map/ppermute | solution.py:509
  54.8 0.0 collective-permute-done.3.refs_10_
  54.8 0.0 all-to-all-done.refs_2_
  54.8 0.0 copy-done.2
  54.8 0.0 copy-done.4
  54.8 4.6 %shard_map.86 = bf16[8,4,32,128]{3,2,1,0:T(8,128)(2,1)} custom-call(bf16[4,2,1,32,384]{4,3,2,1,0:T(8,128)(2,1)S(1)} %get-tuple-element.22.mine_ref.refs_0_, bf16[4,2,1,32,384]{4,3,2,1,0:T(8,128)(2,1)S(1)} %collective-permute-done.came_ref.refs_1_, bf16[8,8,32,384]{3,2,1,0:T(8,128)(2,1)} %all-to-all-done.refs_2_, f32[50,128]{1,0:T(8,128)S(1)} %copy-done.4, ...), custom_call_target="tpu_custom_call" | custom-call | tf_op jit(solution)/shard_map/pallas_call | solution.py:439
  59.4 4.8 %all-to-all-start.1 = ((bf16[32,32,128]{2,1,0:T(8,128)(2,1)}), bf16[32,32,128]{2,1,0:T(8,128)(2,1)S(1)}, u32[]{:S(2)}, u32[]{:S(2)}) async-start(bf16[32,32,128]{2,1,0:T(8,128)(2,1)} %bitcast), calls=%async_computation.1 | async-start | bytes 524288 | tf_op jit(solution)/shard_map/all_to_all | solution.py:496
  64.2 0.0 collective-permute-done.4.refs_0_
  64.2 0.0 collective-permute-done.5.refs_1_
  64.2 6.6 %collective-permute-done.6.refs_2_ = bf16[256,1152]{1,0:T(8,128)(2,1)S(1)} collective-permute-done((bf16[256,1152]{1,0:T(8,128)(2,1)}, bf16[256,1152]{1,0:T(8,128)(2,1)S(1)}, u32[]{:S(2)}, u32[]{:S(2)}) %collective-permute-start.6) | collective-permute-done | bytes 589856 | tf_op jit(solution)/shard_map/ppermute | solution.py:338
  70.9 3.9 %all-to-all-done.1 = bf16[32,32,128]{2,1,0:T(8,128)(2,1)S(1)} async-done(((bf16[32,32,128]{2,1,0:T(8,128)(2,1)}), bf16[32,32,128]{2,1,0:T(8,128)(2,1)S(1)}, u32[]{:S(2)}, u32[]{:S(2)}) %all-to-all-start.1) | async-done | bytes 262176 | tf_op jit(solution)/shard_map/all_to_all | solution.py:496
  74.8 1.4 %shard_map.87 = bf16[96,1024]{1,0:T(8,128)(2,1)} custom-call(bf16[8,4,32,128]{3,2,1,0:T(8,128)(2,1)S(1)} %bitcast.2, bf16[256,128]{1,0:T(8,128)(2,1)S(1)} %get-tuple-element.35.own_ref, bf16[256,1024]{1,0:T(8,128)(2,1)S(1)} %copy-done, bf16[256,1152]{1,0:T(8,128)(2,1)S(1)} %collective-permute-done.4.refs_0_, ...), custom_call_target="tpu_custom_call" | custom-call | tf_op jit(solution)/shard_map/pallas_call | solution.py:486
  (1 shorter events, 0.0 us)
Async XLA Ops:
  2.9 7.5 %copy-start.6 = (bf16[96,1024]{1,0:T(8,128)(2,1)S(1)}, bf16[96,1024]{1,0:T(8,128)(2,1)}, u32[]{:S(2)}) copy-start(bf16[96,1024]{1,0:T(8,128)(2,1)} %param.8) | copy-start | bytes 589828
  3.0 16.2 %copy-start.1 = (bf16[3,1024,256]{2,1,0:T(8,128)(2,1)S(1)}, bf16[3,1024,256]{2,1,0:T(8,128)(2,1)}, u32[]{:S(2)}) copy-start(bf16[3,1024,256]{2,1,0:T(8,128)(2,1)} %weight_ref.3) | copy-start | bytes 4718596
  3.0 16.2 %copy-start.3 = (f32[3,3,256]{2,1,0:T(4,128)S(1)}, f32[3,3,256]{2,1,0:T(4,128)}, u32[]{:S(2)}) copy-start(f32[3,3,256]{2,1,0:T(4,128)} %refs_5_.1) | copy-start | bytes 27652
  3.0 16.2 %copy-start.5 = (f32[2,256]{1,0:T(2,128)S(1)}, f32[2,256]{1,0:T(2,128)}, u32[]{:S(2)}) copy-start(f32[2,256]{1,0:T(2,128)} %refs_6_.1) | copy-start | bytes 6148
  3.0 51.8 %all-to-all-start = ((bf16[8,8,32,384]{3,2,1,0:T(8,128)(2,1)}), bf16[8,8,32,384]{3,2,1,0:T(8,128)(2,1)}, u32[]{:S(2)}, u32[]{:S(2)}) async-start(bf16[8,8,32,384]{3,2,1,0:T(8,128)(2,1)} %shard_map.84), calls=%async_computation | async-start | bytes 3145728 | tf_op jit(solution)/shard_map/all_to_all | solution.py:496
  10.4 13.1 %copy-start = (bf16[256,1024]{1,0:T(8,128)(2,1)S(1)}, bf16[256,1024]{1,0:T(8,128)(2,1)}, u32[]{:S(2)}) copy-start(bf16[256,1024]{1,0:T(8,128)(2,1)} %weight_ref.5) | copy-start | bytes 1572868
  19.2 35.6 %copy-start.2 = (bf16[2,128,128]{2,1,0:T(8,128)(2,1)S(1)}, bf16[2,128,128]{2,1,0:T(8,128)(2,1)}, u32[]{:S(2)}) copy-start(bf16[2,128,128]{2,1,0:T(8,128)(2,1)} %constant.5.clone.refs_4_) | copy-start | bytes 196612
  19.2 35.6 %copy-start.4 = (f32[50,128]{1,0:T(8,128)S(1)}, f32[50,128]{1,0:T(8,128)}, u32[]{:S(2)}) copy-start(f32[50,128]{1,0:T(8,128)} %constant.4.clone.refs_3_) | copy-start | bytes 76804
  21.5 10.8 %collective-permute-start = (bf16[4,2,1,32,384]{4,3,2,1,0:T(8,128)(2,1)S(1)}, bf16[4,2,1,32,384]{4,3,2,1,0:T(8,128)(2,1)S(1)}, u32[]{:S(2)}, u32[]{:S(2)}) collective-permute-start(bf16[4,2,1,32,384]{4,3,2,1,0:T(8,128)(2,1)S(1)} %get-tuple-element.23), channel_id=1, source_target_pairs={{0,4},{4,0},{8,12},{12,8},{16,20},{20,16},{24,28},{28,24},{1,5},{5... | collective-permute-start | bytes 589832 | tf_op jit(solution)/shard_map/ppermute | solution.py:505
  32.3 12.2 %collective-permute-start.1 = (bf16[2,2,1,32,384]{4,3,2,1,0:T(8,128)(2,1)S(1)}, bf16[2,2,1,32,384]{4,3,2,1,0:T(8,128)(2,1)S(1)}, u32[]{:S(2)}, u32[]{:S(2)}) collective-permute-start(bf16[2,2,1,32,384]{4,3,2,1,0:T(8,128)(2,1)S(1)} %get-tuple-element.32), channel_id=1, source_target_pairs={{0,8},{4,12},{8,16},{12,20},{16,24},{20,28},{24,0},{28,4},{1,9},{5... | collective-permute-start | bytes 294920 | tf_op jit(solution)/shard_map/ppermute | solution.py:509
  35.3 19.5 %collective-permute-start.2 = (bf16[2,2,1,32,384]{4,3,2,1,0:T(8,128)(2,1)S(1)}, bf16[2,2,1,32,384]{4,3,2,1,0:T(8,128)(2,1)S(1)}, u32[]{:S(2)}, u32[]{:S(2)}) collective-permute-start(bf16[2,2,1,32,384]{4,3,2,1,0:T(8,128)(2,1)S(1)} %get-tuple-element.33), channel_id=1, source_target_pairs={{0,16},{4,20},{8,24},{12,28},{16,0},{20,4},{24,8},{28,12},{1,17},{... | collective-permute-start | bytes 294920 | tf_op jit(solution)/shard_map/ppermute | solution.py:509
  41.3 13.5 %collective-permute-start.3 = (bf16[2,2,1,32,384]{4,3,2,1,0:T(8,128)(2,1)S(1)}, bf16[2,2,1,32,384]{4,3,2,1,0:T(8,128)(2,1)S(1)}, u32[]{:S(2)}, u32[]{:S(2)}) collective-permute-start(bf16[2,2,1,32,384]{4,3,2,1,0:T(8,128)(2,1)S(1)} %get-tuple-element.34), channel_id=1, source_target_pairs={{0,24},{4,28},{8,0},{12,4},{16,8},{20,12},{24,16},{28,20},{1,25},{... | collective-permute-start | bytes 294920 | tf_op jit(solution)/shard_map/ppermute | solution.py:509
  41.3 22.9 %collective-permute-start.4 = (bf16[256,1152]{1,0:T(8,128)(2,1)}, bf16[256,1152]{1,0:T(8,128)(2,1)S(1)}, u32[]{:S(2)}, u32[]{:S(2)}) collective-permute-start(bf16[256,1152]{1,0:T(8,128)(2,1)} %get-tuple-element.36), channel_id=1, source_target_pairs={{0,1},{1,0},{2,3},{3,2},{4,5},{5,4},{6,7},{7,6},{8,9},{9,8},{10,11... | collective-permute-start | bytes 1769480 | tf_op jit(solution)/shard_map/ppermute | solution.py:338
  41.3 22.9 %collective-permute-start.5 = (bf16[256,1152]{1,0:T(8,128)(2,1)}, bf16[256,1152]{1,0:T(8,128)(2,1)S(1)}, u32[]{:S(2)}, u32[]{:S(2)}) collective-permute-start(bf16[256,1152]{1,0:T(8,128)(2,1)} %get-tuple-element.37), channel_id=1, source_target_pairs={{0,2},{1,3},{2,0},{3,1},{4,6},{5,7},{6,4},{7,5},{8,10},{9,11},{10,... | collective-permute-start | bytes 1769480 | tf_op jit(solution)/shard_map/ppermute | solution.py:338
  44.5 26.4 %collective-permute-start.6 = (bf16[256,1152]{1,0:T(8,128)(2,1)}, bf16[256,1152]{1,0:T(8,128)(2,1)S(1)}, u32[]{:S(2)}, u32[]{:S(2)}) collective-permute-start(bf16[256,1152]{1,0:T(8,128)(2,1)} %get-tuple-element.38), channel_id=1, source_target_pairs={{0,3},{1,2},{2,1},{3,0},{4,7},{5,6},{6,5},{7,4},{8,11},{9,10},{10,... | collective-permute-start | bytes 1769480 | tf_op jit(solution)/shard_map/ppermute | solution.py:338
  59.4 15.4 %all-to-all-start.1 = ((bf16[32,32,128]{2,1,0:T(8,128)(2,1)}), bf16[32,32,128]{2,1,0:T(8,128)(2,1)S(1)}, u32[]{:S(2)}, u32[]{:S(2)}) async-start(bf16[32,32,128]{2,1,0:T(8,128)(2,1)} %bitcast), calls=%async_computation.1 | async-start | bytes 524288 | tf_op jit(solution)/shard_map/all_to_all | solution.py:496

commit v6 on v5

--- a/solution.py
+++ b/solution.py
@@ -379,7 +379,7 @@
     skips = [jnp.broadcast_to(mine[:, 9 + order : 10 + order], (each, LANES)) for order in range(2)]
 
     half = runs * positions
-    steps = row_steps((half + 1) * each, max(1, 160 // each) * each)
+    steps = row_steps((half + 1) * each, max(1, 416 // each) * each)
     for k in (0, half):
         answers[k * each : (k + 1) * each, 2 * LANES :] = jnp.zeros((each, 2 * LANES), jnp.bfloat16)
 

time: 76.5 us -> 76.5 us (level)
  no operation moved by 1% of the time
where the time goes in v6:
time: 76.5 us; the launch traced here: 76.2 us
  waiting for transfers between devices  29.8 us (39%)
  starting transfers between devices  24.8 us (32%)
  Pallas kernels  12.7 us (17%)
  blocking collectives  8.73 us (11%)
    all_to_all x2, starting transfers between devices, spread(): return lax.all_to_all(array, axes, split_axis=0, concat_axis=0, tiled=True)  12.2 us
    ppermute x3, waiting for transfers between devices, local(): lax.ppermute(array, 'seq', [(i, (i + 2 * shift) % count) for i in range(c...  12 us
    ppermute x3, starting transfers between devices, local(): lax.ppermute(array, 'seq', [(i, (i + 2 * shift) % count) for i in range(c...  9.07 us
    all_gather x1, blocking collectives, local(): gathered = lax.all_gather(tokens, 'tp', axis=0, tiled=True)  8.73 us
    ppermute x1, waiting for transfers between devices, local(): came = lax.ppermute(other, 'seq', [(i, i ^ 1) for i in range(count)])  7.28 us
    ppermute x3, waiting for transfers between devices, flipped(): return lax.ppermute(array, 'tp', [(i, i ^ flip) for i in range(size)])  6.64 us
    pallas_call x1, Pallas kernels, convolve(): pl.pallas_call(convolve_kernel, in_specs=[VMEM] * 2 + [ANY] + [VMEM] * 5...  4.63 us
    all_to_all x2, waiting for transfers between devices, spread(): return lax.all_to_all(array, axes, split_axis=0, concat_axis=0, tiled=True)  3.95 us
  transfers between devices with their start and end apart: 9, of which 5 were waited for; matrix products, arithmetic and copies ran while one was open for 0% of the time, Pallas kernels for 11%

profile of v6, /device:TPU:0, one launch (start us, length us, event | category | flops | bytes accessed | tf_op | source)
XLA Modules:
  0.0 76.2 jit_solution(18348274422101374590)
XLA Ops:
  0.0 2.9 %shard_map.84 = bf16[8,8,32,384]{3,2,1,0:T(8,128)(2,1)} custom-call(f32[2,2,2,384,256]{4,3,2,1,0:T(8,128)} %spectra_ref.1), custom_call_target="tpu_custom_call" | custom-call | tf_op jit(solution)/shard_map/pallas_call | solution.py:140
  2.9 0.0 copy-start.6
  3.0 0.0 copy-start.1
  3.0 0.0 copy-start.3
  3.0 0.0 copy-start.5
  3.0 7.4 %all-to-all-start = ((bf16[8,8,32,384]{3,2,1,0:T(8,128)(2,1)}), bf16[8,8,32,384]{3,2,1,0:T(8,128)(2,1)}, u32[]{:S(2)}, u32[]{:S(2)}) async-start(bf16[8,8,32,384]{3,2,1,0:T(8,128)(2,1)} %shard_map.84), calls=%async_computation | async-start | bytes 3145728 | tf_op jit(solution)/shard_map/all_to_all | solution.py:496
  10.4 0.0 copy-done.6
  10.4 0.0 copy-start
  10.4 8.7 %all_gather.3.tokens_ref = bf16[384,1024]{1,0:T(8,128)(2,1)S(1)} all-gather(bf16[96,1024]{1,0:T(8,128)(2,1)S(1)} %copy-done.6), channel_id=1, replica_groups=mesh['seq'=8,'tp'=4] {'tp'}, dimensions={0}, use_global_device_ids=true | all-gather | bytes 983040 | tf_op jit(solution)/shard_map/all_gather | solution.py:503
  19.2 0.0 copy-done.1
  19.2 0.0 copy-done.3
  19.2 0.0 copy-done.5
  19.2 0.0 copy-start.2
  19.2 0.0 copy-start.4
  19.2 2.3 %shard_map.82 = (bf16[4,2,1,32,384]{4,3,2,1,0:T(8,128)(2,1)S(1)}, bf16[4,2,1,32,384]{4,3,2,1,0:T(8,128)(2,1)S(1)}, bf16[32,128]{1,0:T(8,128)(2,1)S(1)}, bf16[256...) custom-call(bf16[384,1024]{1,0:T(8,128)(2,1)S(1)} %all_gather.3.toke, ...), custom_call_target="tpu_custom_call" | custom-call | tf_op jit(solution)/shard_map/pallas_call | solution.py:224
  21.5 2.1 %collective-permute-start = (bf16[4,2,1,32,384]{4,3,2,1,0:T(8,128)(2,1)S(1)}, bf16[4,2,1,32,384]{4,3,2,1,0:T(8,128)(2,1)S(1)}, u32[]{:S(2)}, u32[]{:S(2)}) collective-permute-start(bf16[4,2,1,32,384]{4,3,2,1,0:T(8,128)(2,1)S(1)} %get-tuple-element.23), channel_id=1, source_target_pairs={{0,4},{4,0},{8,12},{12,8},{16,20},{20,16},{24,28},{28,24},{1,5},{5... | collective-permute-start | bytes 589832 | tf_op jit(solution)/shard_map/ppermute | solution.py:505
  23.5 0.0 copy-done
  23.5 1.4 %shard_map.83 = (bf16[256,1152]{1,0:T(8,128)(2,1)}, bf16[256,1152]{1,0:T(8,128)(2,1)}, bf16[256,1152]{1,0:T(8,128)(2,1)}) custom-call(bf16[256,1024]{1,0:T(8,128)(2,1)S(1)} %copy-done, bf16[256,128]{1,0:T(8,128)(2,1)S(1)} %get-tuple-element.24.refs_0_, bf16[256,128]{1,0:T(8,128)(2,1)S(1)} %get-tuple-element.25.refs_1_, ...), custom_call_target="tpu_custom_call" | custom-call | tf_op jit(solution)/shard_map/pallas_call | solution.py:265
  24.9 7.3 %collective-permute-done.came_ref.refs_1_ = bf16[4,2,1,32,384]{4,3,2,1,0:T(8,128)(2,1)S(1)} collective-permute-done((bf16[4,2,1,32,384]{4,3,2,1,0:T(8,128)(2,1)S(1)}, bf16[4,2,1,32,384]{4,3,2,1,0:T(8,128)(2,1)S(1)}, u32[]{:S(2)}, u32[]{:S(2)}) %collective-permute-start) | collective-permute-done | bytes 196640 | tf_op jit(solution)/shard_map/ppermute | solution.py:505
  32.3 3.0 %collective-permute-start.1 = (bf16[2,2,1,32,384]{4,3,2,1,0:T(8,128)(2,1)S(1)}, bf16[2,2,1,32,384]{4,3,2,1,0:T(8,128)(2,1)S(1)}, u32[]{:S(2)}, u32[]{:S(2)}) collective-permute-start(bf16[2,2,1,32,384]{4,3,2,1,0:T(8,128)(2,1)S(1)} %get-tuple-element.32), channel_id=1, source_target_pairs={{0,8},{4,12},{8,16},{12,20},{16,24},{20,28},{24,0},{28,4},{1,9},{5... | collective-permute-start | bytes 294920 | tf_op jit(solution)/shard_map/ppermute | solution.py:509
  35.3 6.1 %collective-permute-start.2 = (bf16[2,2,1,32,384]{4,3,2,1,0:T(8,128)(2,1)S(1)}, bf16[2,2,1,32,384]{4,3,2,1,0:T(8,128)(2,1)S(1)}, u32[]{:S(2)}, u32[]{:S(2)}) collective-permute-start(bf16[2,2,1,32,384]{4,3,2,1,0:T(8,128)(2,1)S(1)} %get-tuple-element.33), channel_id=1, source_target_pairs={{0,16},{4,20},{8,24},{12,28},{16,0},{20,4},{24,8},{28,12},{1,17},{... | collective-permute-start | bytes 294920 | tf_op jit(solution)/shard_map/ppermute | solution.py:509
  41.3 0.0 collective-permute-start.3
  41.3 0.0 collective-permute-start.4
  41.3 1.5 %collective-permute-start.5 = (bf16[256,1152]{1,0:T(8,128)(2,1)}, bf16[256,1152]{1,0:T(8,128)(2,1)S(1)}, u32[]{:S(2)}, u32[]{:S(2)}) collective-permute-start(bf16[256,1152]{1,0:T(8,128)(2,1)} %get-tuple-element.37), channel_id=1, source_target_pairs={{0,2},{1,3},{2,0},{3,1},{4,6},{5,7},{6,4},{7,5},{8,10},{9,11},{10,... | collective-permute-start | bytes 1769480 | tf_op jit(solution)/shard_map/ppermute | solution.py:338
  42.8 1.6 %collective-permute-done.1.refs_8_ = bf16[2,2,1,32,384]{4,3,2,1,0:T(8,128)(2,1)S(1)} collective-permute-done((bf16[2,2,1,32,384]{4,3,2,1,0:T(8,128)(2,1)S(1)}, bf16[2,2,1,32,384]{4,3,2,1,0:T(8,128)(2,1)S(1)}, u32[]{:S(2)}, u32[]{:S(2)}) %collective-permute-start.1) | collective-permute-done | bytes 98336 | tf_op jit(solution)/shard_map/ppermute | solution.py:509
  44.5 0.0 collective-permute-start.6
  44.5 10.3 %collective-permute-done.2.refs_9_ = bf16[2,2,1,32,384]{4,3,2,1,0:T(8,128)(2,1)S(1)} collective-permute-done((bf16[2,2,1,32,384]{4,3,2,1,0:T(8,128)(2,1)S(1)}, bf16[2,2,1,32,384]{4,3,2,1,0:T(8,128)(2,1)S(1)}, u32[]{:S(2)}, u32[]{:S(2)}) %collective-permute-start.2) | collective-permute-done | bytes 98336 | tf_op jit(solution)/shard_map/ppermute | solution.py:509
  54.8 0.0 collective-permute-done.3.refs_10_
  54.8 0.0 all-to-all-done.refs_2_
  54.8 0.0 copy-done.2
  54.8 0.0 copy-done.4
  54.8 4.6 %shard_map.86 = bf16[8,4,32,128]{3,2,1,0:T(8,128)(2,1)} custom-call(bf16[4,2,1,32,384]{4,3,2,1,0:T(8,128)(2,1)S(1)} %get-tuple-element.22.mine_ref.refs_0_, bf16[4,2,1,32,384]{4,3,2,1,0:T(8,128)(2,1)S(1)} %collective-permute-done.came_ref.refs_1_, bf16[8,8,32,384]{3,2,1,0:T(8,128)(2,1)} %all-to-all-done.refs_2_, f32[50,128]{1,0:T(8,128)S(1)} %copy-done.4, ...), custom_call_target="tpu_custom_call" | custom-call | tf_op jit(solution)/shard_map/pallas_call | solution.py:439
  59.5 4.7 %all-to-all-start.1 = ((bf16[32,32,128]{2,1,0:T(8,128)(2,1)}), bf16[32,32,128]{2,1,0:T(8,128)(2,1)S(1)}, u32[]{:S(2)}, u32[]{:S(2)}) async-start(bf16[32,32,128]{2,1,0:T(8,128)(2,1)} %bitcast), calls=%async_computation.1 | async-start | bytes 524288 | tf_op jit(solution)/shard_map/all_to_all | solution.py:496
  64.2 0.0 collective-permute-done.4.refs_0_
  64.2 0.0 collective-permute-done.5.refs_1_
  64.2 6.6 %collective-permute-done.6.refs_2_ = bf16[256,1152]{1,0:T(8,128)(2,1)S(1)} collective-permute-done((bf16[256,1152]{1,0:T(8,128)(2,1)}, bf16[256,1152]{1,0:T(8,128)(2,1)S(1)}, u32[]{:S(2)}, u32[]{:S(2)}) %collective-permute-start.6) | collective-permute-done | bytes 589856 | tf_op jit(solution)/shard_map/ppermute | solution.py:338
  70.9 3.9 %all-to-all-done.1 = bf16[32,32,128]{2,1,0:T(8,128)(2,1)S(1)} async-done(((bf16[32,32,128]{2,1,0:T(8,128)(2,1)}), bf16[32,32,128]{2,1,0:T(8,128)(2,1)S(1)}, u32[]{:S(2)}, u32[]{:S(2)}) %all-to-all-start.1) | async-done | bytes 262176 | tf_op jit(solution)/shard_map/all_to_all | solution.py:496
  74.8 1.4 %shard_map.87 = bf16[96,1024]{1,0:T(8,128)(2,1)} custom-call(bf16[8,4,32,128]{3,2,1,0:T(8,128)(2,1)S(1)} %bitcast.2, bf16[256,128]{1,0:T(8,128)(2,1)S(1)} %get-tuple-element.35.own_ref, bf16[256,1024]{1,0:T(8,128)(2,1)S(1)} %copy-done, bf16[256,1152]{1,0:T(8,128)(2,1)S(1)} %collective-permute-done.4.refs_0_, ...), custom_call_target="tpu_custom_call" | custom-call | tf_op jit(solution)/shard_map/pallas_call | solution.py:486
  (1 shorter events, 0.0 us)
Async XLA Ops:
  2.9 7.5 %copy-start.6 = (bf16[96,1024]{1,0:T(8,128)(2,1)S(1)}, bf16[96,1024]{1,0:T(8,128)(2,1)}, u32[]{:S(2)}) copy-start(bf16[96,1024]{1,0:T(8,128)(2,1)} %param.8) | copy-start | bytes 589828
  3.0 16.2 %copy-start.1 = (bf16[3,1024,256]{2,1,0:T(8,128)(2,1)S(1)}, bf16[3,1024,256]{2,1,0:T(8,128)(2,1)}, u32[]{:S(2)}) copy-start(bf16[3,1024,256]{2,1,0:T(8,128)(2,1)} %weight_ref.3) | copy-start | bytes 4718596
  3.0 16.2 %copy-start.3 = (f32[3,3,256]{2,1,0:T(4,128)S(1)}, f32[3,3,256]{2,1,0:T(4,128)}, u32[]{:S(2)}) copy-start(f32[3,3,256]{2,1,0:T(4,128)} %refs_5_.1) | copy-start | bytes 27652
  3.0 16.2 %copy-start.5 = (f32[2,256]{1,0:T(2,128)S(1)}, f32[2,256]{1,0:T(2,128)}, u32[]{:S(2)}) copy-start(f32[2,256]{1,0:T(2,128)} %refs_6_.1) | copy-start | bytes 6148
  3.0 51.8 %all-to-all-start = ((bf16[8,8,32,384]{3,2,1,0:T(8,128)(2,1)}), bf16[8,8,32,384]{3,2,1,0:T(8,128)(2,1)}, u32[]{:S(2)}, u32[]{:S(2)}) async-start(bf16[8,8,32,384]{3,2,1,0:T(8,128)(2,1)} %shard_map.84), calls=%async_computation | async-start | bytes 3145728 | tf_op jit(solution)/shard_map/all_to_all | solution.py:496
  10.4 13.1 %copy-start = (bf16[256,1024]{1,0:T(8,128)(2,1)S(1)}, bf16[256,1024]{1,0:T(8,128)(2,1)}, u32[]{:S(2)}) copy-start(bf16[256,1024]{1,0:T(8,128)(2,1)} %weight_ref.5) | copy-start | bytes 1572868
  19.2 35.6 %copy-start.2 = (bf16[2,128,128]{2,1,0:T(8,128)(2,1)S(1)}, bf16[2,128,128]{2,1,0:T(8,128)(2,1)}, u32[]{:S(2)}) copy-start(bf16[2,128,128]{2,1,0:T(8,128)(2,1)} %constant.5.clone.refs_4_) | copy-start | bytes 196612
  19.2 35.6 %copy-start.4 = (f32[50,128]{1,0:T(8,128)S(1)}, f32[50,128]{1,0:T(8,128)}, u32[]{:S(2)}) copy-start(f32[50,128]{1,0:T(8,128)} %constant.4.clone.refs_3_) | copy-start | bytes 76804
  21.5 10.8 %collective-permute-start = (bf16[4,2,1,32,384]{4,3,2,1,0:T(8,128)(2,1)S(1)}, bf16[4,2,1,32,384]{4,3,2,1,0:T(8,128)(2,1)S(1)}, u32[]{:S(2)}, u32[]{:S(2)}) collective-permute-start(bf16[4,2,1,32,384]{4,3,2,1,0:T(8,128)(2,1)S(1)} %get-tuple-element.23), channel_id=1, source_target_pairs={{0,4},{4,0},{8,12},{12,8},{16,20},{20,16},{24,28},{28,24},{1,5},{5... | collective-permute-start | bytes 589832 | tf_op jit(solution)/shard_map/ppermute | solution.py:505
  32.3 12.2 %collective-permute-start.1 = (bf16[2,2,1,32,384]{4,3,2,1,0:T(8,128)(2,1)S(1)}, bf16[2,2,1,32,384]{4,3,2,1,0:T(8,128)(2,1)S(1)}, u32[]{:S(2)}, u32[]{:S(2)}) collective-permute-start(bf16[2,2,1,32,384]{4,3,2,1,0:T(8,128)(2,1)S(1)} %get-tuple-element.32), channel_id=1, source_target_pairs={{0,8},{4,12},{8,16},{12,20},{16,24},{20,28},{24,0},{28,4},{1,9},{5... | collective-permute-start | bytes 294920 | tf_op jit(solution)/shard_map/ppermute | solution.py:509
  35.3 19.5 %collective-permute-start.2 = (bf16[2,2,1,32,384]{4,3,2,1,0:T(8,128)(2,1)S(1)}, bf16[2,2,1,32,384]{4,3,2,1,0:T(8,128)(2,1)S(1)}, u32[]{:S(2)}, u32[]{:S(2)}) collective-permute-start(bf16[2,2,1,32,384]{4,3,2,1,0:T(8,128)(2,1)S(1)} %get-tuple-element.33), channel_id=1, source_target_pairs={{0,16},{4,20},{8,24},{12,28},{16,0},{20,4},{24,8},{28,12},{1,17},{... | collective-permute-start | bytes 294920 | tf_op jit(solution)/shard_map/ppermute | solution.py:509
  41.3 13.5 %collective-permute-start.3 = (bf16[2,2,1,32,384]{4,3,2,1,0:T(8,128)(2,1)S(1)}, bf16[2,2,1,32,384]{4,3,2,1,0:T(8,128)(2,1)S(1)}, u32[]{:S(2)}, u32[]{:S(2)}) collective-permute-start(bf16[2,2,1,32,384]{4,3,2,1,0:T(8,128)(2,1)S(1)} %get-tuple-element.34), channel_id=1, source_target_pairs={{0,24},{4,28},{8,0},{12,4},{16,8},{20,12},{24,16},{28,20},{1,25},{... | collective-permute-start | bytes 294920 | tf_op jit(solution)/shard_map/ppermute | solution.py:509
  41.3 22.9 %collective-permute-start.4 = (bf16[256,1152]{1,0:T(8,128)(2,1)}, bf16[256,1152]{1,0:T(8,128)(2,1)S(1)}, u32[]{:S(2)}, u32[]{:S(2)}) collective-permute-start(bf16[256,1152]{1,0:T(8,128)(2,1)} %get-tuple-element.36), channel_id=1, source_target_pairs={{0,1},{1,0},{2,3},{3,2},{4,5},{5,4},{6,7},{7,6},{8,9},{9,8},{10,11... | collective-permute-start | bytes 1769480 | tf_op jit(solution)/shard_map/ppermute | solution.py:338
  41.3 22.9 %collective-permute-start.5 = (bf16[256,1152]{1,0:T(8,128)(2,1)}, bf16[256,1152]{1,0:T(8,128)(2,1)S(1)}, u32[]{:S(2)}, u32[]{:S(2)}) collective-permute-start(bf16[256,1152]{1,0:T(8,128)(2,1)} %get-tuple-element.37), channel_id=1, source_target_pairs={{0,2},{1,3},{2,0},{3,1},{4,6},{5,7},{6,4},{7,5},{8,10},{9,11},{10,... | collective-permute-start | bytes 1769480 | tf_op jit(solution)/shard_map/ppermute | solution.py:338
  44.5 26.4 %collective-permute-start.6 = (bf16[256,1152]{1,0:T(8,128)(2,1)}, bf16[256,1152]{1,0:T(8,128)(2,1)S(1)}, u32[]{:S(2)}, u32[]{:S(2)}) collective-permute-start(bf16[256,1152]{1,0:T(8,128)(2,1)} %get-tuple-element.38), channel_id=1, source_target_pairs={{0,3},{1,2},{2,1},{3,0},{4,7},{5,6},{6,5},{7,4},{8,11},{9,10},{10,... | collective-permute-start | bytes 1769480 | tf_op jit(solution)/shard_map/ppermute | solution.py:338
  59.5 15.3 %all-to-all-start.1 = ((bf16[32,32,128]{2,1,0:T(8,128)(2,1)}), bf16[32,32,128]{2,1,0:T(8,128)(2,1)S(1)}, u32[]{:S(2)}, u32[]{:S(2)}) async-start(bf16[32,32,128]{2,1,0:T(8,128)(2,1)} %bitcast), calls=%async_computation.1 | async-start | bytes 524288 | tf_op jit(solution)/shard_map/all_to_all | solution.py:496
